TPU v7x, 32 devices: a whole 2x2x4 slice. The times are simulated.
32 devices in a mesh: dp: 8 (over y, x, core), tensor: 4 (over z).
Axes of the slice: x: 2, y: 2, z: 4, core: 2. Of those that a mesh axis runs over, the one named last changes fastest.
Arguments:
- tokens: bfloat16 [9216, 2048], P(('dp', 'tensor')), may hold values from -6 to 6
- lengths: int32 [8, 4], P('dp'), may hold values from 1 to 1024, 1152 in all within a row
- attention_gain: bfloat16 [2048], replicated, may hold values from 0.099609375 to 1.8984375
- w_inputs: bfloat16 [2048, 3072], P('dp', 'tensor'), may hold values from -0.125 to 0.125
- w_output: bfloat16 [2048, 2048], P('tensor', 'dp'), may hold values from -1 to 1
- feed_gain: bfloat16 [2048], replicated, may hold values from 0.099609375 to 1.8984375
- w_gate: bfloat16 [2048, 8192], P('dp', 'tensor'), may hold values from -0.125 to 0.125
- w_up: bfloat16 [2048, 8192], P('dp', 'tensor'), may hold values from -0.125 to 0.125
- w_down: bfloat16 [8192, 2048], P('tensor', 'dp'), may hold values from -0.0625 to 0.0625
- cotangent: bfloat16 [9216, 2048], P(('dp', 'tensor')), may hold values from -6 to 6
Outputs:
- block_out: bfloat16 [9216, 2048], P(('dp', 'tensor'))
- tokens_grad: bfloat16 [9216, 2048], P(('dp', 'tensor'))
- attention_gain_grad: float32 [2048], P(('dp', 'tensor'))
- w_inputs_grad: float32 [2048, 3072], P('dp', 'tensor')
- w_output_grad: float32 [2048, 2048], P('tensor', 'dp')
- feed_gain_grad: float32 [2048], P(('dp', 'tensor'))
- w_gate_grad: float32 [2048, 8192], P('dp', 'tensor')
- w_up_grad: float32 [2048, 8192], P('dp', 'tensor')
- w_down_grad: float32 [8192, 2048], P('tensor', 'dp')
Inputs may be any that keep to these rules, and one draw needn't show every extreme that they name: Each row of lengths holds the lengths of the 4 sequences of one group, in order; they sum to 1152, and the longest of each row is 1024.
All inputs are finite; a program needn't handle non-finite values.
Results may differ from a plain program's by a relative error of at most 0.018.
Values may be sent and summed in bfloat16 or wider, within the bound.
No kernel may reach another device: no remote copies, remote signals or barrier semaphores. Data moves between devices by JAX's collectives and lax.ppermute only.
A program may use at most 256 MiB of HBM per device.

v0:
```python
import math

import jax
import jax.numpy as jnp
from jax import lax
from jax.sharding import PartitionSpec as P

KV = 8
HD = 64
QPK = 4


EPS = 1e-05
THETA = 500000.0
FLOOR = -1e30


def layout(lens, rows_count):
    ends = jnp.cumsum(lens)
    rows = jnp.arange(rows_count, dtype=jnp.int32)
    segment = jnp.sum((rows[:, None] >= ends[None, :]).astype(jnp.int32), axis=1)
    starts = ends - lens
    numbers = jnp.arange(lens.shape[0], dtype=jnp.int32)
    picked = jnp.where(segment[:, None] == numbers[None, :], starts[None, :], 0)
    position = rows - jnp.sum(picked, axis=1)
    return (segment, position)


def rotary(position):
    index = jnp.arange(HD // 2, dtype=jnp.float32)
    inverse = jnp.exp(index * (-2.0 * math.log(THETA) / HD))
    angle = position.astype(jnp.float32)[:, None] * inverse[None, :]
    cosine = jnp.cos(angle)
    sine = jnp.sin(angle)
    return (jnp.concatenate([cosine, cosine], 1), jnp.concatenate([sine, sine], 1))


def turn(value, cosine, sine):
    half = value.shape[-1] // 2
    rotated = jnp.concatenate([-value[..., half:], value[..., :half]], -1)
    return value * cosine + rotated * sine


def unturn(value, cosine, sine):
    half = value.shape[-1] // 2
    scaled = value * sine
    return value * cosine + jnp.concatenate([scaled[..., half:], -scaled[..., :half]], -1)


def block_mask(segment, start, block):
    total = segment.shape[0]
    query_rows = start + jnp.arange(block, dtype=jnp.int32)
    key_rows = jnp.arange(total, dtype=jnp.int32)
    query_segment = lax.dynamic_slice_in_dim(segment, start, block, 0)
    return (query_segment[:, None] == segment[None, :]) & (key_rows[None, :] <= query_rows[:, None])


def normalize(value, gain):
    scale = lax.rsqrt(jnp.mean(value * value, axis=1, keepdims=True) + EPS)
    return (value * scale * gain[None, :], scale)


def norm_back(grad, value, scale, gain):
    inner = grad * gain[None, :]
    mean_term = jnp.sum(inner * value, axis=1, keepdims=True) / value.shape[1]
    value_grad = scale * inner - value * (scale * scale * scale) * mean_term
    gain_grad = jnp.sum(grad * value * scale, axis=0)
    return (value_grad, gain_grad)


def product(left, right):
    return jnp.dot(left, right, preferred_element_type=jnp.float32)


def prepare(joint, position, groups):
    rows_count = joint.shape[0]
    cosine, sine = rotary(position)
    grouped = joint.reshape(rows_count, groups, QPK + 2, HD)
    query = turn(grouped[:, :, :QPK, :], cosine[:, None, None, :], sine[:, None, None, :]).astype(
        jnp.bfloat16
    )
    key = turn(grouped[:, :, QPK, :], cosine[:, None, :], sine[:, None, :]).astype(jnp.bfloat16)
    value = grouped[:, :, QPK + 1, :].astype(jnp.bfloat16)
    return (query, key, value, cosine, sine)


def attention_forward(query, key, value, segment):
    rows_count = query.shape[0]
    block = rows_count // 2
    scale = 1.0 / math.sqrt(HD)

    def one_block(index):
        start = index * block
        query_block = lax.dynamic_slice_in_dim(query, start, block, 0)
        allowed = block_mask(segment, start, block)
        scores = (
            jnp.einsum("qgjd,kgd->gjqk", query_block, key, preferred_element_type=jnp.float32)
            * scale
        )
        scores = jnp.where(allowed[None, None], scores, FLOOR)
        top = jnp.max(scores, axis=-1, keepdims=True)
        weights = jnp.exp(scores - top)
        total = jnp.sum(weights, axis=-1, keepdims=True)
        probs = (weights / total).astype(jnp.bfloat16)
        result = jnp.einsum("gjqk,kgd->qgjd", probs, value, preferred_element_type=jnp.float32)
        return (result.astype(jnp.bfloat16), (top + jnp.log(total))[..., 0])

    outputs, log_total = lax.map(one_block, jnp.arange(2, dtype=jnp.int32))
    return (outputs.reshape(rows_count, -1), log_total)


def attention_backward(heads_grad, query, key, value, log_total, segment, cosine, sine):
    rows_count = query.shape[0]
    groups = key.shape[1]
    block = rows_count // 2
    count = 2
    scale = 1.0 / math.sqrt(HD)
    grad_blocks = heads_grad.reshape(count, block, groups, QPK, HD)

    def one_block(carry, item):
        key_grad, value_grad = carry
        index, grad_out, log_block = item
        start = index * block
        query_block = lax.dynamic_slice_in_dim(query, start, block, 0)
        allowed = block_mask(segment, start, block)
        scores = (
            jnp.einsum("qgjd,kgd->gjqk", query_block, key, preferred_element_type=jnp.float32)
            * scale
        )
        scores = jnp.where(allowed[None, None], scores, FLOOR)
        probs = jnp.exp(scores - log_block[..., None])
        low_probs = probs.astype(jnp.bfloat16)
        value_grad = value_grad + jnp.einsum(
            "gjqk,qgjd->kgd", low_probs, grad_out, preferred_element_type=jnp.float32
        )
        prob_grad = jnp.einsum(
            "qgjd,kgd->gjqk", grad_out, value, preferred_element_type=jnp.float32
        )
        delta = jnp.sum(prob_grad * probs, axis=-1, keepdims=True)
        score_grad = (probs * (prob_grad - delta)).astype(jnp.bfloat16)
        query_grad = (
            jnp.einsum("gjqk,kgd->qgjd", score_grad, key, preferred_element_type=jnp.float32)
            * scale
        )
        key_grad = (
            key_grad
            + jnp.einsum(
                "gjqk,qgjd->kgd", score_grad, query_block, preferred_element_type=jnp.float32
            )
            * scale
        )
        return ((key_grad, value_grad), query_grad)

    zeros = jnp.zeros((rows_count, groups, HD), jnp.float32)
    items = (jnp.arange(count, dtype=jnp.int32), grad_blocks, log_total)
    (key_grad, value_grad), query_grad = lax.scan(one_block, (zeros, zeros), items)
    query_grad = unturn(
        query_grad.reshape(rows_count, groups, QPK, HD),
        cosine[:, None, None, :],
        sine[:, None, None, :],
    )
    key_grad = unturn(key_grad, cosine[:, None, :], sine[:, None, :])
    joint_grad = jnp.concatenate(
        [query_grad, key_grad[:, :, None, :], value_grad[:, :, None, :]], 2
    )
    return joint_grad.reshape(rows_count, groups * (QPK + 2) * HD).astype(jnp.bfloat16)


def per_device(
    tokens, lengths, attention_gain, w_inputs, w_output, feed_gain, w_gate, w_up, w_down, cotangent
):
    groups = KV // lax.axis_size("tensor")
    rows_local = tokens.shape[0]
    group_rows = rows_local * lax.axis_size("tensor")
    segment, position = layout(lengths[0], group_rows)
    gain_one = attention_gain.astype(jnp.float32)
    gain_two = feed_gain.astype(jnp.float32)
    inputs_piece, output_piece = (w_inputs, w_output)
    inputs_full, output_full, gate_full, up_full, down_full = (
        lax.all_gather(inputs_piece, "dp", axis=0, tiled=True),
        lax.all_gather(output_piece, "dp", axis=1, tiled=True),
        lax.all_gather(w_gate, "dp", axis=0, tiled=True),
        lax.all_gather(w_up, "dp", axis=0, tiled=True),
        lax.all_gather(w_down, "dp", axis=1, tiled=True),
    )
    inputs_own, output_own = (inputs_full, output_full)
    base = tokens.astype(jnp.float32)
    first, first_scale = normalize(base, gain_one)
    first_all = lax.all_gather(first.astype(jnp.bfloat16), "tensor", axis=0, tiled=True)
    joint = product(first_all, inputs_own)
    query, key, value, cosine, sine = prepare(joint, position, groups)
    heads, log_total = attention_forward(query, key, value, segment)
    mixed = base + lax.psum_scatter(
        product(heads, output_full), "tensor", scatter_dimension=0, tiled=True
    )
    second, second_scale = normalize(mixed, gain_two)
    second_all, grad_all = (
        lax.all_gather(second.astype(jnp.bfloat16), "tensor", axis=0, tiled=True),
        lax.all_gather(cotangent, "tensor", axis=0, tiled=True),
    )
    gate = product(second_all, gate_full)
    up = product(second_all, up_full)
    sigma = jax.nn.sigmoid(gate)
    silu = gate * sigma
    hidden = (silu * up).astype(jnp.bfloat16)
    block_out = mixed + lax.psum_scatter(
        product(hidden, down_full).astype(jnp.bfloat16), "tensor", scatter_dimension=0, tiled=True
    ).astype(jnp.float32)
    hidden_grad = product(grad_all, down_full.T)
    down_wgrad = product(hidden.T, grad_all)
    gate_grad = (hidden_grad * up * sigma * (1.0 + gate * (1.0 - sigma))).astype(jnp.bfloat16)
    up_grad = (hidden_grad * silu).astype(jnp.bfloat16)
    gate_wgrad = product(second_all.T, gate_grad)
    up_wgrad = product(second_all.T, up_grad)
    feed_grads = (
        lax.psum_scatter(
            gate_wgrad.astype(jnp.bfloat16), "dp", scatter_dimension=0, tiled=True
        ).astype(jnp.float32),
        lax.psum_scatter(
            up_wgrad.astype(jnp.bfloat16), "dp", scatter_dimension=0, tiled=True
        ).astype(jnp.float32),
        lax.psum_scatter(
            down_wgrad.astype(jnp.bfloat16), "dp", scatter_dimension=1, tiled=True
        ).astype(jnp.float32),
    )
    second_grad = lax.psum_scatter(
        product(gate_grad, gate_full.T) + product(up_grad, up_full.T),
        "tensor",
        scatter_dimension=0,
        tiled=True,
    )
    mixed_back, gain_two_part = norm_back(second_grad, mixed, second_scale, gain_two)
    mixed_total = cotangent.astype(jnp.float32) + mixed_back
    branch_all = lax.all_gather(mixed_total.astype(jnp.bfloat16), "tensor", axis=0, tiled=True)
    heads_grad = product(branch_all, output_own.T).astype(jnp.bfloat16)
    output_wgrad = product(heads.T, branch_all)
    joint_grad = attention_backward(heads_grad, query, key, value, log_total, segment, cosine, sine)
    inputs_wgrad = product(first_all.T, joint_grad)
    attention_grads = (
        lax.psum_scatter(
            inputs_wgrad.astype(jnp.bfloat16), "dp", scatter_dimension=0, tiled=True
        ).astype(jnp.float32),
        lax.psum_scatter(
            output_wgrad.astype(jnp.bfloat16), "dp", scatter_dimension=1, tiled=True
        ).astype(jnp.float32),
    )
    first_grad = lax.psum_scatter(
        product(joint_grad, inputs_full.T).astype(jnp.bfloat16),
        "tensor",
        scatter_dimension=0,
        tiled=True,
    ).astype(jnp.float32)
    base_back, gain_one_part = norm_back(first_grad, base, first_scale, gain_one)
    tokens_grad = (mixed_total + base_back).astype(jnp.bfloat16)
    gain_sums = (
        lax.psum_scatter(gain_one_part, ("dp", "tensor"), scatter_dimension=0, tiled=True),
        lax.psum_scatter(gain_two_part, ("dp", "tensor"), scatter_dimension=0, tiled=True),
    )
    return (
        block_out.astype(jnp.bfloat16),
        tokens_grad,
        gain_sums[0],
        attention_grads[0],
        attention_grads[1],
        gain_sums[1],
        feed_grads[0],
        feed_grads[1],
        feed_grads[2],
    )


def solution(mesh):
    in_specs = (
        P(("dp", "tensor"), None),
        P("dp", None),
        P(),
        P("dp", "tensor"),
        P("tensor", "dp"),
        P(),
        P("dp", "tensor"),
        P("dp", "tensor"),
        P("tensor", "dp"),
        P(("dp", "tensor"), None),
    )
    out_specs = (
        P(("dp", "tensor"), None),
        P(("dp", "tensor"), None),
        P(("dp", "tensor")),
        P("dp", "tensor"),
        P("tensor", "dp"),
        P(("dp", "tensor")),
        P("dp", "tensor"),
        P("dp", "tensor"),
        P("tensor", "dp"),
    )
    return jax.shard_map(
        per_device, mesh=mesh, in_specs=in_specs, out_specs=out_specs, check_vma=False
    )
```

profile of v0, /device:TPU:0, one launch (start us, length us, event | category | flops | bytes accessed | tf_op | source)
XLA Modules:
  0.0 1596.7 jit_solution(286234257961064831)
XLA Ops:
  15.9 29.0 %all-gather.12.cloned.1.call-done = bf16[2048,768]{1,0:T(8,128)(2,1)} async-done(((bf16[256,768]{1,0:T(8,128)(2,1)}), bf16[2048,768]{1,0:T(8,128)(2,1)}) %all-gather.12.cloned.1.call-update) | async-done | bytes 3145744 | tf_op jit(solution)/shard_map/all_gather | solution.py:180
  45.0 91.6 %all-gather.10.cloned.1.call-done = bf16[1152,2048]{1,0:T(8,128)(2,1)} async-done(((bf16[288,2048]{1,0:T(8,128)(2,1)}), bf16[1152,2048]{1,0:T(8,128)(2,1)}) %all-gather.10.cloned.1.call-update) | async-done | bytes 4718608 | tf_op jit(solution)/shard_map/all_gather | solution.py:189
  146.4 66.0 %while.27 = (s32[]{:T(128)}, bf16[2,576,2,4,64]{1,4,3,2,0:T(8,128)(2,1)S(1)}, f32[2,2,4,576]{3,2,1,0:T(4,128)S(1)}, s32[2]{0:T(128)S(1)}, s32[1152]{0:T(1024)S(1...) while((s32[]{:T(128)}, ...), condition=%wide.region_7.8_spmd, body=%wide.region_4.7_spmd.sunk | while | flops 1424936960 | bytes 153364464 | solution.py:108
  225.3 159.2 %reduce-scatter.10.cloned.1.call-done = f32[288,2048]{1,0:T(8,128)} async-done(((f32[1152,2048]{1,0:T(8,128)}), f32[288,2048]{1,0:T(8,128)}) %reduce-scatter.10.cloned.1.call-update) | async-done | bytes 2359312 | tf_op jit(solution)/shard_map/reduce_scatter | solution.py:193
  390.2 51.3 %all-gather.20.cloned.1.call-done = bf16[2048,2048]{1,0:T(8,128)(2,1)} async-done(((bf16[256,2048]{1,0:T(8,128)(2,1)}), bf16[2048,2048]{1,0:T(8,128)(2,1)}) %all-gather.20.cloned.1.call-update) | async-done | bytes 8388624 | tf_op jit(solution)/shard_map/all_gather | solution.py:183
  441.5 91.4 %all-gather.16.cloned.1.call-done = bf16[1152,2048]{1,0:T(8,128)(2,1)} async-done(((bf16[288,2048]{1,0:T(8,128)(2,1)}), bf16[1152,2048]{1,0:T(8,128)(2,1)}) %all-gather.16.cloned.1.call-update) | async-done | bytes 4718608 | tf_op jit(solution)/shard_map/all_gather | solution.py:198
  548.9 38.9 %all-gather.18.cloned.1.call-done = bf16[2048,2048]{1,0:T(8,128)(2,1)} async-done(((bf16[256,2048]{1,0:T(8,128)(2,1)}), bf16[2048,2048]{1,0:T(8,128)(2,1)}) %all-gather.18.cloned.1.call-update) | async-done | bytes 8388624 | tf_op jit(solution)/shard_map/all_gather | solution.py:182
  603.6 75.1 %all-gather.24.cloned.1.call-done = bf16[1152,2048]{1,0:T(8,128)(2,1)} async-done(((bf16[288,2048]{1,0:T(8,128)(2,1)}), bf16[1152,2048]{1,0:T(8,128)(2,1)}) %all-gather.24.cloned.1.call-update) | async-done | bytes 4718608 | tf_op jit(solution)/shard_map/all_gather | solution.py:199
  678.8 56.3 %all-gather.22.cloned.1.call-done = bf16[2048,2048]{1,0:T(8,128)(2,1)} async-done(((bf16[2048,256]{1,0:T(8,128)(2,1)}), bf16[2048,2048]{1,0:T(8,128)(2,1)}) %all-gather.22.cloned.1.call-update) | async-done | bytes 8388624 | tf_op jit(solution)/shard_map/all_gather | solution.py:184
  735.1 24.7 %multiply_convert_fusion = (bf16[1152,2048]{1,0:T(8,128)(2,1)}, bf16[1152,2048]{1,0:T(8,128)(2,1)}, bf16[1152,2048]{1,0:T(8,128)(2,1)}) fusion(f32[1152,2048]{1,0:T(8,128)} %fusion.71, f32[1152,2048]{1,0:T(8,128)} %fusion.72, bf16[1152,2048]{1,0:T(8,128)(2,1)} %all-gather.24.cloned.1.call-done, bf16[2048,2048]{1,0:T(8,128)(2,1)} %all-gather.22.cloned.1.call-done), kind=kOutput, calls=%fused_computation.56 | convolution fusion | flops 9699065856 | bytes 46137344 | tf_op jit(solution)/shard_map/dot_general | solution.py:72
  805.3 146.1 %reduce-scatter.14.cloned.1.call-done = f32[288,2048]{1,0:T(8,128)} async-done(((f32[1152,2048]{1,0:T(8,128)}), f32[288,2048]{1,0:T(8,128)}) %reduce-scatter.14.cloned.1.call-update) | async-done | bytes 2359312 | tf_op jit(solution)/shard_map/reduce_scatter | solution.py:226
  954.8 85.0 %reduce-scatter.12.cloned.1.call-done = bf16[288,2048]{1,0:T(8,128)(2,1)} async-done(((bf16[1152,2048]{1,0:T(8,128)(2,1)}), bf16[288,2048]{1,0:T(8,128)(2,1)}) %reduce-scatter.12.cloned.1.call-update) | async-done | bytes 1179664 | tf_op jit(solution)/shard_map/reduce_scatter | solution.py:206
  1044.9 16.9 %convolution_convert_fusion.1 = bf16[2048,2048]{1,0:T(8,128)(2,1)} fusion(bf16[1152,2048]{1,0:T(8,128)(2,1)} %all-gather.16.cloned.1.call-done, bf16[1152,2048]{1,0:T(8,128)(2,1)} %get-tuple-element.248), kind=kOutput, calls=%fused_computation.63 | convolution fusion | flops 9667870720 | bytes 17825792 | tf_op jit(solution)/shard_map/dot_general | solution.py:72
  1078.5 16.7 %convolution_convert_fusion = bf16[2048,2048]{1,0:T(8,128)(2,1)} fusion(bf16[1152,2048]{1,0:T(8,128)(2,1)} %get-tuple-element.250, bf16[1152,2048]{1,0:T(8,128)(2,1)} %all-gather.24.cloned.1.call-done), kind=kOutput, calls=%fused_computation.62 | convolution fusion | flops 9667870720 | bytes 17825792 | tf_op jit(solution)/shard_map/dot_general | solution.py:72
  1095.3 39.7 %all-gather.26.cloned.1.call-done = bf16[1152,2048]{1,0:T(8,128)(2,1)} async-done(((bf16[288,2048]{1,0:T(8,128)(2,1)}), bf16[1152,2048]{1,0:T(8,128)(2,1)}) %all-gather.26.cloned.1.call-update) | async-done | bytes 4718608 | tf_op jit(solution)/shard_map/all_gather | solution.py:234
  1147.6 188.7 %while.28 = (s32[]{:T(128)}, f32[1152,2,64]{0,2,1:T(8,128)S(1)}, f32[1152,2,64]{0,2,1:T(8,128)}, f32[2,576,2,4,64]{1,0,4,3,2:T(2,128)}, s32[2]{0:T(128)S(1)}, /*...) while((s32[]{:T(128)}, f32[1152,2,64]{0,2,1:T(8,128)S(1)}, ...), condition=%wide.region_15.16_spmd.clone, body=%wide.region_13.15_spmd.clone.sunk | while | flops 3448180736 | bytes 173631504 | solution.py:156
  1161.2 21.4 %fusion.139 = (f32[2,4,576]{2,1,0:T(4,128)S(1)}, f32[2,4,576,1152]{3,2,1,0:T(8,128)}) fusion(f32[2,576,4,1152]{3,1,2,0:T(8,128)} %fusion.137, f32[2,4,576]{2,1,0:T(4,128)S(1)} %dynamic-slice_bitcast_fusion.2, bf16[1152,2,64]{0,2,1:T(8,128)(2,1)S(1)} %get-tuple-element.465, bf16[1152,2,4,64]{0,3,2,1:T(8,128)(2,1)} %get-tuple-element.463, ...), kind=kOutput, calls=%fused_computation.23.clone.1 | convolution fusion | flops 706014720 | bytes 44118020 | tf_op jit(solution)/shard_map/while/body/eval_jaxpr/qgjd,kgd->gjqk/dot_general | solution.py:127
  1216.1 24.9 %dynamic_update_slice.20 = f32[2,576,2,4,64]{1,0,4,3,2:T(2,128)} dynamic-update-slice(f32[2,576,2,4,64]{1,0,4,3,2:T(2,128)} %get-tuple-element.446, f32[1,576,2,4,64]{1,0,4,3,2:T(1,128)} %copy.57, s32[]{:T(128)S(6)} %copy.74, s32[]{:T(128)} %constant.42.clone.1..sunk.1, s32[]{:T(128)} %constant.42.clone.1..sunk.1, s32[]{:T(128)} %constant.42.clone.1..sunk.1, s32[]{:T(128)} %constant.42.clone.1..sunk.1) | dynamic-update-slice | bytes 2359300 | tf_op jit(solution)/shard_map/while/body/jit(dynamic_update_index_in_dim)/dynamic_update_slice | solution.py:156
  1254.8 20.8 %fusion.139 = (f32[2,4,576]{2,1,0:T(4,128)S(1)}, f32[2,4,576,1152]{3,2,1,0:T(8,128)}) fusion(f32[2,576,4,1152]{3,1,2,0:T(8,128)} %fusion.137, f32[2,4,576]{2,1,0:T(4,128)S(1)} %dynamic-slice_bitcast_fusion.2, bf16[1152,2,64]{0,2,1:T(8,128)(2,1)S(1)} %get-tuple-element.465, bf16[1152,2,4,64]{0,3,2,1:T(8,128)(2,1)} %get-tuple-element.463, ...), kind=kOutput, calls=%fused_computation.23.clone.1 | convolution fusion | flops 706014720 | bytes 44118020 | tf_op jit(solution)/shard_map/while/body/eval_jaxpr/qgjd,kgd->gjqk/dot_general | solution.py:127
  1311.4 24.7 %dynamic_update_slice.20 = f32[2,576,2,4,64]{1,0,4,3,2:T(2,128)} dynamic-update-slice(f32[2,576,2,4,64]{1,0,4,3,2:T(2,128)} %get-tuple-element.446, f32[1,576,2,4,64]{1,0,4,3,2:T(1,128)} %copy.57, s32[]{:T(128)S(6)} %copy.74, s32[]{:T(128)} %constant.42.clone.1..sunk.1, s32[]{:T(128)} %constant.42.clone.1..sunk.1, s32[]{:T(128)} %constant.42.clone.1..sunk.1, s32[]{:T(128)} %constant.42.clone.1..sunk.1) | dynamic-update-slice | bytes 2359300 | tf_op jit(solution)/shard_map/while/body/jit(dynamic_update_index_in_dim)/dynamic_update_slice | solution.py:156
  1374.4 28.1 %reduce-scatter.20.cloned.1.call-done = bf16[512,256]{1,0:T(8,128)(2,1)} async-done(((bf16[512,2048]{1,0:T(8,128)(2,1)}), bf16[512,256]{1,0:T(8,128)(2,1)}) %reduce-scatter.20.cloned.1.call-update) | async-done | bytes 262160 | tf_op jit(solution)/shard_map/reduce_scatter | solution.py:243
  1404.3 47.7 %reduce-scatter.18.cloned.1.call-done = bf16[256,768]{1,0:T(8,128)(2,1)} async-done(((bf16[2048,768]{1,0:T(8,128)(2,1)}), bf16[256,768]{1,0:T(8,128)(2,1)}) %reduce-scatter.18.cloned.1.call-update) | async-done | bytes 393232 | tf_op jit(solution)/shard_map/reduce_scatter | solution.py:240
  1454.0 85.6 %reduce-scatter.16.cloned.1.call-done = bf16[288,2048]{1,0:T(8,128)(2,1)} async-done(((bf16[1152,2048]{1,0:T(8,128)(2,1)}), bf16[288,2048]{1,0:T(8,128)(2,1)}) %reduce-scatter.16.cloned.1.call-update) | async-done | bytes 1179664 | tf_op jit(solution)/shard_map/reduce_scatter | solution.py:247
  1542.2 41.0 %all-reduce.2 = (f32[2048]{0:T(1024)}, f32[2048]{0:T(1024)}) all-reduce(f32[2048]{0:T(1024)} %get-tuple-element.198, f32[2048]{0:T(1024)S(1)} %copy-done.22), channel_id=6, replica_groups=mesh['dp'=8,'tensor'=4] {'dp','tensor'}, use_global_device_ids=true, to_apply=%region_19.20.clone | all-reduce | flops 4096 | bytes 32768
  (206 shorter events, 361.8 us)
Async XLA Ops:
  7.2 37.8 %all-gather.12.cloned.1.call-start = ((), (), s32[]{:S(2)}) async-start(), calls=%async_computation.10 | async-start | bytes 3538944 | tf_op jit(solution)/shard_map/all_gather | solution.py:180
  7.9 128.6 %all-gather.10.cloned.1.call-start = ((), (), s32[]{:S(2)}) async-start(), calls=%async_computation.9 | async-start | bytes 5898240 | tf_op jit(solution)/shard_map/all_gather | solution.py:189
  14.1 202.2 %all-gather.14.cloned.1.call-start = ((), (), s32[]{:S(2)}) async-start(), calls=%async_computation.11 | async-start | bytes 2359296 | tf_op jit(solution)/shard_map/all_gather | solution.py:181
  14.8 369.7 %reduce-scatter.10.cloned.1.call-start = ((), (), s32[]{:S(2)}) async-start(), calls=%async_computation.12 | async-start | bytes 11796480 | tf_op jit(solution)/shard_map/reduce_scatter | solution.py:193
  224.6 159.9 %copy-start.3 = (bf16[288,2048]{1,0:T(8,128)(2,1)S(1)}, bf16[288,2048]{1,0:T(8,128)(2,1)}, u32[]{:S(2)}) copy-start(bf16[288,2048]{1,0:T(8,128)(2,1)} %param.14) | copy-start | bytes 3538948
  224.7 216.9 %all-gather.20.cloned.1.call-start = ((), (), s32[]{:S(2)}) async-start(), calls=%async_computation.15 | async-start | bytes 9437184 | tf_op jit(solution)/shard_map/all_gather | solution.py:183
  225.2 307.7 %all-gather.16.cloned.1.call-start = ((), (), s32[]{:S(2)}) async-start(), calls=%async_computation.13 | async-start | bytes 5898240 | tf_op jit(solution)/shard_map/all_gather | solution.py:198
  387.9 199.8 %all-gather.18.cloned.1.call-start = ((), (), s32[]{:S(2)}) async-start(), calls=%async_computation.14 | async-start | bytes 9437184 | tf_op jit(solution)/shard_map/all_gather | solution.py:182
  388.7 290.1 %all-gather.24.cloned.1.call-start = ((), (), s32[]{:S(2)}) async-start(), calls=%async_computation.18 | async-start | bytes 5898240 | tf_op jit(solution)/shard_map/all_gather | solution.py:199
  389.4 345.7 %all-gather.22.cloned.1.call-start = ((), (), s32[]{:S(2)}) async-start(), calls=%async_computation.16 | async-start | bytes 9437184 | tf_op jit(solution)/shard_map/all_gather | solution.py:184
  390.2 561.2 %reduce-scatter.14.cloned.1.call-start = ((), (), s32[]{:S(2)}) async-start(), calls=%async_computation.19 | async-start | bytes 11796480 | tf_op jit(solution)/shard_map/reduce_scatter | solution.py:226
  789.9 249.9 %reduce-scatter.12.cloned.1.call-start = ((), (), s32[]{:S(2)}) async-start(), calls=%async_computation.17 | async-start | bytes 5898240 | tf_op jit(solution)/shard_map/reduce_scatter | solution.py:206
  805.2 234.6 %copy-start.13 = (bf16[288,2048]{1,0:T(8,128)(2,1)S(1)}, bf16[288,2048]{1,0:T(8,128)(2,1)}, u32[]{:S(2)}) copy-start(bf16[288,2048]{1,0:T(8,128)(2,1)} %param.23) | copy-start | bytes 3538948
  805.2 329.7 %all-gather.26.cloned.1.call-start = ((), (), s32[]{:S(2)}) async-start(), calls=%async_computation.20 | async-start | bytes 5898240 | tf_op jit(solution)/shard_map/all_gather | solution.py:234
  1044.9 320.8 %reduce-scatter.24.cloned.1.call-start = ((), (), s32[]{:S(2)}) async-start(), calls=%async_computation.25 | async-start | bytes 9437184 | tf_op jit(solution)/shard_map/reduce_scatter | solution.py:219
  1061.8 306.8 %reduce-scatter.22.cloned.1.call-start = ((), (), s32[]{:S(2)}) async-start(), calls=%async_computation.24 | async-start | bytes 9437184 | tf_op jit(solution)/shard_map/reduce_scatter | solution.py:216
  1078.4 293.1 %reduce-scatter.26.cloned.1.call-start = ((), (), s32[]{:S(2)}) async-start(), calls=%async_computation.26 | async-start | bytes 9437184 | tf_op jit(solution)/shard_map/reduce_scatter | solution.py:222
  1095.2 307.3 %reduce-scatter.20.cloned.1.call-start = ((), (), s32[]{:S(2)}) async-start(), calls=%async_computation.23 | async-start | bytes 2359296 | tf_op jit(solution)/shard_map/reduce_scatter | solution.py:243
  1344.5 107.6 %reduce-scatter.18.cloned.1.call-start = ((), (), s32[]{:S(2)}) async-start(), calls=%async_computation.22 | async-start | bytes 3538944 | tf_op jit(solution)/shard_map/reduce_scatter | solution.py:240
  1358.1 181.5 %reduce-scatter.16.cloned.1.call-start = ((), (), s32[]{:S(2)}) async-start(), calls=%async_computation.21 | async-start | bytes 5898240 | tf_op jit(solution)/shard_map/reduce_scatter | solution.py:247
  1371.5 168.1 %copy-start.4 = (bf16[288,2048]{1,0:T(8,128)(2,1)S(1)}, bf16[288,2048]{1,0:T(8,128)(2,1)}, u32[]{:S(2)}) copy-start(bf16[288,2048]{1,0:T(8,128)(2,1)} %param.14) | copy-start | bytes 3538948
  1371.5 168.1 %copy-start.21 = (f32[2048]{0:T(1024)S(1)}, f32[2048]{0:T(1024)}, u32[]{:S(2)}) copy-start(f32[2048]{0:T(1024)} %copy-done.20) | copy-start | bytes 24580
  1371.5 170.7 %copy-start.22 = (f32[2048]{0:T(1024)S(1)}, f32[2048]{0:T(1024)}, u32[]{:S(2)}) copy-start(f32[2048]{0:T(1024)} %get-tuple-element.196) | copy-start | bytes 24580
  1371.5 214.9 %copy-start.8 = (f32[288,2048]{1,0:T(8,128)S(1)}, f32[288,2048]{1,0:T(8,128)}, u32[]{:S(2)}) copy-start(f32[288,2048]{1,0:T(8,128)} %get-tuple-element.241) | copy-start | bytes 7077892
  (24 other events, 414.5 us)
Sparse Core Ops, SparseCore 0:
  9.9 35.0 all-gather.11
  47.1 89.4 all-gather.9
  138.4 26.6 all-gather.13
  224.8 159.7 reduce-scatter.9
  386.3 55.2 all-gather.19
  443.5 89.4 all-gather.15
  534.9 52.8 all-gather.17
  589.3 89.4 all-gather.23
  680.7 54.3 all-gather.21
  790.0 161.2 reduce-scatter.13
  953.7 86.0 reduce-scatter.11
  1045.0 89.9 all-gather.25
  1138.4 69.6 reduce-scatter.23
  1211.9 71.2 reduce-scatter.21
  1286.5 71.2 reduce-scatter.25
  1361.3 41.2 reduce-scatter.19
  1405.8 46.2 reduce-scatter.17
  1454.3 85.2 reduce-scatter.15
where the time goes:
time: 1610 us; the launch traced here: 1600 us
  waiting for transfers between devices  1030 us (64%)
  matrix products  328 us (20%)
  local copies, waits for them, and re-layouts  90.5 us (6%)
  other arithmetic  88.8 us (6%)
  blocking collectives  41 us (3%)
    dot_general x15, matrix products, product(): return jnp.dot(left, right, preferred_element_type=jnp.float32)  194 us
    reduce_scatter x1, waiting for transfers between devices, per_device(): lax.psum_scatter(product(heads, output_full), 'tensor', scatter_dimension...  159 us
    reduce_scatter x1, waiting for transfers between devices, per_device(): lax.psum_scatter(product(gate_grad, gate_full.T) + product(up_grad, up_fu...  146 us
    all_gather x1, waiting for transfers between devices, per_device(): lax.all_gather(first.astype(jnp.bfloat16), 'tensor', axis=0, tiled=True)  91.6 us
    all_gather x1, waiting for transfers between devices, per_device(): lax.all_gather(second.astype(jnp.bfloat16), 'tensor', axis=0, tiled=True)  91.4 us
    reduce_scatter x1, waiting for transfers between devices, per_device(): lax.psum_scatter(product(joint_grad, inputs_full.T).astype(jnp.bfloat16),...  85.6 us
    reduce_scatter x1, waiting for transfers between devices, per_device(): lax.psum_scatter(product(hidden, down_full).astype(jnp.bfloat16), 'tensor...  85 us
    all_gather x1, waiting for transfers between devices, per_device(): lax.all_gather(cotangent, 'tensor', axis=0, tiled=True)  75.1 us
  transfers between devices with their start and end apart: 18, of which 14 were waited for; matrix products, arithmetic and copies ran while one was open for 26% of the time, Pallas kernels for 0%

commit v1 on v0

v1 whole, which is shorter than its diff:
```python
import math

import jax
import jax.numpy as jnp
from jax import lax
from jax.experimental import pallas as pl
from jax.experimental.pallas import tpu as pltpu
from jax.sharding import PartitionSpec as P

KV = 8
HD = 64
QPK = 4
EPS = 1e-05
THETA = 500000.0
FLOOR = -1e30
LANES = 128
BLOCK = 128
PARTS = 3
VMEM = 56 << 20
NT = (((1,), (1,)), ((), ()))
NN = (((1,), (0,)), ((), ()))
TN = (((0,), (0,)), ((), ()))


def layout(lens, rows_count):
    ends = jnp.cumsum(lens)
    rows = jnp.arange(rows_count, dtype=jnp.int32)
    segment = jnp.sum((rows[:, None] >= ends[None, :]).astype(jnp.int32), axis=1)
    starts = ends - lens
    numbers = jnp.arange(lens.shape[0], dtype=jnp.int32)
    picked = jnp.where(segment[:, None] == numbers[None, :], starts[None, :], 0)
    return segment, rows - jnp.sum(picked, axis=1)


def tables(lens, rows_count):
    segment, position = layout(lens, rows_count)
    index = (jnp.arange(LANES, dtype=jnp.int32) % (HD // 2)).astype(jnp.float32)
    inverse = jnp.exp(index * (-2.0 * math.log(THETA) / HD))
    angle = position.astype(jnp.float32)[:, None] * inverse[None, :]
    count = lens.shape[0]
    lane = jnp.arange(LANES, dtype=jnp.int32)[None, :] - HD
    same = lane == segment[:, None]
    inside = (lane >= 0) & (lane < count)
    extra = (lane >= count) & (lane < count + PARTS)
    key_lanes = jnp.where((same & inside) | extra, 1.0, 0.0).astype(jnp.bfloat16)
    query_lanes = jnp.where(inside & ~same, FLOOR, 0.0).astype(jnp.bfloat16)
    return jnp.cos(angle), jnp.sin(angle), query_lanes, key_lanes


def dot(left, right, dims=NN):
    return lax.dot_general(left, right, dims, preferred_element_type=jnp.float32)


def rotate(value, cosine, sine):
    low = lax.broadcasted_iota(jnp.int32, value.shape, 1) % HD < HD // 2
    up = pltpu.roll(value, LANES - HD // 2, 1)
    down = pltpu.roll(value, HD // 2, 1)
    return value * cosine + jnp.where(low, -up, down) * sine


def unrotate(value, cosine, sine):
    low = lax.broadcasted_iota(jnp.int32, value.shape, 1) % HD < HD // 2
    scaled = value * sine
    up = pltpu.roll(scaled, LANES - HD // 2, 1)
    down = pltpu.roll(scaled, HD // 2, 1)
    return value * cosine + jnp.where(low, up, -down)


def split(value, parts):
    out = []
    for _ in range(parts):
        piece = value.astype(jnp.bfloat16).astype(jnp.float32)
        out.append(piece)
        value = value - piece
    return out


def forward_kernel(count, joint, cos, sin, query_lanes, key_lanes, heads, query, key, value):
    rows = joint.shape[0]
    cosine, sine = cos[...], sin[...]
    lane = lax.broadcasted_iota(jnp.int32, (rows, LANES), 1)
    left = lane < HD
    beside = query_lanes[...].astype(jnp.float32)
    for pair in range(QPK // 2):
        both = rotate(joint[:, pair * LANES : (pair + 1) * LANES], cosine, sine) * (1.0 / math.sqrt(HD))
        query[2 * pair] = jnp.where(left, both, beside).astype(jnp.bfloat16)
        query[2 * pair + 1] = jnp.where(left, pltpu.roll(both, HD, 1), beside).astype(jnp.bfloat16)
    last = joint[:, QPK * HD : QPK * HD + LANES]
    key[...] = jnp.where(left, rotate(last, cosine, sine), key_lanes[...].astype(jnp.float32)).astype(
        jnp.bfloat16
    )
    ones = jnp.where((lane >= HD) & (lane < HD + PARTS), 1.0, 0.0)
    value[...] = jnp.where(left, pltpu.roll(last, HD, 1), ones).astype(jnp.bfloat16)
    lower = lax.broadcasted_iota(jnp.int32, (BLOCK, BLOCK), 1) <= lax.broadcasted_iota(
        jnp.int32, (BLOCK, BLOCK), 0
    )
    lower = jnp.concatenate([lower] * QPK, 0)
    narrow = lax.broadcasted_iota(jnp.int32, (QPK * BLOCK, LANES), 1)
    for block in range(rows // BLOCK):
        start = block * BLOCK
        end = start + BLOCK
        own = query[:, start:end, :].reshape(QPK * BLOCK, LANES)
        near = jnp.where(lower, dot(own, key[start:end, :], NT), FLOOR)
        top = jnp.max(near, 1, keepdims=True)
        if block:
            far = dot(own, key[0:start, :], NT)
            top = jnp.maximum(top, jnp.max(far, 1, keepdims=True))
        out = dot(jnp.exp(near - top).astype(jnp.bfloat16), value[start:end, :])
        if block:
            out = out + dot(jnp.exp(far - top).astype(jnp.bfloat16), value[0:start, :])
        total = out[:, HD : HD + 1]
        out = out * (1.0 / total)
        held = own.astype(jnp.float32)
        for part, piece in enumerate(split(top + jnp.log(total), PARTS)):
            held = jnp.where(narrow == HD + count + part, -piece, held)
        query[:, start:end, :] = held.astype(jnp.bfloat16).reshape(QPK, BLOCK, LANES)
        each = [out[head * BLOCK : (head + 1) * BLOCK] for head in range(QPK)]
        half = narrow[:BLOCK] < HD
        for pair in range(QPK // 2):
            heads[start:end, pair * LANES : (pair + 1) * LANES] = jnp.where(
                half, each[2 * pair], pltpu.roll(each[2 * pair + 1], HD, 1)
            ).astype(jnp.bfloat16)


def whole(*shape):
    return pl.BlockSpec(shape, lambda g: (0,) * len(shape))


def grouped(*shape):
    return pl.BlockSpec((None,) + shape, lambda g: (g,) + (0,) * len(shape))


def columns(rows, width):
    return pl.BlockSpec((rows, width), lambda g: (0, g))


def attention_forward(joint, held, count, groups):
    rows = joint.shape[0]
    shape = jax.ShapeDtypeStruct
    low = jnp.bfloat16
    return pl.pallas_call(
        lambda *refs: forward_kernel(count, *refs),
        grid=(groups,),
        in_specs=[columns(rows, (QPK + 2) * HD)] + [whole(rows, LANES)] * 4,
        out_specs=[
            columns(rows, QPK * HD),
            grouped(QPK, rows, LANES),
            grouped(rows, LANES),
            grouped(rows, LANES),
        ],
        out_shape=[
            shape((rows, groups * QPK * HD), low),
            shape((groups, QPK, rows, LANES), low),
            shape((groups, rows, LANES), low),
            shape((groups, rows, LANES), low),
        ],
        compiler_params=pltpu.CompilerParams(vmem_limit_bytes=VMEM),
        cost_estimate=pl.CostEstimate(
            flops=groups * 12 * rows * rows * QPK * HD,
            bytes_accessed=16 << 20,
            transcendentals=groups * QPK * rows * rows // 2,
        ),
    )(joint, *held)


def backward_kernel(query, key, value, heads, grads, cos, sin, out, query_grad, key_grad, value_grad):
    rows = key.shape[0]
    key_grad[...] = jnp.zeros_like(key_grad)
    value_grad[...] = jnp.zeros_like(value_grad)
    turned = key[...].astype(jnp.float32).T.astype(jnp.bfloat16)
    upper = lax.broadcasted_iota(jnp.int32, (BLOCK, BLOCK), 0) <= lax.broadcasted_iota(
        jnp.int32, (BLOCK, BLOCK), 1
    )
    upper = jnp.concatenate([upper] * QPK, 1)
    lane = lax.broadcasted_iota(jnp.int32, (QPK * BLOCK, LANES), 1)
    half = lane[:BLOCK] < HD

    def stacked(ref, start, end):
        pieces = []
        for pair in range(QPK // 2):
            both = ref[start:end, pair * LANES : (pair + 1) * LANES].astype(jnp.float32)
            pieces += [both, pltpu.roll(both, HD, 1)]
        return jnp.where(lane < HD, jnp.concatenate(pieces, 0), 0.0)

    for block in range(rows // BLOCK):
        start = block * BLOCK
        end = start + BLOCK
        own = query[:, start:end, :].reshape(QPK * BLOCK, LANES)
        grad = stacked(grads, start, end)
        inner = jnp.sum(grad * stacked(heads, start, end), 1, keepdims=True)
        low = grad.astype(jnp.bfloat16)
        for part, piece in enumerate(split(inner, PARTS)):
            grad = jnp.where(lane == HD + part, -piece, grad)
        beside = grad.astype(jnp.bfloat16)
        turned_grad = None
        for first, last in ([(0, start)] if block else []) + [(start, end)]:
            scores = dot(key[first:last, :], own, NT)
            if first == start:
                scores = jnp.where(upper, scores, FLOOR)
            probs = jnp.exp(scores)
            score_grad = (probs * dot(value[first:last, :], beside, NT)).astype(jnp.bfloat16)
            value_grad[first:last, :] += dot(probs.astype(jnp.bfloat16), low)
            key_grad[first:last, :] += dot(score_grad, own)
            piece = dot(turned[:, first:last], score_grad)
            turned_grad = piece if turned_grad is None else turned_grad + piece
        back = turned_grad.T * (1.0 / math.sqrt(HD))
        each = [back[head * BLOCK : (head + 1) * BLOCK] for head in range(QPK)]
        for pair in range(QPK // 2):
            query_grad[start:end, pair * LANES : (pair + 1) * LANES] = jnp.where(
                half, each[2 * pair], pltpu.roll(each[2 * pair + 1], HD, 1)
            )
    cosine, sine = cos[...], sin[...]
    for pair in range(QPK // 2):
        at = slice(pair * LANES, (pair + 1) * LANES)
        out[:, at] = unrotate(query_grad[:, at], cosine, sine).astype(jnp.bfloat16)
    left = lax.broadcasted_iota(jnp.int32, (rows, LANES), 1) < HD
    key_part = unrotate(jnp.where(left, key_grad[...], 0.0), cosine, sine)
    out[:, QPK * HD : QPK * HD + LANES] = jnp.where(
        left, key_part, pltpu.roll(value_grad[...], HD, 1)
    ).astype(jnp.bfloat16)


def attention_backward(query, key, value, heads, grads, held, groups):
    rows = key.shape[1]
    wide = (QPK + 2) * HD
    return pl.pallas_call(
        backward_kernel,
        grid=(groups,),
        in_specs=[grouped(QPK, rows, LANES), grouped(rows, LANES), grouped(rows, LANES)]
        + [columns(rows, QPK * HD)] * 2
        + [whole(rows, LANES)] * 2,
        out_specs=columns(rows, wide),
        out_shape=jax.ShapeDtypeStruct((rows, groups * wide), jnp.bfloat16),
        scratch_shapes=[
            pltpu.VMEM((rows, QPK * HD), jnp.float32),
            pltpu.VMEM((rows, LANES), jnp.float32),
            pltpu.VMEM((rows, LANES), jnp.float32),
        ],
        compiler_params=pltpu.CompilerParams(vmem_limit_bytes=VMEM),
        cost_estimate=pl.CostEstimate(
            flops=groups * 30 * rows * rows * QPK * HD,
            bytes_accessed=16 << 20,
            transcendentals=groups * QPK * rows * rows // 2,
        ),
    )(query, key, value, heads, grads, held[0], held[1])


def call(kernel, grid, operands, specs, out_specs, out_shape, flops, earlier=(), scratch=()):
    count, extra = len(operands), len(earlier)
    return pl.pallas_call(
        lambda *refs: kernel(*refs[:count], *refs[count + extra :]),
        grid=(grid,),
        in_specs=specs + [pl.BlockSpec(memory_space=pl.ANY)] * extra,
        out_specs=out_specs,
        out_shape=out_shape,
        scratch_shapes=list(scratch),
        compiler_params=pltpu.CompilerParams(vmem_limit_bytes=VMEM),
        cost_estimate=pl.CostEstimate(flops=flops, bytes_accessed=16 << 20, transcendentals=0),
    )(*operands, *earlier)


def column_block(rows, wide):
    return pl.BlockSpec((rows, wide), lambda f: (0, f))


def row_block(wide, width):
    return pl.BlockSpec((wide, width), lambda f: (f, 0))


def low_shape(*shape):
    return jax.ShapeDtypeStruct(shape, jnp.bfloat16)


def block_size(extent):
    return 256 if extent % 256 == 0 else extent


def tied(value, *earlier):
    rows, width = value.shape
    wide = rows // 2 if rows % 32 == 0 else rows

    def kernel(source, target):
        target[...] = source[...]

    block = row_block(wide, width)
    return call(kernel, rows // wide, (value,), [block], block, low_shape(rows, width), 0, earlier)


def tied_sum(left, right, *earlier):
    rows, width = left.shape
    wide = rows // 2 if rows % 32 == 0 else rows

    def kernel(left, right, out):
        out[...] = (left[...].astype(jnp.float32) + right[...].astype(jnp.float32)).astype(out.dtype)

    block = row_block(wide, width)
    return call(
        kernel, rows // wide, (left, right), [block] * 2, block, low_shape(rows, width), 0, earlier
    )


def project(slots, weight, places):
    count = len(slots)
    local, width = slots[0].shape
    extent = weight.shape[1]
    wide = block_size(extent)

    def kernel(*refs):
        places, weight, out = refs[count], refs[count + 1], refs[count + 2]
        for slot in range(count):
            start = pl.multiple_of(places[slot] * local, 16)
            out[pl.ds(start, local), :] = dot(refs[slot][...], weight[...])

    return call(
        kernel,
        extent // wide,
        (*slots, places, weight),
        [whole(local, width)] * count
        + [pl.BlockSpec(memory_space=pltpu.SMEM), column_block(width, wide)],
        column_block(count * local, wide),
        jax.ShapeDtypeStruct((count * local, extent), jnp.float32),
        2 * count * local * width * extent,
    )


def to_slots(value, places, *earlier):
    count = places.shape[0]
    rows, width = value.shape
    local = rows // count

    def kernel(value, places, *out):
        for slot in range(count):
            start = pl.multiple_of(places[slot] * local, 16)
            out[slot][...] = value[pl.ds(start, local), :]

    return call(
        kernel,
        1,
        (value, places),
        [whole(rows, width), pl.BlockSpec(memory_space=pltpu.SMEM)],
        [whole(local, width)] * count,
        [low_shape(local, width)] * count,
        0,
        earlier,
    )


def from_slots(slots, places, *earlier):
    count = len(slots)
    local, width = slots[0].shape

    def kernel(*refs):
        for slot in range(count):
            start = pl.multiple_of(refs[count][slot] * local, 16)
            refs[-1][pl.ds(start, local), :] = refs[slot][...]

    return call(
        kernel,
        1,
        (*slots, places),
        [whole(local, width)] * count + [pl.BlockSpec(memory_space=pltpu.SMEM)],
        whole(count * local, width),
        low_shape(count * local, width),
        0,
        earlier,
    )


def feed_forward(slots, w_gate, w_up, *earlier):
    count = len(slots)
    rows, width = slots[0].shape
    extent = w_gate.shape[1]
    wide = block_size(extent)

    def kernel(*refs):
        w_gate, w_up = refs[count], refs[count + 1]
        out = refs[count + 2 :]
        for slot in range(count):
            one = dot(refs[slot][...], w_gate[...])
            two = dot(refs[slot][...], w_up[...])
            out[slot][...] = (one * jax.nn.sigmoid(one) * two).astype(jnp.bfloat16)
            out[count + slot][...] = one.astype(jnp.bfloat16)
            out[2 * count + slot][...] = two.astype(jnp.bfloat16)

    out = call(
        kernel,
        extent // wide,
        (*slots, w_gate, w_up),
        [whole(rows, width)] * count + [column_block(width, wide)] * 2,
        [column_block(rows, wide)] * (3 * count),
        [low_shape(rows, extent)] * (3 * count),
        4 * count * rows * width * extent,
        earlier,
    )
    return out[:count], out[count : 2 * count], out[2 * count :]


def feed_backward(grads, w_down, gates, ups, *earlier):
    count = len(grads)
    rows, width = grads[0].shape
    extent = w_down.shape[0]
    wide = block_size(extent)

    def kernel(*refs):
        w_down = refs[3 * count]
        out = refs[3 * count + 1 :]
        for slot in range(count):
            hidden_grad = dot(refs[slot][...], w_down[...], NT)
            one = refs[count + slot][...].astype(jnp.float32)
            sigma = jax.nn.sigmoid(one)
            scaled = hidden_grad * sigma
            slope = refs[2 * count + slot][...].astype(jnp.float32) * (1.0 + one * (1.0 - sigma))
            out[slot][...] = (scaled * slope).astype(jnp.bfloat16)
            out[count + slot][...] = (scaled * one).astype(jnp.bfloat16)

    out = call(
        kernel,
        extent // wide,
        (*grads, *gates, *ups, w_down),
        [whole(rows, width)] * count
        + [column_block(rows, wide)] * (2 * count)
        + [row_block(wide, width)],
        [column_block(rows, wide)] * (2 * count),
        [low_shape(rows, extent)] * (2 * count),
        2 * count * rows * width * extent,
        earlier,
    )
    return out[:count], out[count:]


def sum_of_products(terms, *earlier):
    count = len(terms[0][0])
    rows, depth = terms[0][0][0].shape
    extent = terms[0][1].shape[0]
    wide = block_size(extent)
    total = len(terms)

    def kernel(*refs):
        weights = refs[total * count : total * count + total]
        out = refs[total * count + total :]
        for slot in range(count):
            sums = dot(refs[slot][...], weights[0][...], NT)
            for term in range(1, total):
                sums = sums + dot(refs[term * count + slot][...], weights[term][...], NT)
            out[slot][...] = sums.astype(jnp.bfloat16)

    slots = [slot for term in terms for slot in term[0]]
    return call(
        kernel,
        extent // wide,
        (*slots, *[term[1] for term in terms]),
        [whole(rows, depth)] * (total * count) + [row_block(wide, depth)] * total,
        [column_block(rows, wide)] * count,
        [low_shape(rows, extent)] * count,
        2 * total * count * rows * depth * extent,
        earlier,
    )


def product(slots, right, *earlier):
    count = len(slots)
    rows, depth = slots[0].shape
    extent = right.shape[1]
    wide = block_size(extent)

    def kernel(*refs):
        for slot in range(count):
            refs[count + 1 + slot][...] = dot(refs[slot][...], refs[count][...]).astype(jnp.bfloat16)

    return call(
        kernel,
        extent // wide,
        (*slots, right),
        [whole(rows, depth)] * count + [column_block(depth, wide)],
        [column_block(rows, wide)] * count,
        [low_shape(rows, extent)] * count,
        2 * count * rows * depth * extent,
        earlier,
    )


def weight_grad(lefts, rights, *earlier):
    count = len(lefts)
    rows, extent = lefts[0].shape
    width = rights[0].shape[1]
    wide = block_size(extent)
    narrow = 512 if width % 512 == 0 else width

    def kernel(*refs):
        out, left, right = refs[2 * count :]

        @pl.when(pl.program_id(0) == 0)
        def _():
            for slot in range(count):
                right[slot * rows : (slot + 1) * rows, :] = refs[count + slot][...]

        for slot in range(count):
            left[slot * rows : (slot + 1) * rows, :] = refs[slot][...]
        for start in range(0, width, narrow):
            at = slice(start, start + narrow)
            out[:, at] = dot(left[...], right[:, at], TN).astype(jnp.bfloat16)

    return call(
        kernel,
        extent // wide,
        (*lefts, *rights),
        [column_block(rows, wide)] * count + [whole(rows, width)] * count,
        row_block(wide, width),
        low_shape(extent, width),
        2 * count * rows * width * extent,
        earlier,
        [pltpu.VMEM((count * rows, wide), jnp.bfloat16), pltpu.VMEM((count * rows, width), jnp.bfloat16)],
    )


def after(value, *earlier):
    return lax.optimization_barrier((value,) + earlier)[0]


def ring():
    count = lax.axis_size("tensor")
    return [0] + list(range(1, count, 2)) + list(range(2, count, 2))[::-1]


def ring_shift(value, by):
    order = ring()
    count = len(order)
    return lax.ppermute(value, "tensor", [(order[k], order[(k + by) % count]) for k in range(count)])


def slot_places():
    order = ring()
    count = len(order)
    me = lax.axis_index("tensor")
    at = sum(jnp.where(me == device, place, 0) for place, device in enumerate(order))
    back = (at - jnp.arange(count, dtype=jnp.int32)) % count
    return sum(jnp.where(back == place, device, 0) for place, device in enumerate(order)).astype(jnp.int32)


def ring_gather(piece, pauses=()):
    pauses = dict(pauses)
    slots = [piece]
    for step in range(1, lax.axis_size("tensor")):
        last = slots[-1]
        if step in pauses:
            last = tied(last, *pauses[step])
        slots.append(ring_shift(last, 1))
    return slots


def ring_scatter(parts, pauses=()):
    pauses = dict(pauses)
    count = len(parts)
    arrivals = []
    moving = parts[1]
    for step in range(1, count):
        arrivals.append(ring_shift(moving, 1))
        if step < count - 1:
            if step + 1 in pauses:
                moving = tied_sum(arrivals[-1], parts[step + 1], *pauses[step + 1])
            else:
                moving = add(arrivals[-1], parts[step + 1])
    total = parts[0].astype(jnp.float32) + arrivals[-1].astype(jnp.float32)
    return total, arrivals


def add(left, right):
    return (left.astype(jnp.float32) + right.astype(jnp.float32)).astype(jnp.bfloat16)


def exchange(parts):
    count = len(parts)
    return [parts[0]] + [ring_shift(parts[count - q], q) for q in range(1, count)]


def flip(value, bits):
    count = lax.axis_size("dp")
    return lax.ppermute(value, "dp", [(k, k ^ bits) for k in range(count)])


def cube_scatter(pick):
    me = lax.axis_index("dp")
    both = {bits: add(pick(me ^ bits), flip(pick(me ^ bits ^ 1), 1)) for bits in (6, 2, 4, 0)}
    half = both[0].shape[0] // 2
    corner = both[6]
    from_x = flip(corner[:half], 2)
    from_y = flip(corner[half:], 4)
    go_y = jnp.concatenate([add(both[4][:half], from_x), both[4][half:]], 0)
    go_x = jnp.concatenate([both[2][:half], add(both[2][half:], from_y)], 0)
    wide = jnp.float32
    return both[0].astype(wide) + flip(go_x, 2).astype(wide) + flip(go_y, 4).astype(wide)


def gather_rows(piece):
    return lax.all_gather(piece, "dp", axis=0, tiled=True)


def gather_columns(piece):
    return lax.all_gather(piece, "dp", axis=1, tiled=True)


def sum_rows(value):
    return lax.psum_scatter(value, "dp", scatter_dimension=0, tiled=True).astype(jnp.float32)


def sum_columns(value):
    return lax.psum_scatter(value, "dp", scatter_dimension=1, tiled=True).astype(jnp.float32)


def sum_gain(value, places):
    count = lax.axis_size("tensor")
    copies = lax.axis_size("dp")
    me = lax.axis_index("dp")
    cut = value.reshape(copies, count, -1).transpose(1, 0, 2)
    pieces = [lax.dynamic_index_in_dim(cut, places[slot], 0, False) for slot in range(count)]
    total = sum(exchange(pieces))
    bits = copies // 2
    while bits:
        mine = (me // bits) % 2
        pair = total.reshape(2, bits, -1)
        keep = lax.dynamic_index_in_dim(pair, mine, 0, False)
        give = lax.dynamic_index_in_dim(pair, 1 - mine, 0, False)
        total = keep + lax.ppermute(give, "dp", [(k, k ^ bits) for k in range(copies)])
        bits //= 2
    return total.reshape(-1)


def scatter_product(left, right, axis):
    count = lax.axis_size("dp")
    if count != 8:
        value = dot(left, right, TN).astype(jnp.bfloat16)
        return sum_columns(value) if axis else sum_rows(value)
    if axis:
        cut = right.reshape(right.shape[0], count, -1).transpose(1, 0, 2)
        pick = lambda i: dot(left, lax.dynamic_index_in_dim(cut, i, 0, False), TN).astype(jnp.bfloat16)
    else:
        value = dot(left, right, TN).astype(jnp.bfloat16).reshape(count, -1, right.shape[1])
        pick = lambda i: lax.dynamic_index_in_dim(value, i, 0, False)
    return cube_scatter(pick)


def normalize(value, gain):
    scale = lax.rsqrt(jnp.mean(value * value, axis=1, keepdims=True) + EPS)
    return (value * scale * gain[None, :], scale)


def norm_back(grad, value, scale, gain):
    inner = grad * gain[None, :]
    mean_term = jnp.sum(inner * value, axis=1, keepdims=True) / value.shape[1]
    value_grad = scale * inner - value * (scale * scale * scale) * mean_term
    gain_grad = jnp.sum(grad * value * scale, axis=0)
    return (value_grad, gain_grad)


def per_device(
    tokens, lengths, attention_gain, w_inputs, w_output, feed_gain, w_gate, w_up, w_down, cotangent
):
    count = lax.axis_size("tensor")
    groups = KV // count
    local, width = tokens.shape
    rows = local * count
    low = jnp.bfloat16
    held = tables(lengths[0], rows)
    sequences = lengths.shape[1]
    gain_one = attention_gain.astype(jnp.float32)
    gain_two = feed_gain.astype(jnp.float32)

    places = slot_places()
    base = tokens.astype(jnp.float32)
    first, first_scale = normalize(base, gain_one)
    first = first.astype(low)
    inputs_full = gather_rows(w_inputs)
    first_slots = ring_gather(first)
    output_slots = ring_gather(w_output, {2: [first_slots[1]], 3: [first_slots[2]]})
    output_line = jnp.concatenate(output_slots, 0)
    output_full = gather_columns(output_line)
    gate_full = gather_rows(w_gate)
    up_full = gather_rows(tied(w_up, output_line))
    down_full = gather_columns(tied(w_down, output_line))

    joint = project(first_slots, inputs_full, places)
    heads, query, key, value = attention_forward(joint, held, sequences, groups)
    grad_slots = ring_gather(tied(cotangent, first_slots[-1]))
    heads_own = exchange(to_slots(heads, places, grad_slots[1]))
    heads_own = jnp.concatenate(heads_own, 1)
    mixed = base + dot(heads_own, output_full)
    second, second_scale = normalize(mixed, gain_two)
    second_slots = ring_gather(second.astype(low))
    half = max(count // 2, 1)
    ahead = feed_forward(second_slots[:half], gate_full, up_full)
    rest = feed_forward(second_slots[half:], gate_full, up_full)
    hidden, gate, up = [list(one) + list(two) for one, two in zip(ahead, rest)]
    block_parts = product(hidden, down_full)
    gate_grad, up_grad = feed_backward(grad_slots, down_full, gate, up, block_parts[0])
    block_moving = ring_shift(block_parts[1], 1)
    second_parts = sum_of_products(((gate_grad, gate_full), (up_grad, up_full)), block_moving)
    second_grad, second_back = ring_scatter(second_parts)
    down_grad = sum_columns(weight_grad(hidden, grad_slots, second_parts[0]))
    gate_wgrad = sum_rows(weight_grad(second_slots, gate_grad, second_parts[0]))
    up_wgrad = sum_rows(weight_grad(second_slots, up_grad, second_parts[0]))

    mixed_back, gain_two_part = norm_back(second_grad, mixed, second_scale, gain_two)
    mixed_total = cotangent.astype(jnp.float32) + mixed_back
    branch = mixed_total.astype(low)
    heads_back = dot(branch, output_full, NT).astype(low).reshape(local, count, -1)
    heads_grad = exchange([heads_back[:, slot] for slot in range(count)])
    block_sum, block_back = ring_scatter(block_parts, {2: [second_back[-1]], 3: [heads_grad[-1]]})
    block_out = mixed + block_sum
    heads_grad = from_slots(heads_grad, places, block_back[1])
    joint_grad = attention_backward(query, key, value, heads, heads_grad, held, groups)
    joint_slots = to_slots(joint_grad, places)
    first_parts = sum_of_products(((joint_slots, inputs_full),), block_back[2])
    first_grad, first_back = ring_scatter(first_parts)
    output_sum = scatter_product(heads_own, branch, 1).astype(low)
    output_parts = output_sum.reshape(count, -1, output_sum.shape[1])
    output_grad, _ = ring_scatter([output_parts[slot] for slot in range(count)])
    inputs_grad = scatter_product(jnp.concatenate(first_slots, 0), jnp.concatenate(joint_slots, 0), 0)
    base_back, gain_one_part = norm_back(first_grad, base, first_scale, gain_one)
    tokens_grad = (mixed_total + base_back).astype(low)
    return (
        block_out.astype(low),
        tokens_grad,
        sum_gain(gain_one_part, places),
        inputs_grad,
        output_grad,
        sum_gain(gain_two_part, places),
        gate_wgrad,
        up_wgrad,
        down_grad,
    )


def solution(mesh):
    in_specs = (
        P(("dp", "tensor"), None),
        P("dp", None),
        P(),
        P("dp", "tensor"),
        P("tensor", "dp"),
        P(),
        P("dp", "tensor"),
        P("dp", "tensor"),
        P("tensor", "dp"),
        P(("dp", "tensor"), None),
    )
    out_specs = (
        P(("dp", "tensor"), None),
        P(("dp", "tensor"), None),
        P(("dp", "tensor")),
        P("dp", "tensor"),
        P("tensor", "dp"),
        P(("dp", "tensor")),
        P("dp", "tensor"),
        P("dp", "tensor"),
        P("tensor", "dp"),
    )
    return jax.shard_map(
        per_device, mesh=mesh, in_specs=in_specs, out_specs=out_specs, check_vma=False
    )
```

time: 1610 us -> 817 us (0.51)
  waiting for transfers between devices: 1030 us -> 377 us
  matrix products: 328 us -> 36.3 us
  Pallas kernels: 0 us -> 225 us
  starting transfers between devices: 0.73 us -> 69.2 us
  local copies, waits for them, and re-layouts: 90.5 us -> 29.4 us
  blocking collectives: 41 us -> 0 us
  other arithmetic: 88.8 us -> 51.4 us
    reduce_scatter x9 -> x3, waiting for transfers between devices: 552 us -> 0.01 us  [the longest x2 0.01 us: sum_rows(): lax.psum_scatter(value, 'dp', scatter_dimension=0, tiled=True)]
    all_gather x9 -> x5, waiting for transfers between devices: 473 us -> 7.81 us  [the longest x2 7.77 us: gather_columns(): return lax.all_gather(piece, 'dp', axis=1, tiled=True)]
    ppermute x0 -> x58, waiting for transfers between devices: none -> 368 us  [the longest x36 355 us: ring_shift(): lax.ppermute(value, 'tensor', [(order[k], order[(k + by) % count]) for k...]
    dot_general x29 -> x11, matrix products: 328 us -> 36.3 us  [dot(): lax.dot_general(left, right, dims, preferred_element_type=jnp.float32)]
    pallas_call x0 -> x22, Pallas kernels: none -> 225 us  [the longest x20 184 us: call(): pl.pallas_call(lambda *refs: kernel(*refs[:count], *refs[count + extra:])...]
    ppermute x0 -> x58, starting transfers between devices: none -> 68.8 us  [the longest x36 50.9 us: ring_shift(): lax.ppermute(value, 'tensor', [(order[k], order[(k + by) % count]) for k...]
    dynamic_update_slice x4 -> x0, local copies, waits for them, and re-layouts: 54.4 us -> none  [attention_backward(): lax.scan(one_block, (zeros, zeros), items)]
    unnamed x1 -> x0, blocking collectives: 41 us -> none
  transfers between devices with their start and end apart: 18 -> 66, of which waited for: 14 -> 30; matrix products, arithmetic and copies ran while one was open for 26% -> 13% of each run, Pallas kernels for 0% -> 22%
where the time goes in v1:
time: 817 us; the launch traced here: 811 us
  waiting for transfers between devices  377 us (46%)
  Pallas kernels  225 us (28%)
  starting transfers between devices  69.2 us (8%)
  other arithmetic  51.4 us (6%)
  matrix products  36.3 us (4%)
  local copies, waits for them, and re-layouts  29.4 us (4%)
  between operations  22.9 us (3%)
    ppermute x36, waiting for transfers between devices, ring_shift(): lax.ppermute(value, 'tensor', [(order[k], order[(k + by) % count]) for k...  355 us
    pallas_call x20, Pallas kernels, call(): pl.pallas_call(lambda *refs: kernel(*refs[:count], *refs[count + extra:])...  184 us
    ppermute x36, starting transfers between devices, ring_shift(): lax.ppermute(value, 'tensor', [(order[k], order[(k + by) % count]) for k...  50.9 us
    dot_general x11, matrix products, dot(): lax.dot_general(left, right, dims, preferred_element_type=jnp.float32)  36.3 us
    pallas_call x1, Pallas kernels, attention_backward(): pl.pallas_call(backward_kernel, grid=(groups,), in_specs=[grouped(QPK, ro...  21.8 us
    pallas_call x1, Pallas kernels, attention_forward(): pl.pallas_call(lambda *refs: forward_kernel(count, *refs), grid=(groups,)...  19.3 us
  transfers between devices with their start and end apart: 66, of which 30 were waited for; matrix products, arithmetic and copies ran while one was open for 13% of the time, Pallas kernels for 22%

profile of v1, /device:TPU:0, one launch (start us, length us, event | category | flops | bytes accessed | tf_op | source)
XLA Modules:
  0.0 811.2 jit_solution(14490216323274508910)
XLA Ops:
  14.9 27.0 %collective-permute-done.refs_1_ = bf16[288,2048]{1,0:T(8,128)(2,1)S(1)} collective-permute-done((bf16[288,2048]{1,0:T(8,128)(2,1)S(1)}, bf16[288,2048]{1,0:T(8,128)(2,1)S(1)}, u32[]{:S(2)}, u32[]{:S(2)}) %collective-permute-start) | collective-permute-done | bytes 1179680 | tf_op jit(solution)/shard_map/ppermute | solution.py:528
  46.1 29.5 %collective-permute-done.7.refs_0_ = bf16[512,256]{1,0:T(8,128)(2,1)S(1)} collective-permute-done((bf16[512,256]{1,0:T(8,128)(2,1)S(1)}, bf16[512,256]{1,0:T(8,128)(2,1)S(1)}, u32[]{:S(2)}, u32[]{:S(2)}) %collective-permute-start.7) | collective-permute-done | bytes 262176 | tf_op jit(solution)/shard_map/ppermute | solution.py:528
  108.0 20.3 %collective-permute-done.2.refs_3_.refs_1_ = bf16[288,2048]{1,0:T(8,128)(2,1)S(1)} collective-permute-done((bf16[288,2048]{1,0:T(8,128)(2,1)S(1)}, bf16[288,2048]{1,0:T(8,128)(2,1)S(1)}, u32[]{:S(2)}, u32[]{:S(2)}) %collective-permute-start.2) | collective-permute-done | bytes 1179680 | tf_op jit(solution)/shard_map/ppermute | solution.py:528
  140.5 19.3 %shard_map.170 = (bf16[1152,512]{1,0:T(8,128)(2,1)}, bf16[2,4,1152,128]{3,2,1,0:T(8,128)(2,1)}, bf16[2,1152,128]{2,1,0:T(8,128)(2,1)}, bf16[2,1152,128]{2,1,0:T(8,128)(2,1)}) custom-call(f32[1152,768]{1,0:T(8,128)} %shard_map.169.refs_0_, f32[1152,128]{1,0:T(8,128)} %get-tuple-element.137.refs_1_.cos, f32[1152,128]{1,0:T(8,128)} %get-tuple-element.136.refs_2_.sin, ...), custom_call_target="tpu_custom_call" | custom-call | flops 8153726976 | bytes 16777216 | tf_op jit(solution)/shard_map/pallas_call | solution.py:141
  168.9 15.6 %collective-permute-done.4 = bf16[288,512]{1,0:T(8,128)(2,1)S(1)} collective-permute-done((bf16[288,512]{1,0:T(8,128)(2,1)}, bf16[288,512]{1,0:T(8,128)(2,1)S(1)}, u32[]{:S(2)}, u32[]{:S(2)}) %collective-permute-start.4) | collective-permute-done | bytes 294944 | tf_op jit(solution)/shard_map/ppermute | solution.py:528
  195.9 24.4 %collective-permute-done.10.refs_1_ = bf16[288,2048]{1,0:T(8,128)(2,1)S(1)} collective-permute-done((bf16[288,2048]{1,0:T(8,128)(2,1)S(1)}, bf16[288,2048]{1,0:T(8,128)(2,1)S(1)}, u32[]{:S(2)}, u32[]{:S(2)}) %collective-permute-start.10) | collective-permute-done | bytes 1179680 | tf_op jit(solution)/shard_map/ppermute | solution.py:528
  222.7 27.5 %collective-permute-done.11.refs_0_.refs_2_ = bf16[288,2048]{1,0:T(8,128)(2,1)} collective-permute-done((bf16[288,2048]{1,0:T(8,128)(2,1)S(1)}, bf16[288,2048]{1,0:T(8,128)(2,1)}, u32[]{:S(2)}, u32[]{:S(2)}) %collective-permute-start.11) | collective-permute-done | bytes 1179680 | tf_op jit(solution)/shard_map/ppermute | solution.py:528
  250.2 25.3 %collective-permute-done.14.refs_2_.refs_6_ = bf16[288,2048]{1,0:T(8,128)(2,1)} collective-permute-done((bf16[288,2048]{1,0:T(8,128)(2,1)S(1)}, bf16[288,2048]{1,0:T(8,128)(2,1)}, u32[]{:S(2)}, u32[]{:S(2)}) %collective-permute-start.14) | collective-permute-done | bytes 1179680 | tf_op jit(solution)/shard_map/ppermute | solution.py:528
  276.2 16.3 %shard_map.176 = (bf16[288,2048]{1,0:T(8,128)(2,1)}, bf16[288,2048]{1,0:T(8,128)(2,1)}, bf16[288,2048]{1,0:T(8,128)(2,1)}, bf16[288,2048]{1,0:T(8,128)(2,1)}, bf...) custom-call(bf16[288,2048]{1,0:T(8,128)(2,1)} %copy-done.13, bf16[288,2048]{1,0:T(8,128)(2,1)} %copy-done.58, ...), custom_call_target="tpu_custom_call" | custom-call | flops 9663676416 | bytes 16777216 | tf_op jit(solution)/shard_map/pallas_call | solution.py:250
  300.8 16.0 %shard_map.177 = (bf16[288,2048]{1,0:T(8,128)(2,1)}, bf16[288,2048]{1,0:T(8,128)(2,1)}, bf16[288,2048]{1,0:T(8,128)(2,1)}, bf16[288,2048]{1,0:T(8,128)(2,1)}, bf...) custom-call(bf16[288,2048]{1,0:T(8,128)(2,1)} %collective-permute-done.11.refs_0_.refs_2_, ...), custom_call_target="tpu_custom_call" | custom-call | flops 9663676416 | bytes 16777216 | tf_op jit(solution)/shard_map/pallas_call | solution.py:250
  324.6 14.7 %shard_map.179 = (bf16[288,2048]{1,0:T(8,128)(2,1)}, bf16[288,2048]{1,0:T(8,128)(2,1)}, bf16[288,2048]{1,0:T(8,128)(2,1)}, bf16[288,2048]{1,0:T(8,128)(2,1)}) custom-call(bf16[288,2048]{1,0:T(8,128)(2,1)} %get-tuple-element.58.refs_0_, bf16[288,2048]{1,0:T(8,128)(2,1)} %get-tuple-element.59.refs_1_, bf16[288,2048]{1,0:T(8,128)(2,1)} %get-tuple-element.60.refs_2_, ...), custom_call_target="tpu_custom_call" | custom-call | flops 9663676416 | bytes 16777216 | tf_op jit(solution)/shard_map/pallas_call | solution.py:250
  340.8 18.7 %shard_map.180 = (bf16[288,2048]{1,0:T(8,128)(2,1)}, bf16[288,2048]{1,0:T(8,128)(2,1)}, bf16[288,2048]{1,0:T(8,128)(2,1)}, bf16[288,2048]{1,0:T(8,128)(2,1)}, bf...) custom-call(bf16[288,2048]{1,0:T(8,128)(2,1)} %shard_map.171.refs_0_, ...), custom_call_target="tpu_custom_call" | custom-call | flops 9663676416 | bytes 16777216 | tf_op jit(solution)/shard_map/pallas_call | solution.py:250
  369.6 26.4 %shard_map.181 = (bf16[288,2048]{1,0:T(8,128)(2,1)}, bf16[288,2048]{1,0:T(8,128)(2,1)}, bf16[288,2048]{1,0:T(8,128)(2,1)}, bf16[288,2048]{1,0:T(8,128)(2,1)}) custom-call(bf16[288,2048]{1,0:T(8,128)(2,1)} %get-tuple-element.73.refs_0_.refs_4_, bf16[288,2048]{1,0:T(8,128)(2,1)} %get-tuple-element.74.refs_1_.refs_5_, ...), custom_call_target="tpu_custom_call" | custom-call | flops 19327352832 | bytes 16777216 | tf_op jit(solution)/shard_map/pallas_call | solution.py:250
  396.0 16.7 %shard_map.190 = bf16[2048,2048]{1,0:T(8,128)(2,1)} custom-call(bf16[288,2048]{1,0:T(8,128)(2,1)} %get-tuple-element.58.refs_0_, bf16[288,2048]{1,0:T(8,128)(2,1)} %get-tuple-element.59.refs_1_, bf16[288,2048]{1,0:T(8,128)(2,1)} %get-tuple-element.60.refs_2_, bf16[288,2048]{1,0:T(8,128)(2,1)} %get-tuple-element.61.refs_3_, ...), custom_call_target="tpu_custom_call" | custom-call | flops 9663676416 | bytes 16777216 | tf_op jit(solution)/shard_map/pallas_call | solution.py:250
  412.8 17.1 %shard_map.189 = bf16[2048,2048]{1,0:T(8,128)(2,1)} custom-call(bf16[288,2048]{1,0:T(8,128)(2,1)} %copy-done.13, bf16[288,2048]{1,0:T(8,128)(2,1)} %copy-done.58, bf16[288,2048]{1,0:T(8,128)(2,1)} %collective-permute-done.11.refs_0_.refs_2_, bf16[288,2048]{1,0:T(8,128)(2,1)} %collective-permute-done.12.refs_1_.refs_3_, ...), custom_call_target="tpu_custom_call" | custom-call | flops 9663676416 | bytes 16777216 | tf_op jit(solution)/shard_map/pallas_call | solution.py:250
  430.5 27.8 %collective-permute-done.16 = bf16[288,2048]{1,0:T(8,128)(2,1)S(1)} collective-permute-done((bf16[288,2048]{1,0:T(8,128)(2,1)}, bf16[288,2048]{1,0:T(8,128)(2,1)S(1)}, u32[]{:S(2)}, u32[]{:S(2)}) %collective-permute-start.16) | collective-permute-done | bytes 1179680 | tf_op jit(solution)/shard_map/ppermute | solution.py:528
  460.8 26.4 %collective-permute-done.17 = bf16[288,2048]{1,0:T(8,128)(2,1)S(1)} collective-permute-done((bf16[288,2048]{1,0:T(8,128)(2,1)S(1)}, bf16[288,2048]{1,0:T(8,128)(2,1)S(1)}, u32[]{:S(2)}, u32[]{:S(2)}) %collective-permute-start.17) | collective-permute-done | bytes 1179680 | tf_op jit(solution)/shard_map/ppermute | solution.py:528
  497.8 17.9 %shard_map.188 = bf16[2048,2048]{1,0:T(8,128)(2,1)} custom-call(bf16[288,2048]{1,0:T(8,128)(2,1)} %copy-done.13, bf16[288,2048]{1,0:T(8,128)(2,1)} %copy-done.58, bf16[288,2048]{1,0:T(8,128)(2,1)} %collective-permute-done.11.refs_0_.refs_2_, bf16[288,2048]{1,0:T(8,128)(2,1)} %collective-permute-done.12.refs_1_.refs_3_, ...), custom_call_target="tpu_custom_call" | custom-call | flops 9663676416 | bytes 16777216 | tf_op jit(solution)/shard_map/pallas_call | solution.py:250
  573.2 20.7 %collective-permute-done.20.refs_2_.refs_3_ = bf16[288,512]{1,0:T(8,128)(2,1)S(1)} collective-permute-done((bf16[288,512]{1,0:T(8,128)(2,1)S(1)}, bf16[288,512]{1,0:T(8,128)(2,1)S(1)}, u32[]{:S(2)}, u32[]{:S(2)}) %collective-permute-start.20) | collective-permute-done | bytes 294944 | tf_op jit(solution)/shard_map/ppermute | solution.py:528
  609.5 21.8 %shard_map.185.refs_0_ = bf16[1152,768]{1,0:T(8,128)(2,1)} custom-call(bf16[2,4,1152,128]{3,2,1,0:T(8,128)(2,1)} %get-tuple-element.86.query, bf16[2,1152,128]{2,1,0:T(8,128)(2,1)} %get-tuple-element.87.key, bf16[2,1152,128]{2,1,0:T(8,128)(2,1)} %get-tuple-element.88.value, bf16[1152,512]{1,0:T(8,128)(2,1)} %get-tuple-element.53.refs_0_.heads, ...), custom_call_target="tpu_custom_call" | custom-call | flops 20384317440 | bytes 16777216 | tf_op jit(solution)/shard_map/pallas_call | solution.py:226
  657.9 11.8 %collective-permute-done.21.refs_5_ = bf16[288,2048]{1,0:T(8,128)(2,1)S(1)} collective-permute-done((bf16[288,2048]{1,0:T(8,128)(2,1)}, bf16[288,2048]{1,0:T(8,128)(2,1)S(1)}, u32[]{:S(2)}, u32[]{:S(2)}) %collective-permute-start.21) | collective-permute-done | bytes 1179680 | tf_op jit(solution)/shard_map/ppermute | solution.py:528
  686.5 21.3 %collective-permute-done.24 = bf16[288,2048]{1,0:T(8,128)(2,1)S(1)} collective-permute-done((bf16[288,2048]{1,0:T(8,128)(2,1)}, bf16[288,2048]{1,0:T(8,128)(2,1)S(1)}, u32[]{:S(2)}, u32[]{:S(2)}) %collective-permute-start.24) | collective-permute-done | bytes 1179680 | tf_op jit(solution)/shard_map/ppermute | solution.py:528
  725.1 11.2 %collective-permute-done.25 = bf16[288,2048]{1,0:T(8,128)(2,1)} collective-permute-done((bf16[288,2048]{1,0:T(8,128)(2,1)}, bf16[288,2048]{1,0:T(8,128)(2,1)}, u32[]{:S(2)}, u32[]{:S(2)}) %collective-permute-start.25) | collective-permute-done | bytes 1179680 | tf_op jit(solution)/shard_map/ppermute | solution.py:528
  749.5 20.1 %collective-permute-done.49 = bf16[512,256]{1,0:T(8,128)(2,1)S(1)} collective-permute-done((bf16[512,256]{1,0:T(8,128)(2,1)S(1)}, bf16[512,256]{1,0:T(8,128)(2,1)S(1)}, u32[]{:S(2)}, u32[]{:S(2)}) %collective-permute-start.49) | collective-permute-done | bytes 262176 | tf_op jit(solution)/shard_map/ppermute | solution.py:528
  (358 shorter events, 294.5 us)
Async XLA Ops:
  7.2 125.0 %all-gather.6.cloned.1.call-start = ((), (), s32[]{:S(2)}) async-start(), calls=%async_computation.3 | async-start | bytes 3538944 | tf_op jit(solution)/shard_map/all_gather | solution.py:595
  7.9 177.8 %all-gather.8.cloned.1.call-start = ((), (), s32[]{:S(2)}) async-start(), calls=%async_computation.4 | async-start | bytes 9437184 | tf_op jit(solution)/shard_map/all_gather | solution.py:599
  11.9 30.1 %collective-permute-start = (bf16[288,2048]{1,0:T(8,128)(2,1)S(1)}, bf16[288,2048]{1,0:T(8,128)(2,1)S(1)}, u32[]{:S(2)}, u32[]{:S(2)}) collective-permute-start(bf16[288,2048]{1,0:T(8,128)(2,1)S(1)} %fusion.29.refs_0_), channel_id=1, source_target_pairs={{0,1},{1,3},{3,2},{2,0},{4,5},{5,7},{7,6},{6,4},{8,9},{9,11},{11,1... | collective-permute-start | bytes 3538952 | tf_op jit(solution)/shard_map/ppermute | solution.py:528
  41.9 43.7 %collective-permute-start.1 = (bf16[288,2048]{1,0:T(8,128)(2,1)S(1)}, bf16[288,2048]{1,0:T(8,128)(2,1)S(1)}, u32[]{:S(2)}, u32[]{:S(2)}) collective-permute-start(bf16[288,2048]{1,0:T(8,128)(2,1)S(1)} %collective-permute-done.refs_1_), channel_id=1, source_target_pairs={{0,1},{1,3},{3,2},{2,0},{4,5},{5,7},{7,6},{6,4},{8,9},{9,11},{11,1... | collective-permute-start | bytes 3538952 | tf_op jit(solution)/shard_map/ppermute | solution.py:528
  42.8 32.8 %collective-permute-start.7 = (bf16[512,256]{1,0:T(8,128)(2,1)S(1)}, bf16[512,256]{1,0:T(8,128)(2,1)S(1)}, u32[]{:S(2)}, u32[]{:S(2)}) collective-permute-start(bf16[512,256]{1,0:T(8,128)(2,1)S(1)} %copy-done.44), channel_id=1, source_target_pairs={{0,1},{1,3},{3,2},{2,0},{4,5},{5,7},{7,6},{6,4},{8,9},{9,11},{11,1... | collective-permute-start | bytes 786440 | tf_op jit(solution)/shard_map/ppermute | solution.py:528
  97.5 178.6 %all-gather.10.cloned.1.call-start = ((), (), s32[]{:S(2)}) async-start(), calls=%async_computation.5 | async-start | bytes 9437184 | tf_op jit(solution)/shard_map/all_gather | solution.py:595
  98.2 177.9 %all-gather.12.cloned.1.call-start = ((), (), s32[]{:S(2)}) async-start(), calls=%async_computation.6 | async-start | bytes 9437184 | tf_op jit(solution)/shard_map/all_gather | solution.py:595
  100.4 224.2 %all-gather.14.cloned.1.call-start = ((), (), s32[]{:S(2)}) async-start(), calls=%async_computation.7 | async-start | bytes 9437184 | tf_op jit(solution)/shard_map/all_gather | solution.py:599
  102.7 693.3 %reduce-scatter.8.cloned.1.call-start = ((), (), s32[]{:S(2)}) async-start(), calls=%async_computation.10 | async-start | bytes 9437184 | tf_op jit(solution)/shard_map/reduce_scatter | solution.py:607
  220.3 29.9 %collective-permute-start.11 = (bf16[288,2048]{1,0:T(8,128)(2,1)S(1)}, bf16[288,2048]{1,0:T(8,128)(2,1)}, u32[]{:S(2)}, u32[]{:S(2)}) collective-permute-start(bf16[288,2048]{1,0:T(8,128)(2,1)S(1)} %collective-permute-done.10.refs_1_), channel_id=1, source_target_pairs={{0,1},{1,3},{3,2},{2,0},{4,5},{5,7},{7,6},{6,4},{8,9},{9,11},{11,1... | collective-permute-start | bytes 3538952 | tf_op jit(solution)/shard_map/ppermute | solution.py:528
  220.8 54.7 %collective-permute-start.14 = (bf16[288,2048]{1,0:T(8,128)(2,1)S(1)}, bf16[288,2048]{1,0:T(8,128)(2,1)}, u32[]{:S(2)}, u32[]{:S(2)}) collective-permute-start(bf16[288,2048]{1,0:T(8,128)(2,1)S(1)} %copy-done.18), channel_id=1, source_target_pairs={{0,1},{1,3},{3,2},{2,0},{4,5},{5,7},{7,6},{6,4},{8,9},{9,11},{11,1... | collective-permute-start | bytes 3538952 | tf_op jit(solution)/shard_map/ppermute | solution.py:528
  250.2 50.6 %collective-permute-start.12 = (bf16[288,2048]{1,0:T(8,128)(2,1)}, bf16[288,2048]{1,0:T(8,128)(2,1)}, u32[]{:S(2)}, u32[]{:S(2)}) collective-permute-start(bf16[288,2048]{1,0:T(8,128)(2,1)} %collective-permute-done.11.refs_0_.refs_2_), channel_id=1, source_target_pairs={{0,1},{1,3},{3,2},{2,0},{4,5},{5,7},{7,6},{6,4},{8,9},{9,11},{11,1... | collective-permute-start | bytes 3538952 | tf_op jit(solution)/shard_map/ppermute | solution.py:528
  275.5 65.3 %collective-permute-start.15 = (bf16[288,2048]{1,0:T(8,128)(2,1)}, bf16[288,2048]{1,0:T(8,128)(2,1)}, u32[]{:S(2)}, u32[]{:S(2)}) collective-permute-start(bf16[288,2048]{1,0:T(8,128)(2,1)} %collective-permute-done.14.refs_2_.refs_6_), channel_id=1, source_target_pairs={{0,1},{1,3},{3,2},{2,0},{4,5},{5,7},{7,6},{6,4},{8,9},{9,11},{11,1... | collective-permute-start | bytes 3538952 | tf_op jit(solution)/shard_map/ppermute | solution.py:528
  412.8 385.8 %reduce-scatter.6.cloned.1.call-start = ((), (), s32[]{:S(2)}) async-start(), calls=%async_computation.9 | async-start | bytes 9437184 | tf_op jit(solution)/shard_map/reduce_scatter | solution.py:603
  430.0 371.4 %reduce-scatter.4.cloned.1.call-start = ((), (), s32[]{:S(2)}) async-start(), calls=%async_computation.8 | async-start | bytes 9437184 | tf_op jit(solution)/shard_map/reduce_scatter | solution.py:603
  550.8 99.4 %collective-permute-start.46 = (bf16[2048,256]{1,0:T(8,128)(2,1)}, bf16[2048,256]{1,0:T(8,128)(2,1)}, u32[]{:S(2)}, u32[]{:S(2)}) collective-permute-start(bf16[2048,256]{1,0:T(8,128)(2,1)} %convolution_convert_fusion.1), channel_id=1, source_target_pairs={{0,4},{4,0},{8,12},{12,8},{16,20},{20,16},{24,28},{28,24},{1,5},{5... | collective-permute-start | bytes 3145736 | tf_op jit(solution)/shard_map/ppermute | solution.py:578
  556.3 49.6 %collective-permute-start.19 = (bf16[288,2048]{1,0:T(8,128)(2,1)}, bf16[288,2048]{1,0:T(8,128)(2,1)S(1)}, u32[]{:S(2)}, u32[]{:S(2)}) collective-permute-start(bf16[288,2048]{1,0:T(8,128)(2,1)} %shard_map.182), channel_id=1, source_target_pairs={{0,1},{1,3},{3,2},{2,0},{4,5},{5,7},{7,6},{6,4},{8,9},{9,11},{11,1... | collective-permute-start | bytes 3538952 | tf_op jit(solution)/shard_map/ppermute | solution.py:528
  561.6 32.3 %collective-permute-start.20 = (bf16[288,512]{1,0:T(8,128)(2,1)S(1)}, bf16[288,512]{1,0:T(8,128)(2,1)S(1)}, u32[]{:S(2)}, u32[]{:S(2)}) collective-permute-start(bf16[288,512]{1,0:T(8,128)(2,1)S(1)} %bitcast.131), channel_id=1, source_target_pairs={{0,2},{1,0},{3,1},{2,3},{4,6},{5,4},{7,5},{6,7},{8,10},{9,8},{11,9... | collective-permute-start | bytes 884744 | tf_op jit(solution)/shard_map/ppermute | solution.py:528
  563.9 35.6 %collective-permute-start.22 = (bf16[288,512]{1,0:T(8,128)(2,1)S(1)}, bf16[288,512]{1,0:T(8,128)(2,1)S(1)}, u32[]{:S(2)}, u32[]{:S(2)}) collective-permute-start(bf16[288,512]{1,0:T(8,128)(2,1)S(1)} %bitcast.130), channel_id=1, source_target_pairs={{0,1},{1,3},{3,2},{2,0},{4,5},{5,7},{7,6},{6,4},{8,9},{9,11},{11,1... | collective-permute-start | bytes 884744 | tf_op jit(solution)/shard_map/ppermute | solution.py:528
  566.9 39.0 %collective-permute-start.23 = (bf16[288,512]{1,0:T(8,128)(2,1)S(1)}, bf16[288,512]{1,0:T(8,128)(2,1)S(1)}, u32[]{:S(2)}, u32[]{:S(2)}) collective-permute-start(bf16[288,512]{1,0:T(8,128)(2,1)S(1)} %bitcast.129), channel_id=1, source_target_pairs={{0,3},{1,2},{3,0},{2,1},{4,7},{5,6},{7,4},{6,5},{8,11},{9,10},{11,... | collective-permute-start | bytes 884744 | tf_op jit(solution)/shard_map/ppermute | solution.py:528
  593.8 119.8 %collective-permute-start.57 = (f32[1,64]{1,0:T(1,128)S(1)}, f32[1,64]{1,0:T(1,128)S(1)}, u32[]{:S(2)}, u32[]{:S(2)}) collective-permute-start(f32[1,64]{1,0:T(1,128)S(1)} %constant_dynamic-slice_fusion.27), channel_id=1, source_target_pairs={{0,4},{4,0},{8,12},{12,8},{16,20},{20,16},{24,28},{28,24},{1,5},{5... | collective-permute-start | bytes 776 | tf_op jit(solution)/shard_map/ppermute | solution.py:623
  636.9 32.8 %collective-permute-start.21 = (bf16[288,2048]{1,0:T(8,128)(2,1)}, bf16[288,2048]{1,0:T(8,128)(2,1)S(1)}, u32[]{:S(2)}, u32[]{:S(2)}) collective-permute-start(bf16[288,2048]{1,0:T(8,128)(2,1)} %shard_map.183), channel_id=1, source_target_pairs={{0,1},{1,3},{3,2},{2,0},{4,5},{5,7},{7,6},{6,4},{8,9},{9,11},{11,1... | collective-permute-start | bytes 3538952 | tf_op jit(solution)/shard_map/ppermute | solution.py:528
  657.6 56.1 %collective-permute-start.33 = (bf16[256,768]{1,0:T(8,128)(2,1)}, bf16[256,768]{1,0:T(8,128)(2,1)}, u32[]{:S(2)}, u32[]{:S(2)}) collective-permute-start(bf16[256,768]{1,0:T(8,128)(2,1)} %get-tuple-element.103), channel_id=1, source_target_pairs={{0,4},{4,0},{8,12},{12,8},{16,20},{20,16},{24,28},{28,24},{1,5},{5... | collective-permute-start | bytes 1179656 | tf_op jit(solution)/shard_map/ppermute | solution.py:578
  738.1 32.5 %collective-permute-start.26 = (bf16[288,2048]{1,0:T(8,128)(2,1)S(1)}, bf16[288,2048]{1,0:T(8,128)(2,1)S(1)}, u32[]{:S(2)}, u32[]{:S(2)}) collective-permute-start(bf16[288,2048]{1,0:T(8,128)(2,1)S(1)} %add_convert_fusion), channel_id=1, source_target_pairs={{0,1},{1,3},{3,2},{2,0},{4,5},{5,7},{7,6},{6,4},{8,9},{9,11},{11,1... | collective-permute-start | bytes 3538952 | tf_op jit(solution)/shard_map/ppermute | solution.py:528
  (103 other events, 1677.5 us)
Sparse Core Ops, SparseCore 0:
  9.9 35.0 all-gather.5
  97.6 56.7 all-gather.7
  156.3 54.3 all-gather.9
  212.5 54.3 all-gather.11
  268.6 55.9 all-gather.13
  412.9 71.2 reduce-scatter.7
  488.1 71.3 reduce-scatter.5
  562.9 71.2 reduce-scatter.3

commit v2 on v1

--- a/solution.py
+++ b/solution.py
@@ -17,6 +17,7 @@
 BLOCK = 128
 PARTS = 3
 VMEM = 56 << 20
+HEAVY = 10**12
 NT = (((1,), (1,)), ((), ()))
 NN = (((1,), (0,)), ((), ()))
 TN = (((0,), (0,)), ((), ()))
@@ -157,14 +158,21 @@
         compiler_params=pltpu.CompilerParams(vmem_limit_bytes=VMEM),
         cost_estimate=pl.CostEstimate(
             flops=groups * 12 * rows * rows * QPK * HD,
-            bytes_accessed=16 << 20,
-            transcendentals=groups * QPK * rows * rows // 2,
+            bytes_accessed=1 << 20,
+            transcendentals=0,
         ),
     )(joint, *held)
 
 
-def backward_kernel(query, key, value, heads, grads, cos, sin, out, query_grad, key_grad, value_grad):
+def backward_kernel(count, *refs):
+    query, key, value, heads = refs[:4]
+    places, cos, sin = refs[4 + count : 7 + count]
+    out, grads, query_grad, key_grad, value_grad = refs[-5:]
     rows = key.shape[0]
+    local = rows // count
+    for slot in range(count):
+        start = pl.multiple_of(places[slot] * local, 16)
+        grads[pl.ds(start, local), :] = refs[4 + slot][...]
     key_grad[...] = jnp.zeros_like(key_grad)
     value_grad[...] = jnp.zeros_like(value_grad)
     turned = key[...].astype(jnp.float32).T.astype(jnp.bfloat16)
@@ -220,29 +228,30 @@
     ).astype(jnp.bfloat16)
 
 
-def attention_backward(query, key, value, heads, grads, held, groups):
+def attention_backward(query, key, value, heads, slots, places, held, groups, *earlier):
     rows = key.shape[1]
     wide = (QPK + 2) * HD
-    return pl.pallas_call(
-        backward_kernel,
-        grid=(groups,),
-        in_specs=[grouped(QPK, rows, LANES), grouped(rows, LANES), grouped(rows, LANES)]
-        + [columns(rows, QPK * HD)] * 2
+    count = len(slots)
+    operands = (query, key, value, heads, *slots, places, held[0], held[1])
+    return call(
+        lambda *refs: backward_kernel(count, *refs),
+        groups,
+        operands,
+        [grouped(QPK, rows, LANES), grouped(rows, LANES), grouped(rows, LANES), columns(rows, QPK * HD)]
+        + [columns(rows // count, QPK * HD)] * count
+        + [pl.BlockSpec(memory_space=pltpu.SMEM)]
         + [whole(rows, LANES)] * 2,
-        out_specs=columns(rows, wide),
-        out_shape=jax.ShapeDtypeStruct((rows, groups * wide), jnp.bfloat16),
-        scratch_shapes=[
+        columns(rows, wide),
+        jax.ShapeDtypeStruct((rows, groups * wide), jnp.bfloat16),
+        HEAVY,
+        earlier,
+        [
+            pltpu.VMEM((rows, QPK * HD), jnp.bfloat16),
             pltpu.VMEM((rows, QPK * HD), jnp.float32),
             pltpu.VMEM((rows, LANES), jnp.float32),
             pltpu.VMEM((rows, LANES), jnp.float32),
         ],
-        compiler_params=pltpu.CompilerParams(vmem_limit_bytes=VMEM),
-        cost_estimate=pl.CostEstimate(
-            flops=groups * 30 * rows * rows * QPK * HD,
-            bytes_accessed=16 << 20,
-            transcendentals=groups * QPK * rows * rows // 2,
-        ),
-    )(query, key, value, heads, grads, held[0], held[1])
+    )
 
 
 def call(kernel, grid, operands, specs, out_specs, out_shape, flops, earlier=(), scratch=()):
@@ -255,7 +264,7 @@
         out_shape=out_shape,
         scratch_shapes=list(scratch),
         compiler_params=pltpu.CompilerParams(vmem_limit_bytes=VMEM),
-        cost_estimate=pl.CostEstimate(flops=flops, bytes_accessed=16 << 20, transcendentals=0),
+        cost_estimate=pl.CostEstimate(flops=flops, bytes_accessed=1 << 20, transcendentals=0),
     )(*operands, *earlier)
 
 
@@ -286,7 +295,7 @@
     return call(kernel, rows // wide, (value,), [block], block, low_shape(rows, width), 0, earlier)
 
 
-def tied_sum(left, right, *earlier):
+def tied_sum(left, right, weight, *earlier):
     rows, width = left.shape
     wide = rows // 2 if rows % 32 == 0 else rows
 
@@ -295,7 +304,7 @@
 
     block = row_block(wide, width)
     return call(
-        kernel, rows // wide, (left, right), [block] * 2, block, low_shape(rows, width), 0, earlier
+        kernel, rows // wide, (left, right), [block] * 2, block, low_shape(rows, width), weight, earlier
     )
 
 
@@ -479,15 +488,16 @@
     )
 
 
-def weight_grad(lefts, rights, *earlier):
+def weight_grad(lefts, rights, *earlier, half=None, into=None):
     count = len(lefts)
     rows, extent = lefts[0].shape
     width = rights[0].shape[1]
     wide = block_size(extent)
     narrow = 512 if width % 512 == 0 else width
-
-    def kernel(*refs):
-        out, left, right = refs[2 * count :]
+    total = 2 * count + (into is not None) + len(earlier)
+
+    def kernel(*refs):
+        out, left, right = refs[total:]
 
         @pl.when(pl.program_id(0) == 0)
         def _():
@@ -500,16 +510,327 @@
             at = slice(start, start + narrow)
             out[:, at] = dot(left[...], right[:, at], TN).astype(jnp.bfloat16)
 
+    held = () if into is None else (into,)
+    return pl.pallas_call(
+        kernel,
+        grid=(extent // wide,),
+        in_specs=[column_block(rows, wide)] * count
+        + [whole(rows, width)] * count
+        + [pl.BlockSpec(memory_space=pl.ANY)] * (len(held) + len(earlier)),
+        out_specs=pl.BlockSpec((wide, width), lambda f: (f, half or 0)),
+        out_shape=low_shape(extent, width if half is None else 2 * width),
+        input_output_aliases={} if into is None else {2 * count: 0},
+        scratch_shapes=[
+            pltpu.VMEM((count * rows, wide), jnp.bfloat16),
+            pltpu.VMEM((count * rows, width), jnp.bfloat16),
+        ],
+        compiler_params=pltpu.CompilerParams(vmem_limit_bytes=VMEM),
+        cost_estimate=pl.CostEstimate(
+            flops=2 * count * rows * width * extent, bytes_accessed=1 << 20, transcendentals=0
+        ),
+    )(*lefts, *rights, *held, *earlier)
+
+
+def spread_product(value, weight, places, slots, *earlier):
+    count = places.shape[0]
+    rows, depth = value.shape
+    local = rows // count
+    extent = weight.shape[0]
+    wide = extent // 2 if extent % 512 == 0 else extent
+
+    def kernel(value, places, weight, *out):
+        for at, slot in enumerate(slots):
+            start = pl.multiple_of(places[slot] * local, 16)
+            out[at][...] = dot(value[pl.ds(start, local), :], weight[...], NT).astype(jnp.bfloat16)
+
     return call(
         kernel,
         extent // wide,
-        (*lefts, *rights),
-        [column_block(rows, wide)] * count + [whole(rows, width)] * count,
-        row_block(wide, width),
-        low_shape(extent, width),
-        2 * count * rows * width * extent,
-        earlier,
-        [pltpu.VMEM((count * rows, wide), jnp.bfloat16), pltpu.VMEM((count * rows, width), jnp.bfloat16)],
+        (value, places, weight),
+        [whole(rows, depth), pl.BlockSpec(memory_space=pltpu.SMEM), row_block(wide, depth)],
+        [column_block(local, wide)] * len(slots),
+        [low_shape(local, extent)] * len(slots),
+        2 * len(slots) * local * depth * extent,
+        earlier,
+    )
+
+
+def cube_call(kernel, operands, specs, piece, scratch, flops, earlier):
+    count, extra = len(operands), len(earlier)
+
+    def body(me, *refs):
+        away, home = refs[count + extra : count + extra + 2]
+        value = kernel(*refs[:count], *refs[count + extra + 2 :])
+        step = pl.program_id(0)
+
+        @pl.when(step < 4)
+        def _():
+            away[...] = value
+
+        @pl.when(step >= 4)
+        def _():
+            home[...] = value
+
+    me = lax.axis_index("dp").astype(jnp.int32).reshape(1)
+    return pl.pallas_call(
+        body,
+        grid_spec=pltpu.PrefetchScalarGridSpec(
+            num_scalar_prefetch=1,
+            grid=(8,),
+            in_specs=specs + [pl.BlockSpec(memory_space=pl.ANY)] * extra,
+            out_specs=[
+                pl.BlockSpec((None,) + piece, lambda i, me: (jnp.minimum(i, 3), 0, 0)),
+                pl.BlockSpec((None,) + piece, lambda i, me: (jnp.maximum(i - 4, 0), 0, 0)),
+            ],
+            scratch_shapes=scratch,
+        ),
+        out_shape=[low_shape(4, *piece)] * 2,
+        compiler_params=pltpu.CompilerParams(vmem_limit_bytes=VMEM),
+        cost_estimate=pl.CostEstimate(flops=flops, bytes_accessed=1 << 20, transcendentals=0),
+    )(me, *operands, *earlier)
+
+
+def cube_place(step, me):
+    return jnp.bitwise_xor(me[0], 2 * (step % 4) + 1 - step // 4)
+
+
+def cube_columns(lefts, right, *earlier):
+    count = len(lefts)
+    rows, wide = lefts[0].shape
+    block = right.shape[1] // 8
+
+    def kernel(*refs):
+        left = refs[-1]
+
+        @pl.when(pl.program_id(0) == 0)
+        def _():
+            for slot in range(count):
+                turned = refs[slot][...].astype(jnp.float32).T
+                left[slot * wide : (slot + 1) * wide, :] = turned.astype(jnp.bfloat16)
+
+        return dot(left[...], refs[count][...]).astype(jnp.bfloat16)
+
+    fixed = pl.BlockSpec((rows, wide), lambda i, me: (0, 0))
+    moving = pl.BlockSpec((rows, block), lambda i, me: (0, cube_place(i, me)))
+    scratch = [pltpu.VMEM((count * wide, rows), jnp.bfloat16)]
+    flops = 2 * rows * count * wide * right.shape[1]
+    piece = (count * wide, block)
+    return cube_call(kernel, (*lefts, right), [fixed] * count + [moving], piece, scratch, flops, earlier)
+
+
+def cube_rows(lefts, right, places, cost, *earlier):
+    count = len(lefts)
+    rows, width = lefts[0].shape
+    extent = right.shape[1]
+    block = width // 8
+
+    def kernel(*refs):
+        left, turned = refs[-2:]
+
+        @pl.when(pl.program_id(0) == 0)
+        def _():
+            for slot in range(count):
+                start = pl.multiple_of(refs[count + 1][slot] * rows, 16)
+                turned[slot * rows : (slot + 1) * rows, :] = refs[count][pl.ds(start, rows), :]
+
+        for slot in range(count):
+            left[slot * rows : (slot + 1) * rows, :] = refs[slot][...]
+        return dot(left[...], turned[...], TN).astype(jnp.bfloat16)
+
+    moving = pl.BlockSpec((rows, block), lambda i, me: (0, cube_place(i, me)))
+    fixed = pl.BlockSpec((count * rows, extent), lambda i, me: (0, 0))
+    scratch = [
+        pltpu.VMEM((count * rows, block), jnp.bfloat16),
+        pltpu.VMEM((count * rows, extent), jnp.bfloat16),
+    ]
+    specs = [moving] * count + [fixed, pl.BlockSpec(memory_space=pltpu.SMEM)]
+    return cube_call(kernel, (*lefts, right, places), specs, (block, extent), scratch, cost, earlier)
+
+
+def cube_pair(home, arrived, *earlier):
+    _, rows, width = home.shape
+    half = rows // 2
+
+    def kernel(home, arrived, own, over_x, over_y, top, bottom):
+        total = lambda at: (
+            home[at].astype(jnp.float32) + arrived[at].astype(jnp.float32)
+        ).astype(jnp.bfloat16)
+        own[...] = total(0)
+        over_x[...] = total(1)
+        over_y[...] = total(2)
+        corner = total(3)
+        top[...] = corner[:half]
+        bottom[...] = corner[half:]
+
+    full, part = whole(rows, width), whole(half, width)
+    return call(
+        kernel,
+        1,
+        (home, arrived),
+        [whole(4, rows, width)] * 2,
+        [full] * 3 + [part] * 2,
+        [low_shape(rows, width)] * 3 + [low_shape(half, width)] * 2,
+        0,
+        earlier,
+    )
+
+
+def cube_turn(over_x, over_y, from_x, from_y, *earlier):
+    rows, width = over_x.shape
+    half = rows // 2
+
+    def kernel(over_x, over_y, from_x, from_y, go_x, go_y):
+        both = lambda one, two: (one.astype(jnp.float32) + two.astype(jnp.float32)).astype(jnp.bfloat16)
+        go_y[:half, :] = both(over_y[:half, :], from_x[...])
+        go_y[half:, :] = over_y[half:, :]
+        go_x[:half, :] = over_x[:half, :]
+        go_x[half:, :] = both(over_x[half:, :], from_y[...])
+
+    full, part = whole(rows, width), whole(half, width)
+    return call(
+        kernel,
+        1,
+        (over_x, over_y, from_x, from_y),
+        [full] * 2 + [part] * 2,
+        [full] * 2,
+        [low_shape(rows, width)] * 2,
+        0,
+        earlier,
+    )
+
+
+def total_of(terms, dtype, *earlier):
+    rows, width = terms[0].shape
+    wide = rows // 2 if rows % 32 == 0 else rows
+
+    def kernel(*refs):
+        total = refs[0][...].astype(jnp.float32)
+        for ref in refs[1:-1]:
+            total = total + ref[...].astype(jnp.float32)
+        refs[-1][...] = total.astype(dtype)
+
+    block = row_block(wide, width)
+    shape = jax.ShapeDtypeStruct((rows, width), dtype)
+    return call(kernel, rows // wide, tuple(terms), [block] * len(terms), block, shape, 0, earlier)
+
+
+def norm_grad(grads, value, gain, beside):
+    width = value.shape[1]
+    grad = grads[0].astype(jnp.float32)
+    for term in grads[1:]:
+        grad = grad + term.astype(jnp.float32)
+    value = value.astype(jnp.float32)
+    scale = lax.rsqrt(jnp.sum(value * value, 1, keepdims=True) * (1.0 / width) + EPS)
+    scaled = value * scale
+    inner = grad * gain.astype(jnp.float32)
+    mean = jnp.sum(inner * scaled, 1, keepdims=True) * (1.0 / width)
+    return beside.astype(jnp.float32) + scale * (inner - scaled * mean)
+
+
+def norm_backward(grads, value, gain, beside, *earlier):
+    rows, width = value.shape
+    terms = len(grads)
+    wide = 96 if rows % 96 == 0 else rows
+
+    def kernel(*refs):
+        value, gain, beside, out = refs[terms:]
+        grads = [ref[...] for ref in refs[:terms]]
+        out[...] = norm_grad(grads, value[...], gain[...], beside[...]).astype(out.dtype)
+
+    block = row_block(wide, width)
+    return call(
+        kernel,
+        rows // wide,
+        (*grads, value, gain.reshape(1, width), beside),
+        [block] * (terms + 1) + [whole(1, width), block],
+        block,
+        low_shape(rows, width),
+        0,
+        earlier,
+    )
+
+
+def norm_split(grads, value, gain, beside, right, count, *earlier):
+    rows, width = value.shape
+    terms = len(grads)
+    wide = right.shape[0] // count
+
+    def kernel(*refs):
+        value, gain, beside, right, total, rounded = refs[terms : terms + 6]
+        out = refs[terms + 6 :]
+
+        @pl.when(pl.program_id(0) == 0)
+        def _():
+            for at in [slice(start, start + 96) for start in range(0, rows, 96)] if rows % 96 == 0 else [slice(0, rows)]:
+                one = norm_grad([ref[at, :] for ref in refs[:terms]], value[at, :], gain[...], beside[at, :])
+                total[at, :] = one
+                rounded[at, :] = one.astype(jnp.bfloat16)
+
+        part = dot(rounded[...], right[...], NT).astype(jnp.bfloat16)
+        for slot in range(count):
+
+            @pl.when(pl.program_id(0) == slot)
+            def _(slot=slot):
+                out[slot][...] = part
+
+    block = whole(rows, width)
+    out = call(
+        kernel,
+        count,
+        (*grads, value, gain.reshape(1, width), beside, right),
+        [block] * (terms + 1) + [whole(1, width), block, row_block(wide, width)],
+        [block] * 2 + [whole(rows, wide)] * count,
+        [jax.ShapeDtypeStruct((rows, width), jnp.float32), low_shape(rows, width)]
+        + [low_shape(rows, wide)] * count,
+        HEAVY,
+        earlier,
+    )
+    return out[0], out[1], out[2:]
+
+
+def widen(terms, weight, part=0, *earlier):
+    rows, width = weight.shape
+    wide = rows // 2 if rows % 32 == 0 else rows
+    count = len(terms)
+
+    def kernel(*refs):
+        weight, out, share = refs[count:]
+        total = refs[0][...].astype(jnp.float32)
+        for ref in refs[1:count]:
+            total = total + ref[...].astype(jnp.float32)
+        out[...] = total
+        share[...] = jnp.sum(total * weight[...].astype(jnp.float32), 1, keepdims=True)
+
+    block = row_block(wide, width)
+    return call(
+        kernel,
+        rows // wide,
+        (*terms, weight),
+        [pl.BlockSpec((wide, width), lambda f: (f, part))] * count + [block],
+        [block, row_block(wide, 1)],
+        [jax.ShapeDtypeStruct((rows, width), jnp.float32), jax.ShapeDtypeStruct((rows, 1), jnp.float32)],
+        0,
+        earlier,
+    )
+
+
+def widen_turned(value, part):
+    rows, width = value.shape
+    width = width // 2
+    wide = 256 if width % 256 == 0 else width
+    blocks = width // wide
+
+    def kernel(source, target):
+        target[...] = source[...].astype(jnp.float32).T
+
+    return call(
+        kernel,
+        blocks,
+        (value,),
+        [pl.BlockSpec((rows, wide), lambda f: (0, part * blocks + f))],
+        row_block(wide, rows),
+        jax.ShapeDtypeStruct((width, rows), jnp.float32),
+        0,
     )
 
 
@@ -548,7 +869,11 @@
     return slots
 
 
-def ring_scatter(parts, pauses=()):
+def direct_gather(piece):
+    return [piece] + [ring_shift(piece, by) for by in range(1, lax.axis_size("tensor"))]
+
+
+def ring_scatter(parts, pauses=(), heavy=0):
     pauses = dict(pauses)
     count = len(parts)
     arrivals = []
@@ -557,11 +882,12 @@
         arrivals.append(ring_shift(moving, 1))
         if step < count - 1:
             if step + 1 in pauses:
-                moving = tied_sum(arrivals[-1], parts[step + 1], *pauses[step + 1])
+                moving = tied_sum(
+                    arrivals[-1], parts[step + 1], HEAVY if step + 1 == heavy else 0, *pauses[step + 1]
+                )
             else:
                 moving = add(arrivals[-1], parts[step + 1])
-    total = parts[0].astype(jnp.float32) + arrivals[-1].astype(jnp.float32)
-    return total, arrivals
+    return (parts[0], arrivals[-1]), arrivals
 
 
 def add(left, right):
@@ -578,17 +904,22 @@
     return lax.ppermute(value, "dp", [(k, k ^ bits) for k in range(count)])
 
 
-def cube_scatter(pick):
-    me = lax.axis_index("dp")
-    both = {bits: add(pick(me ^ bits), flip(pick(me ^ bits ^ 1), 1)) for bits in (6, 2, 4, 0)}
-    half = both[0].shape[0] // 2
-    corner = both[6]
-    from_x = flip(corner[:half], 2)
-    from_y = flip(corner[half:], 4)
-    go_y = jnp.concatenate([add(both[4][:half], from_x), both[4][half:]], 0)
-    go_x = jnp.concatenate([both[2][:half], add(both[2][half:], from_y)], 0)
-    wide = jnp.float32
-    return both[0].astype(wide) + flip(go_x, 2).astype(wide) + flip(go_y, 4).astype(wide)
+def cube_pairs(parts, *earlier):
+    away, home = parts
+    return cube_pair(home, flip(away, 1), *earlier)
+
+
+def cube_turns(pairs, *earlier):
+    _, over_x, over_y, top, bottom = pairs
+    return cube_turn(over_x, over_y, flip(top, 2), flip(bottom, 4), *earlier)
+
+
+def cube_terms(pairs, turns):
+    return (pairs[0], flip(turns[0], 2), flip(turns[1], 4))
+
+
+def cube_total(pairs, turns, dtype, *earlier):
+    return total_of(cube_terms(pairs, turns), dtype, *earlier)
 
 
 def gather_rows(piece):
@@ -600,56 +931,26 @@
 
 
 def sum_rows(value):
-    return lax.psum_scatter(value, "dp", scatter_dimension=0, tiled=True).astype(jnp.float32)
+    return lax.psum_scatter(value, "dp", scatter_dimension=0, tiled=True)
 
 
 def sum_columns(value):
-    return lax.psum_scatter(value, "dp", scatter_dimension=1, tiled=True).astype(jnp.float32)
-
-
-def sum_gain(value, places):
-    count = lax.axis_size("tensor")
-    copies = lax.axis_size("dp")
-    me = lax.axis_index("dp")
-    cut = value.reshape(copies, count, -1).transpose(1, 0, 2)
-    pieces = [lax.dynamic_index_in_dim(cut, places[slot], 0, False) for slot in range(count)]
-    total = sum(exchange(pieces))
-    bits = copies // 2
-    while bits:
-        mine = (me // bits) % 2
-        pair = total.reshape(2, bits, -1)
-        keep = lax.dynamic_index_in_dim(pair, mine, 0, False)
-        give = lax.dynamic_index_in_dim(pair, 1 - mine, 0, False)
-        total = keep + lax.ppermute(give, "dp", [(k, k ^ bits) for k in range(copies)])
-        bits //= 2
-    return total.reshape(-1)
-
-
-def scatter_product(left, right, axis):
-    count = lax.axis_size("dp")
-    if count != 8:
-        value = dot(left, right, TN).astype(jnp.bfloat16)
-        return sum_columns(value) if axis else sum_rows(value)
-    if axis:
-        cut = right.reshape(right.shape[0], count, -1).transpose(1, 0, 2)
-        pick = lambda i: dot(left, lax.dynamic_index_in_dim(cut, i, 0, False), TN).astype(jnp.bfloat16)
-    else:
-        value = dot(left, right, TN).astype(jnp.bfloat16).reshape(count, -1, right.shape[1])
-        pick = lambda i: lax.dynamic_index_in_dim(value, i, 0, False)
-    return cube_scatter(pick)
+    return lax.psum_scatter(value, "dp", scatter_dimension=1, tiled=True)
+
+
+def gain_sums(shares, gains, places):
+    count = places.shape[0]
+    rows = shares[0].shape[0]
+    start = lax.axis_index("dp") * rows
+    own = [share[:, 0] / lax.dynamic_slice_in_dim(gain, start, rows, 0) for share, gain in zip(shares, gains)]
+    cut = jnp.stack(own).reshape(len(own), count, -1)
+    pieces = [lax.dynamic_index_in_dim(cut, places[slot], 1, False) for slot in range(count)]
+    return sum(exchange(pieces))
 
 
 def normalize(value, gain):
     scale = lax.rsqrt(jnp.mean(value * value, axis=1, keepdims=True) + EPS)
     return (value * scale * gain[None, :], scale)
-
-
-def norm_back(grad, value, scale, gain):
-    inner = grad * gain[None, :]
-    mean_term = jnp.sum(inner * value, axis=1, keepdims=True) / value.shape[1]
-    value_grad = scale * inner - value * (scale * scale * scale) * mean_term
-    gain_grad = jnp.sum(grad * value * scale, axis=0)
-    return (value_grad, gain_grad)
 
 
 def per_device(
@@ -667,25 +968,22 @@
 
     places = slot_places()
     base = tokens.astype(jnp.float32)
-    first, first_scale = normalize(base, gain_one)
-    first = first.astype(low)
+    first = normalize(base, gain_one)[0].astype(low)
     inputs_full = gather_rows(w_inputs)
     first_slots = ring_gather(first)
-    output_slots = ring_gather(w_output, {2: [first_slots[1]], 3: [first_slots[2]]})
-    output_line = jnp.concatenate(output_slots, 0)
+    output_line = jnp.concatenate(direct_gather(w_output), 0)
     output_full = gather_columns(output_line)
     gate_full = gather_rows(w_gate)
-    up_full = gather_rows(tied(w_up, output_line))
-    down_full = gather_columns(tied(w_down, output_line))
+    up_full = gather_rows(w_up)
+    down_full = gather_columns(w_down)
 
     joint = project(first_slots, inputs_full, places)
     heads, query, key, value = attention_forward(joint, held, sequences, groups)
     grad_slots = ring_gather(tied(cotangent, first_slots[-1]))
     heads_own = exchange(to_slots(heads, places, grad_slots[1]))
-    heads_own = jnp.concatenate(heads_own, 1)
-    mixed = base + dot(heads_own, output_full)
-    second, second_scale = normalize(mixed, gain_two)
-    second_slots = ring_gather(second.astype(low))
+    mixed = base + dot(jnp.concatenate(heads_own, 1), output_full)
+    second = normalize(mixed, gain_two)[0].astype(low)
+    second_slots = ring_gather(second)
     half = max(count // 2, 1)
     ahead = feed_forward(second_slots[:half], gate_full, up_full)
     rest = feed_forward(second_slots[half:], gate_full, up_full)
@@ -693,37 +991,66 @@
     block_parts = product(hidden, down_full)
     gate_grad, up_grad = feed_backward(grad_slots, down_full, gate, up, block_parts[0])
     block_moving = ring_shift(block_parts[1], 1)
-    second_parts = sum_of_products(((gate_grad, gate_full), (up_grad, up_full)), block_moving)
-    second_grad, second_back = ring_scatter(second_parts)
-    down_grad = sum_columns(weight_grad(hidden, grad_slots, second_parts[0]))
-    gate_wgrad = sum_rows(weight_grad(second_slots, gate_grad, second_parts[0]))
-    up_wgrad = sum_rows(weight_grad(second_slots, up_grad, second_parts[0]))
-
-    mixed_back, gain_two_part = norm_back(second_grad, mixed, second_scale, gain_two)
-    mixed_total = cotangent.astype(jnp.float32) + mixed_back
-    branch = mixed_total.astype(low)
-    heads_back = dot(branch, output_full, NT).astype(low).reshape(local, count, -1)
-    heads_grad = exchange([heads_back[:, slot] for slot in range(count)])
+    pick = lambda slots: ((([gate_grad[s] for s in slots]), gate_full), ([up_grad[s] for s in slots], up_full))
+    part_one = sum_of_products(pick([1]), block_moving)
+    others = [0] + list(range(2, count))
+    part_others = sum_of_products(pick(others), part_one[0])
+    second_parts = [part_others[0], part_one[0]] + list(part_others[1:])
+    second_early = ring_shift(second_parts[1], 1)
+    gate_wpart = weight_grad(second_slots, gate_grad, second_early)
+    gate_wgrad = sum_rows(gate_wpart)
+    second_grad, second_back = ring_scatter(second_parts, {3: [gate_wpart]}, 3)
+    up_wpart = weight_grad(second_slots, up_grad, second_back[1], half=0)
+
+    mixed_total, branch, heads_back = norm_split(
+        second_grad, mixed, gain_two, cotangent, output_full, count, up_wpart
+    )
+    heads_grad = exchange(heads_back)
+    both_wpart = weight_grad(grad_slots, hidden, branch, half=1, into=up_wpart)
+    both_wgrad = sum_rows(both_wpart)
     block_sum, block_back = ring_scatter(block_parts, {2: [second_back[-1]], 3: [heads_grad[-1]]})
-    block_out = mixed + block_sum
-    heads_grad = from_slots(heads_grad, places, block_back[1])
-    joint_grad = attention_backward(query, key, value, heads, heads_grad, held, groups)
-    joint_slots = to_slots(joint_grad, places)
-    first_parts = sum_of_products(((joint_slots, inputs_full),), block_back[2])
-    first_grad, first_back = ring_scatter(first_parts)
-    output_sum = scatter_product(heads_own, branch, 1).astype(low)
-    output_parts = output_sum.reshape(count, -1, output_sum.shape[1])
-    output_grad, _ = ring_scatter([output_parts[slot] for slot in range(count)])
-    inputs_grad = scatter_product(jnp.concatenate(first_slots, 0), jnp.concatenate(joint_slots, 0), 0)
-    base_back, gain_one_part = norm_back(first_grad, base, first_scale, gain_one)
-    tokens_grad = (mixed_total + base_back).astype(low)
+    cube = lax.axis_size("dp") == 8
+    output_parts = cube_columns(heads_own, branch, both_wpart) if cube else ()
+    joint_grad = attention_backward(
+        query, key, value, heads, heads_grad, places, held, groups, block_back[1], both_wpart, *output_parts[:1]
+    )
+    first_one = spread_product(joint_grad, inputs_full, places, [1], block_back[2])
+    first_others = spread_product(joint_grad, inputs_full, places, others, first_one[0])
+    first_parts = [first_others[0], first_one[0]] + list(first_others[1:])
+    gate_wgrad, gate_share = widen([gate_wgrad], w_gate)
+    if cube:
+        output_pairs = cube_pairs(output_parts, first_one[0])
+        output_turns = cube_turns(output_pairs)
+        inputs_parts = cube_rows(first_slots, joint_grad, places, HEAVY, output_pairs[0])
+        second_pause = [output_turns[0], inputs_parts[0]]
+        first_next = tied_sum(ring_shift(first_parts[1], 1), first_parts[2], 0, *second_pause)
+        inputs_pairs = cube_pairs(inputs_parts, first_next)
+        third_pause = [inputs_pairs[0], gate_wgrad]
+        first_last = tied_sum(ring_shift(first_next, 1), first_parts[3], 0, *third_pause)
+        inputs_turns = cube_turns(inputs_pairs, first_last)
+        output_sum = cube_total(output_pairs, output_turns, low, first_last)
+        first_grad, first_back = ring_scatter(first_parts, {2: second_pause, 3: third_pause})
+        block_out = total_of((*block_sum, mixed), low, first_last)
+        inputs_grad, inputs_share = widen(cube_terms(inputs_pairs, inputs_turns), w_inputs)
+    else:
+        first_grad, first_back = ring_scatter(first_parts)
+        block_out = total_of((*block_sum, mixed), low)
+        output_sum = sum_columns(weight_grad([jnp.concatenate(heads_own, 1)], [branch]))
+        inputs_grad = sum_rows(weight_grad(first_slots, to_slots(joint_grad, places)))
+        inputs_grad, inputs_share = widen([inputs_grad], w_inputs)
+    output_cut = output_sum.reshape(count, -1, output_sum.shape[1])
+    output_grad = total_of(exchange([output_cut[slot] for slot in range(count)]), jnp.float32)
+    up_wgrad, up_share = widen([both_wgrad], w_up)
+    down_grad = widen_turned(both_wgrad, 1)
+    gain_grads = gain_sums([inputs_share, gate_share + up_share], [gain_one, gain_two], places)
+    tokens_grad = norm_backward(first_grad, tokens, gain_one, mixed_total)
     return (
-        block_out.astype(low),
+        block_out,
         tokens_grad,
-        sum_gain(gain_one_part, places),
+        gain_grads[0],
         inputs_grad,
         output_grad,
-        sum_gain(gain_two_part, places),
+        gain_grads[1],
         gate_wgrad,
         up_wgrad,
         down_grad,

time: 817 us -> 683 us (0.84)
  waiting for transfers between devices: 377 us -> 253 us
  Pallas kernels: 225 us -> 302 us
  other arithmetic: 51.4 us -> 14 us
  matrix products: 36.3 us -> 7.86 us
  local copies, waits for them, and re-layouts: 29.4 us -> 18 us
  starting transfers between devices: 69.2 us -> 61 us
    ppermute x36 -> x33, waiting for transfers between devices: 355 us -> 222 us  [ring_shift(): lax.ppermute(value, 'tensor', [(order[k], order[(k + by) % count]) for k...]
    pallas_call x1 -> x5, Pallas kernels: 21.8 us -> 72.1 us  [the longest x3 50.5 us: weight_grad(): pl.pallas_call(kernel, grid=(extent // wide,), in_specs=[column_block(row...]
    dot_general x11 -> x1, matrix products: 36.3 us -> 7.86 us  [dot(): lax.dot_general(left, right, dims, preferred_element_type=jnp.float32)]
    pallas_call x20 -> x30, Pallas kernels: 184 us -> 211 us  [call(): pl.pallas_call(lambda *refs: kernel(*refs[:count], *refs[count + extra:])...]
    convert_element_type x8 -> x2, other arithmetic: 17.8 us -> 0.76 us  [the longest x1 0.42 us: per_device(): second = normalize(mixed, gain_two)[0].astype(low)]
    ppermute x16 -> x10, waiting for transfers between devices: 10.9 us -> 24.7 us  [flip(): return lax.ppermute(value, 'dp', [(k, k ^ bits) for k in range(count)])]
    ppermute x36 -> x33, starting transfers between devices: 50.9 us -> 51.7 us  [ring_shift(): lax.ppermute(value, 'tensor', [(order[k], order[(k + by) % count]) for k...]
  transfers between devices with their start and end apart: 66 -> 50, of which waited for: 30 -> 20; matrix products, arithmetic and copies ran while one was open for 13% -> 3% of each run, Pallas kernels for 22% -> 42%
where the time goes in v2:
time: 683 us; the launch traced here: 678 us
  Pallas kernels  302 us (44%)
  waiting for transfers between devices  253 us (37%)
  starting transfers between devices  61 us (9%)
  between operations  22.6 us (3%)
  local copies, waits for them, and re-layouts  18 us (3%)
  other arithmetic  14 us (2%)
  matrix products  7.86 us (1%)
    ppermute x33, waiting for transfers between devices, ring_shift(): lax.ppermute(value, 'tensor', [(order[k], order[(k + by) % count]) for k...  222 us
    pallas_call x30, Pallas kernels, call(): pl.pallas_call(lambda *refs: kernel(*refs[:count], *refs[count + extra:])...  211 us
    ppermute x33, starting transfers between devices, ring_shift(): lax.ppermute(value, 'tensor', [(order[k], order[(k + by) % count]) for k...  51.7 us
    pallas_call x3, Pallas kernels, weight_grad(): pl.pallas_call(kernel, grid=(extent // wide,), in_specs=[column_block(row...  50.5 us
    ppermute x10, waiting for transfers between devices, flip(): return lax.ppermute(value, 'dp', [(k, k ^ bits) for k in range(count)])  24.7 us
    pallas_call x2, Pallas kernels, cube_call(): pl.pallas_call(body, grid_spec=pltpu.PrefetchScalarGridSpec(num_scalar_pr...  21.6 us
    pallas_call x1, Pallas kernels, attention_forward(): pl.pallas_call(lambda *refs: forward_kernel(count, *refs), grid=(groups,)...  19.1 us
    unnamed x72, local copies, waits for them, and re-layouts  14.8 us
  transfers between devices with their start and end apart: 50, of which 20 were waited for; matrix products, arithmetic and copies ran while one was open for 3% of the time, Pallas kernels for 42%

profile of v2, /device:TPU:0, one launch (start us, length us, event | category | flops | bytes accessed | tf_op | source)
XLA Modules:
  0.0 678.2 jit_solution(10547483547716642252)
XLA Ops:
  42.2 26.9 %collective-permute-done.refs_1_ = bf16[288,2048]{1,0:T(8,128)(2,1)S(1)} collective-permute-done((bf16[288,2048]{1,0:T(8,128)(2,1)S(1)}, bf16[288,2048]{1,0:T(8,128)(2,1)S(1)}, u32[]{:S(2)}, u32[]{:S(2)}) %collective-permute-start) | collective-permute-done | bytes 1179680 | tf_op jit(solution)/shard_map/ppermute | solution.py:849
  70.1 26.2 %collective-permute-done.1.refs_2_ = bf16[288,2048]{1,0:T(8,128)(2,1)} collective-permute-done((bf16[288,2048]{1,0:T(8,128)(2,1)S(1)}, bf16[288,2048]{1,0:T(8,128)(2,1)}, u32[]{:S(2)}, u32[]{:S(2)}) %collective-permute-start.1) | collective-permute-done | bytes 1179680 | tf_op jit(solution)/shard_map/ppermute | solution.py:849
  100.6 22.0 %collective-permute-done.2.refs_3_.refs_1_ = bf16[288,2048]{1,0:T(8,128)(2,1)S(1)} collective-permute-done((bf16[288,2048]{1,0:T(8,128)(2,1)}, bf16[288,2048]{1,0:T(8,128)(2,1)S(1)}, u32[]{:S(2)}, u32[]{:S(2)}) %collective-permute-start.2) | collective-permute-done | bytes 1179680 | tf_op jit(solution)/shard_map/ppermute | solution.py:849
  126.4 8.3 %shard_map.169.refs_0_ = f32[1152,768]{1,0:T(8,128)} custom-call(bf16[288,2048]{1,0:T(8,128)(2,1)} %copy-done.9, bf16[288,2048]{1,0:T(8,128)(2,1)} %copy-done.30, bf16[288,2048]{1,0:T(8,128)(2,1)} %collective-permute-done.1.refs_2_, bf16[288,2048]{1,0:T(8,128)(2,1)} %copy-done.7, s32[4]{0:T(128)} %fusion.28.refs_4_.refs_1_.refs_8_.refs_5_, ...), custom_call_target="tpu_custom_call" | custom-call | flops 3623878656 | bytes 1048576 | tf_op jit(solution)/shard_map/pallas_call | solution.py:259
  134.7 19.1 %shard_map.170 = (bf16[1152,512]{1,0:T(8,128)(2,1)}, bf16[2,4,1152,128]{3,2,1,0:T(8,128)(2,1)}, bf16[2,1152,128]{2,1,0:T(8,128)(2,1)}, bf16[2,1152,128]{2,1,0:T(8,128)(2,1)}) custom-call(f32[1152,768]{1,0:T(8,128)} %shard_map.169.refs_0_, f32[1152,128]{1,0:T(8,128)} %get-tuple-element.154.refs_1_.refs_9_, f32[1152,128]{1,0:T(8,128)} %get-tuple-element.153.refs_2_.refs_10_, ...), custom_call_target="tpu_custom_call" | custom-call | flops 8153726976 | bytes 1048576 | tf_op jit(solution)/shard_map/pallas_call | solution.py:142
  161.7 18.2 %collective-permute-done.4.refs_1_ = bf16[288,512]{1,0:T(8,128)(2,1)S(1)} collective-permute-done((bf16[288,512]{1,0:T(8,128)(2,1)}, bf16[288,512]{1,0:T(8,128)(2,1)S(1)}, u32[]{:S(2)}, u32[]{:S(2)}) %collective-permute-start.4) | collective-permute-done | bytes 294944 | tf_op jit(solution)/shard_map/ppermute | solution.py:849
  192.5 23.5 %collective-permute-done.10.refs_1_ = bf16[288,2048]{1,0:T(8,128)(2,1)S(1)} collective-permute-done((bf16[288,2048]{1,0:T(8,128)(2,1)S(1)}, bf16[288,2048]{1,0:T(8,128)(2,1)S(1)}, u32[]{:S(2)}, u32[]{:S(2)}) %collective-permute-start.10) | collective-permute-done | bytes 1179680 | tf_op jit(solution)/shard_map/ppermute | solution.py:849
  218.6 27.3 %collective-permute-done.11.refs_0_.refs_2_ = bf16[288,2048]{1,0:T(8,128)(2,1)} collective-permute-done((bf16[288,2048]{1,0:T(8,128)(2,1)S(1)}, bf16[288,2048]{1,0:T(8,128)(2,1)}, u32[]{:S(2)}, u32[]{:S(2)}) %collective-permute-start.11) | collective-permute-done | bytes 1179680 | tf_op jit(solution)/shard_map/ppermute | solution.py:849
  247.5 23.6 %collective-permute-done.14.refs_2_ = bf16[288,2048]{1,0:T(8,128)(2,1)S(1)} collective-permute-done((bf16[288,2048]{1,0:T(8,128)(2,1)S(1)}, bf16[288,2048]{1,0:T(8,128)(2,1)S(1)}, u32[]{:S(2)}, u32[]{:S(2)}) %collective-permute-start.14) | collective-permute-done | bytes 1179680 | tf_op jit(solution)/shard_map/ppermute | solution.py:849
  272.7 16.0 %shard_map.173 = (bf16[288,2048]{1,0:T(8,128)(2,1)}, bf16[288,2048]{1,0:T(8,128)(2,1)}, bf16[288,2048]{1,0:T(8,128)(2,1)}, bf16[288,2048]{1,0:T(8,128)(2,1)}, bf...) custom-call(bf16[288,2048]{1,0:T(8,128)(2,1)} %copy-done.11, bf16[288,2048]{1,0:T(8,128)(2,1)} %copy-done.31, ...), custom_call_target="tpu_custom_call" | custom-call | flops 9663676416 | bytes 1048576 | tf_op jit(solution)/shard_map/pallas_call | solution.py:259
  296.5 16.1 %shard_map.174 = (bf16[288,2048]{1,0:T(8,128)(2,1)}, bf16[288,2048]{1,0:T(8,128)(2,1)}, bf16[288,2048]{1,0:T(8,128)(2,1)}, bf16[288,2048]{1,0:T(8,128)(2,1)}, bf...) custom-call(bf16[288,2048]{1,0:T(8,128)(2,1)} %collective-permute-done.11.refs_0_.refs_2_, ...), custom_call_target="tpu_custom_call" | custom-call | flops 9663676416 | bytes 1048576 | tf_op jit(solution)/shard_map/pallas_call | solution.py:259
  312.6 14.7 %shard_map.175 = (bf16[288,2048]{1,0:T(8,128)(2,1)}, bf16[288,2048]{1,0:T(8,128)(2,1)}, bf16[288,2048]{1,0:T(8,128)(2,1)}, bf16[288,2048]{1,0:T(8,128)(2,1)}) custom-call(bf16[288,2048]{1,0:T(8,128)(2,1)} %get-tuple-element.82.refs_0_.refs_4_, bf16[288,2048]{1,0:T(8,128)(2,1)} %get-tuple-element.83.refs_1_.refs_5_, ...), custom_call_target="tpu_custom_call" | custom-call | flops 9663676416 | bytes 1048576 | tf_op jit(solution)/shard_map/pallas_call | solution.py:259
  330.0 18.7 %shard_map.176 = (bf16[288,2048]{1,0:T(8,128)(2,1)}, bf16[288,2048]{1,0:T(8,128)(2,1)}, bf16[288,2048]{1,0:T(8,128)(2,1)}, bf16[288,2048]{1,0:T(8,128)(2,1)}, bf...) custom-call(bf16[288,2048]{1,0:T(8,128)(2,1)} %shard_map.171.refs_0_, ...), custom_call_target="tpu_custom_call" | custom-call | flops 9663676416 | bytes 1048576 | tf_op jit(solution)/shard_map/pallas_call | solution.py:259
  349.8 12.3 %shard_map.177.refs_8_ = bf16[288,2048]{1,0:T(8,128)(2,1)} custom-call(bf16[288,2048]{1,0:T(8,128)(2,1)} %get-tuple-element.97.refs_0_.refs_5_, bf16[288,2048]{1,0:T(8,128)(2,1)} %get-tuple-element.98.refs_1_.refs_5_, bf16[2048,2048]{1,0:T(8,128)(2,1)} %all-gather.10.cloned.1.call-done.refs_2_.refs_6_, ...), custom_call_target="tpu_custom_call" | custom-call | flops 4831838208 | bytes 1048576 | tf_op jit(solution)/shard_map/pallas_call | solution.py:259
  363.1 20.9 %shard_map.178 = (bf16[288,2048]{1,0:T(8,128)(2,1)}, bf16[288,2048]{1,0:T(8,128)(2,1)}, bf16[288,2048]{1,0:T(8,128)(2,1)}) custom-call(bf16[288,2048]{1,0:T(8,128)(2,1)} %get-tuple-element.99.refs_0_.refs_4_, bf16[288,2048]{1,0:T(8,128)(2,1)} %get-tuple-element.100.refs_1_.refs_6_, bf16[288,2048]{1,0:T(8,128)(2,1)} %get-tuple-element.101.refs_2_.refs_7_, ...), custom_call_target="tpu_custom_call" | custom-call | flops 14495514624 | bytes 1048576 | tf_op jit(solution)/shard_map/pallas_call | solution.py:259
  386.2 16.7 %shard_map.179.refs_2_ = bf16[2048,2048]{1,0:T(8,128)(2,1)} custom-call(bf16[288,2048]{1,0:T(8,128)(2,1)} %copy-done.11, bf16[288,2048]{1,0:T(8,128)(2,1)} %copy-done.31, bf16[288,2048]{1,0:T(8,128)(2,1)} %collective-permute-done.11.refs_0_.refs_2_, bf16[288,2048]{1,0:T(8,128)(2,1)} %collective-permute-done.12.refs_1_.refs_3_, ...), custom_call_target="tpu_custom_call" | custom-call | flops 9663676416 | bytes 1048576 | tf_op jit(solution)/shard_map/pallas_call | solution.py:514
  412.2 16.9 %shard_map.182.refs_6_.refs_8_ = bf16[2048,4096]{1,0:T(8,128)(2,1)} custom-call(bf16[288,2048]{1,0:T(8,128)(2,1)} %copy-done.11, bf16[288,2048]{1,0:T(8,128)(2,1)} %copy-done.31, bf16[288,2048]{1,0:T(8,128)(2,1)} %collective-permute-done.11.refs_0_.refs_2_, bf16[288,2048]{1,0:T(8,128)(2,1)} %collective-permute-done.12.refs_1_.refs_3_, ...), custom_call_target="tpu_custom_call" | custom-call | flops 9663676416 | bytes 1048576 | tf_op jit(solution)/shard_map/pallas_call | solution.py:514
  438.2 11.9 %shard_map.183 = (f32[288,2048]{1,0:T(8,128)}, bf16[288,2048]{1,0:T(8,128)(2,1)}, bf16[288,512]{1,0:T(8,128)(2,1)}, bf16[288,512]{1,0:T(8,128)(2,1)}, bf16[288,5...) custom-call(bf16[288,2048]{1,0:T(8,128)(2,1)} %get-tuple-element.108.refs_0_, bf16[288,2048]{1,0:T(8,128)(2,1)} %copy-done.12, ...), custom_call_target="tpu_custom_call" | custom-call | flops 999999995904 | bytes 1048576 | tf_op jit(solution)/shard_map/pallas_call | solution.py:259
  455.7 16.8 %shard_map.185.refs_5_.refs_12_ = bf16[2048,4096]{1,0:T(8,128)(2,1)} custom-call(bf16[288,2048]{1,0:T(8,128)(2,1)} %shard_map.171.refs_0_, bf16[288,2048]{1,0:T(8,128)(2,1)} %copy-done.1, bf16[288,2048]{1,0:T(8,128)(2,1)} %copy-done.5, bf16[288,2048]{1,0:T(8,128)(2,1)} %copy-done.6, ...), custom_call_target="tpu_custom_call", output_to_operand_aliasing={{}: (8, {})} | custom-call | flops 9663676416 | bytes 1048576 | tf_op jit(solution)/shard_map/pallas_call | solution.py:514
  472.5 10.8 %shard_map.186 = (bf16[4,2048,256]{2,1,0:T(8,128)(2,1)}, bf16[4,2048,256]{2,1,0:T(8,128)(2,1)}) custom-call(s32[1]{0:T(128)} %bitcast.5.me, bf16[288,512]{1,0:T(8,128)(2,1)} %get-tuple-element.78.refs_0_, bf16[288,512]{1,0:T(8,128)(2,1)} %copy-done.17, bf16[288,512]{1,0:T(8,128)(2,1)} %copy-done.18, bf16[288,512]{1,0:T(8,128)(2,1)} %copy-done.19, ...), custom_call_target="tpu_custom_call" | custom-call | flops 2415919104 | bytes 1048576 | tf_op jit(solution)/shard_map/pallas_call | solution.py:575
  488.2 22.0 %shard_map.187.refs_0_.refs_4_ = bf16[1152,768]{1,0:T(8,128)(2,1)} custom-call(bf16[2,4,1152,128]{3,2,1,0:T(8,128)(2,1)} %get-tuple-element.110.refs_0_, bf16[2,1152,128]{2,1,0:T(8,128)(2,1)} %get-tuple-element.111.refs_1_, bf16[2,1152,128]{2,1,0:T(8,128)(2,1)} %get-tuple-element.112.refs_2_, bf16[1152,512]{1,0:T(8,128)(2,1)} %get-tuple-element.77.refs_0_.refs_3_, ...), custom_call_target="tpu_custom_call" | custom-call | flops 999999995904 | bytes 1048576 | tf_op jit(solution)/shard_map/pallas_call | solution.py:259
  529.8 10.8 %shard_map.192 = (bf16[4,256,768]{2,1,0:T(8,128)(2,1)}, bf16[4,256,768]{2,1,0:T(8,128)(2,1)}) custom-call(s32[1]{0:T(128)} %bitcast.5.me, bf16[288,2048]{1,0:T(8,128)(2,1)} %copy-done.9, bf16[288,2048]{1,0:T(8,128)(2,1)} %copy-done.30, bf16[288,2048]{1,0:T(8,128)(2,1)} %collective-permute-done.1.refs_2_, bf16[288,2048]{1,0:T(8,128)(2,1)} %copy-done.7, ...), custom_call_target="tpu_custom_call" | custom-call | flops 999999995904 | bytes 1048576 | tf_op jit(solution)/shard_map/pallas_call | solution.py:575
  572.8 14.6 %collective-permute-done.28.refs_0_ = bf16[288,2048]{1,0:T(8,128)(2,1)S(1)} collective-permute-done((bf16[288,2048]{1,0:T(8,128)(2,1)}, bf16[288,2048]{1,0:T(8,128)(2,1)S(1)}, u32[]{:S(2)}, u32[]{:S(2)}) %collective-permute-start.28) | collective-permute-done | bytes 1179680 | tf_op jit(solution)/shard_map/ppermute | solution.py:849
  591.9 17.6 %collective-permute-done.31.refs_2_ = bf16[128,768]{1,0:T(8,128)(2,1)S(1)} collective-permute-done((bf16[128,768]{1,0:T(8,128)(2,1)}, bf16[128,768]{1,0:T(8,128)(2,1)S(1)}, u32[]{:S(2)}, u32[]{:S(2)}) %collective-permute-start.31) | collective-permute-done | bytes 196640 | tf_op jit(solution)/shard_map/ppermute | solution.py:904
  (223 shorter events, 223.6 us)
Async XLA Ops:
  7.2 119.3 %all-gather.6.cloned.1.call-start = ((), (), s32[]{:S(2)}) async-start(), calls=%async_computation.2 | async-start | bytes 3538944 | tf_op jit(solution)/shard_map/all_gather | solution.py:926
  7.9 172.0 %all-gather.8.cloned.1.call-start = ((), (), s32[]{:S(2)}) async-start(), calls=%async_computation.3 | async-start | bytes 9437184 | tf_op jit(solution)/shard_map/all_gather | solution.py:930
  31.8 240.9 %all-gather.10.cloned.1.call-start = ((), (), s32[]{:S(2)}) async-start(), calls=%async_computation.4 | async-start | bytes 9437184 | tf_op jit(solution)/shard_map/all_gather | solution.py:926
  32.6 240.1 %all-gather.12.cloned.1.call-start = ((), (), s32[]{:S(2)}) async-start(), calls=%async_computation.5 | async-start | bytes 9437184 | tf_op jit(solution)/shard_map/all_gather | solution.py:926
  33.2 279.5 %all-gather.14.cloned.1.call-start = ((), (), s32[]{:S(2)}) async-start(), calls=%async_computation.6 | async-start | bytes 9437184 | tf_op jit(solution)/shard_map/all_gather | solution.py:930
  33.7 536.3 %reduce-scatter.3.cloned.1.call-start = ((), (), s32[]{:S(2)}) async-start(), calls=%async_computation.7 | async-start | bytes 9437184 | tf_op jit(solution)/shard_map/reduce_scatter | solution.py:934
  35.6 33.5 %collective-permute-start = (bf16[288,2048]{1,0:T(8,128)(2,1)S(1)}, bf16[288,2048]{1,0:T(8,128)(2,1)S(1)}, u32[]{:S(2)}, u32[]{:S(2)}) collective-permute-start(bf16[288,2048]{1,0:T(8,128)(2,1)S(1)} %fusion.7.refs_0_), channel_id=1, source_target_pairs={{0,1},{1,3},{3,2},{2,0},{4,5},{5,7},{7,6},{6,4},{8,9},{9,11},{11,1... | collective-permute-start | bytes 3538952 | tf_op jit(solution)/shard_map/ppermute | solution.py:849
  216.0 29.9 %collective-permute-start.11 = (bf16[288,2048]{1,0:T(8,128)(2,1)S(1)}, bf16[288,2048]{1,0:T(8,128)(2,1)}, u32[]{:S(2)}, u32[]{:S(2)}) collective-permute-start(bf16[288,2048]{1,0:T(8,128)(2,1)S(1)} %collective-permute-done.10.refs_1_), channel_id=1, source_target_pairs={{0,1},{1,3},{3,2},{2,0},{4,5},{5,7},{7,6},{6,4},{8,9},{9,11},{11,1... | collective-permute-start | bytes 3538952 | tf_op jit(solution)/shard_map/ppermute | solution.py:849
  218.5 52.6 %collective-permute-start.14 = (bf16[288,2048]{1,0:T(8,128)(2,1)S(1)}, bf16[288,2048]{1,0:T(8,128)(2,1)S(1)}, u32[]{:S(2)}, u32[]{:S(2)}) collective-permute-start(bf16[288,2048]{1,0:T(8,128)(2,1)S(1)} %copy-done.2), channel_id=1, source_target_pairs={{0,1},{1,3},{3,2},{2,0},{4,5},{5,7},{7,6},{6,4},{8,9},{9,11},{11,1... | collective-permute-start | bytes 3538952 | tf_op jit(solution)/shard_map/ppermute | solution.py:849
  245.9 50.6 %collective-permute-start.12 = (bf16[288,2048]{1,0:T(8,128)(2,1)}, bf16[288,2048]{1,0:T(8,128)(2,1)}, u32[]{:S(2)}, u32[]{:S(2)}) collective-permute-start(bf16[288,2048]{1,0:T(8,128)(2,1)} %collective-permute-done.11.refs_0_.refs_2_), channel_id=1, source_target_pairs={{0,1},{1,3},{3,2},{2,0},{4,5},{5,7},{7,6},{6,4},{8,9},{9,11},{11,1... | collective-permute-start | bytes 3538952 | tf_op jit(solution)/shard_map/ppermute | solution.py:849
  271.1 57.8 %collective-permute-start.15 = (bf16[288,2048]{1,0:T(8,128)(2,1)S(1)}, bf16[288,2048]{1,0:T(8,128)(2,1)S(1)}, u32[]{:S(2)}, u32[]{:S(2)}) collective-permute-start(bf16[288,2048]{1,0:T(8,128)(2,1)S(1)} %collective-permute-done.14.refs_2_), channel_id=1, source_target_pairs={{0,1},{1,3},{3,2},{2,0},{4,5},{5,7},{7,6},{6,4},{8,9},{9,11},{11,1... | collective-permute-start | bytes 3538952 | tf_op jit(solution)/shard_map/ppermute | solution.py:849
  412.1 233.0 %reduce-scatter.5.cloned.1.call-start = ((), (), s32[]{:S(2)}) async-start(), calls=%async_computation.8 | async-start | bytes 18874368 | tf_op jit(solution)/shard_map/reduce_scatter | solution.py:934
  438.0 45.4 %collective-permute-start.19 = (bf16[288,2048]{1,0:T(8,128)(2,1)}, bf16[288,2048]{1,0:T(8,128)(2,1)}, u32[]{:S(2)}, u32[]{:S(2)}) collective-permute-start(bf16[288,2048]{1,0:T(8,128)(2,1)} %shard_map.181), channel_id=1, source_target_pairs={{0,1},{1,3},{3,2},{2,0},{4,5},{5,7},{7,6},{6,4},{8,9},{9,11},{11,1... | collective-permute-start | bytes 3538952 | tf_op jit(solution)/shard_map/ppermute | solution.py:849
  450.0 33.3 %collective-permute-start.20 = (bf16[288,512]{1,0:T(8,128)(2,1)}, bf16[288,512]{1,0:T(8,128)(2,1)S(1)}, u32[]{:S(2)}, u32[]{:S(2)}) collective-permute-start(bf16[288,512]{1,0:T(8,128)(2,1)} %get-tuple-element.109), channel_id=1, source_target_pairs={{0,2},{1,0},{3,1},{2,3},{4,6},{5,4},{7,5},{6,7},{8,10},{9,8},{11,9... | collective-permute-start | bytes 884744 | tf_op jit(solution)/shard_map/ppermute | solution.py:849
  452.9 34.5 %collective-permute-start.22 = (bf16[288,512]{1,0:T(8,128)(2,1)}, bf16[288,512]{1,0:T(8,128)(2,1)S(1)}, u32[]{:S(2)}, u32[]{:S(2)}) collective-permute-start(bf16[288,512]{1,0:T(8,128)(2,1)} %get-tuple-element.114), channel_id=1, source_target_pairs={{0,1},{1,3},{3,2},{2,0},{4,5},{5,7},{7,6},{6,4},{8,9},{9,11},{11,1... | collective-permute-start | bytes 884744 | tf_op jit(solution)/shard_map/ppermute | solution.py:849
  452.9 34.5 %collective-permute-start.23 = (bf16[288,512]{1,0:T(8,128)(2,1)}, bf16[288,512]{1,0:T(8,128)(2,1)S(1)}, u32[]{:S(2)}, u32[]{:S(2)}) collective-permute-start(bf16[288,512]{1,0:T(8,128)(2,1)} %get-tuple-element.115), channel_id=1, source_target_pairs={{0,3},{1,2},{3,0},{2,1},{4,7},{5,6},{7,4},{6,5},{8,11},{9,10},{11,... | collective-permute-start | bytes 884744 | tf_op jit(solution)/shard_map/ppermute | solution.py:849
  483.3 37.4 %collective-permute-start.25 = (bf16[4,2048,256]{2,1,0:T(8,128)(2,1)}, bf16[4,2048,256]{2,1,0:T(8,128)(2,1)}, u32[]{:S(2)}, u32[]{:S(2)}) collective-permute-start(bf16[4,2048,256]{2,1,0:T(8,128)(2,1)} %get-tuple-element.117.refs_13_), channel_id=1, source_target_pairs={{0,4},{4,0},{8,12},{12,8},{16,20},{20,16},{24,28},{28,24},{1,5},{5... | collective-permute-start | bytes 12582920 | tf_op jit(solution)/shard_map/ppermute | solution.py:904
  486.7 29.6 %collective-permute-start.21 = (bf16[288,2048]{1,0:T(8,128)(2,1)}, bf16[288,2048]{1,0:T(8,128)(2,1)}, u32[]{:S(2)}, u32[]{:S(2)}) collective-permute-start(bf16[288,2048]{1,0:T(8,128)(2,1)} %shard_map.184), channel_id=1, source_target_pairs={{0,1},{1,3},{3,2},{2,0},{4,5},{5,7},{7,6},{6,4},{8,9},{9,11},{11,1... | collective-permute-start | bytes 3538952 | tf_op jit(solution)/shard_map/ppermute | solution.py:849
  520.5 36.5 %collective-permute-start.24 = (bf16[288,2048]{1,0:T(8,128)(2,1)}, bf16[288,2048]{1,0:T(8,128)(2,1)}, u32[]{:S(2)}, u32[]{:S(2)}) collective-permute-start(bf16[288,2048]{1,0:T(8,128)(2,1)} %shard_map.188.refs_3_.refs_2_), channel_id=1, source_target_pairs={{0,1},{1,3},{3,2},{2,0},{4,5},{5,7},{7,6},{6,4},{8,9},{9,11},{11,1... | collective-permute-start | bytes 3538952 | tf_op jit(solution)/shard_map/ppermute | solution.py:849
  561.6 61.2 %collective-permute-start.38 = (bf16[2048,256]{1,0:T(8,128)(2,1)S(1)}, bf16[2048,256]{1,0:T(8,128)(2,1)S(1)}, u32[]{:S(2)}, u32[]{:S(2)}) collective-permute-start(bf16[2048,256]{1,0:T(8,128)(2,1)S(1)} %copy-done.14), channel_id=1, source_target_pairs={{0,8},{4,12},{8,0},{12,4},{16,24},{20,28},{24,16},{28,20},{1,9},{5... | collective-permute-start | bytes 3145736 | tf_op jit(solution)/shard_map/ppermute | solution.py:904
  562.0 60.8 %collective-permute-start.39 = (bf16[2048,256]{1,0:T(8,128)(2,1)}, bf16[2048,256]{1,0:T(8,128)(2,1)}, u32[]{:S(2)}, u32[]{:S(2)}) collective-permute-start(bf16[2048,256]{1,0:T(8,128)(2,1)} %get-tuple-element.143), channel_id=1, source_target_pairs={{0,16},{4,20},{8,24},{12,28},{16,0},{20,4},{24,8},{28,12},{1,17},{... | collective-permute-start | bytes 3145736 | tf_op jit(solution)/shard_map/ppermute | solution.py:904
  568.0 41.4 %collective-permute-start.31 = (bf16[128,768]{1,0:T(8,128)(2,1)}, bf16[128,768]{1,0:T(8,128)(2,1)S(1)}, u32[]{:S(2)}, u32[]{:S(2)}) collective-permute-start(bf16[128,768]{1,0:T(8,128)(2,1)} %get-tuple-element.135), channel_id=1, source_target_pairs={{0,8},{4,12},{8,0},{12,4},{16,24},{20,28},{24,16},{28,20},{1,9},{5... | collective-permute-start | bytes 589832 | tf_op jit(solution)/shard_map/ppermute | solution.py:904
  569.9 39.7 %collective-permute-start.32 = (bf16[128,768]{1,0:T(8,128)(2,1)}, bf16[128,768]{1,0:T(8,128)(2,1)}, u32[]{:S(2)}, u32[]{:S(2)}) collective-permute-start(bf16[128,768]{1,0:T(8,128)(2,1)} %get-tuple-element.136), channel_id=1, source_target_pairs={{0,16},{4,20},{8,24},{12,28},{16,0},{20,4},{24,8},{28,12},{1,17},{... | collective-permute-start | bytes 589832 | tf_op jit(solution)/shard_map/ppermute | solution.py:904
  591.0 67.6 %collective-permute-start.30 = (bf16[288,2048]{1,0:T(8,128)(2,1)}, bf16[288,2048]{1,0:T(8,128)(2,1)S(1)}, u32[]{:S(2)}, u32[]{:S(2)}) collective-permute-start(bf16[288,2048]{1,0:T(8,128)(2,1)} %shard_map.196.refs_3_.refs_4_), channel_id=1, source_target_pairs={{0,1},{1,3},{3,2},{2,0},{4,5},{5,7},{7,6},{6,4},{8,9},{9,11},{11,1... | collective-permute-start | bytes 3538952 | tf_op jit(solution)/shard_map/ppermute | solution.py:849
  (62 other events, 876.0 us)
Sparse Core Ops, SparseCore 0:
  9.9 35.0 all-gather.5
  46.8 55.9 all-gather.7
  104.7 54.3 all-gather.9
  160.9 54.3 all-gather.11
  217.1 55.9 all-gather.13
  412.3 72.1 reduce-scatter.2
  488.5 156.6 reduce-scatter.4

commit v3 on v2

--- a/solution.py
+++ b/solution.py
@@ -675,6 +675,30 @@
     )
 
 
+def total_slots(terms, count, *earlier):
+    rows, width = terms[0].shape
+    local = rows // count
+
+    def kernel(*refs):
+        for slot in range(count):
+            at = slice(slot * local, (slot + 1) * local)
+            total = refs[0][at, :].astype(jnp.float32)
+            for ref in refs[1 : len(terms)]:
+                total = total + ref[at, :].astype(jnp.float32)
+            refs[len(terms) + slot][...] = total.astype(jnp.bfloat16)
+
+    return call(
+        kernel,
+        1,
+        tuple(terms),
+        [whole(rows, width)] * len(terms),
+        [whole(local, width)] * count,
+        [low_shape(local, width)] * count,
+        0,
+        earlier,
+    )
+
+
 def cube_turn(over_x, over_y, from_x, from_y, *earlier):
     rows, width = over_x.shape
     half = rows // 2
@@ -699,7 +723,7 @@
     )
 
 
-def total_of(terms, dtype, *earlier):
+def total_of(terms, dtype, *earlier, cost=0):
     rows, width = terms[0].shape
     wide = rows // 2 if rows % 32 == 0 else rows
 
@@ -782,7 +806,7 @@
         [block] * 2 + [whole(rows, wide)] * count,
         [jax.ShapeDtypeStruct((rows, width), jnp.float32), low_shape(rows, width)]
         + [low_shape(rows, wide)] * count,
-        HEAVY,
+        HEAVY // 32,
         earlier,
     )
     return out[0], out[1], out[2:]
@@ -817,7 +841,7 @@
 def widen_turned(value, part):
     rows, width = value.shape
     width = width // 2
-    wide = 256 if width % 256 == 0 else width
+    wide = 512 if width % 512 == 0 else width
     blocks = width // wide
 
     def kernel(source, target):
@@ -982,7 +1006,7 @@
     grad_slots = ring_gather(tied(cotangent, first_slots[-1]))
     heads_own = exchange(to_slots(heads, places, grad_slots[1]))
     mixed = base + dot(jnp.concatenate(heads_own, 1), output_full)
-    second = normalize(mixed, gain_two)[0].astype(low)
+    second = tied(normalize(mixed, gain_two)[0].astype(low), grad_slots[min(2, count - 1)])
     second_slots = ring_gather(second)
     half = max(count // 2, 1)
     ahead = feed_forward(second_slots[:half], gate_full, up_full)
@@ -1028,9 +1052,9 @@
         third_pause = [inputs_pairs[0], gate_wgrad]
         first_last = tied_sum(ring_shift(first_next, 1), first_parts[3], 0, *third_pause)
         inputs_turns = cube_turns(inputs_pairs, first_last)
-        output_sum = cube_total(output_pairs, output_turns, low, first_last)
+        output_cut = total_slots(cube_terms(output_pairs, output_turns), count, first_last)
         first_grad, first_back = ring_scatter(first_parts, {2: second_pause, 3: third_pause})
-        block_out = total_of((*block_sum, mixed), low, first_last)
+        block_out = total_of((*block_sum, mixed), low, first_last, cost=HEAVY)
         inputs_grad, inputs_share = widen(cube_terms(inputs_pairs, inputs_turns), w_inputs)
     else:
         first_grad, first_back = ring_scatter(first_parts)
@@ -1038,12 +1062,14 @@
         output_sum = sum_columns(weight_grad([jnp.concatenate(heads_own, 1)], [branch]))
         inputs_grad = sum_rows(weight_grad(first_slots, to_slots(joint_grad, places)))
         inputs_grad, inputs_share = widen([inputs_grad], w_inputs)
-    output_cut = output_sum.reshape(count, -1, output_sum.shape[1])
-    output_grad = total_of(exchange([output_cut[slot] for slot in range(count)]), jnp.float32)
-    up_wgrad, up_share = widen([both_wgrad], w_up)
+        output_sum = output_sum.reshape(count, -1, output_sum.shape[1])
+        output_cut = [output_sum[slot] for slot in range(count)]
+    tokens_grad = norm_backward(first_grad, tokens, gain_one, mixed_total, block_out)
+    up_wgrad, up_share = widen([both_wgrad], w_up, 0, tokens_grad)
     down_grad = widen_turned(both_wgrad, 1)
     gain_grads = gain_sums([inputs_share, gate_share + up_share], [gain_one, gain_two], places)
-    tokens_grad = norm_backward(first_grad, tokens, gain_one, mixed_total)
+    output_grad = exchange(output_cut)
+    output_grad = total_of(output_grad, jnp.float32, tokens_grad)
     return (
         block_out,
         tokens_grad,

time: 683 us -> 671 us (0.982)
  starting transfers between devices: 61 us -> 52.7 us
  waiting for transfers between devices: 253 us -> 246 us
    ppermute x33, starting transfers between devices: 51.7 us -> 42.4 us  [ring_shift(): lax.ppermute(value, 'tensor', [(order[k], order[(k + by) % count]) for k...]
    unnamed x72 -> x80, local copies, waits for them, and re-layouts: 14.8 us -> 16.4 us
    pallas_call x30 -> x31, Pallas kernels: 211 us -> 211 us  [call(): pl.pallas_call(lambda *refs: kernel(*refs[:count], *refs[count + extra:])...]
  transfers between devices with their start and end apart: 50 -> 50, of which waited for: 20 -> 18; matrix products, arithmetic and copies ran while one was open for 3% -> 3% of each run, Pallas kernels for 42% -> 44%
where the time goes in v3:
time: 671 us; the launch traced here: 665 us
  Pallas kernels  304 us (45%)
  waiting for transfers between devices  246 us (37%)
  starting transfers between devices  52.7 us (8%)
  between operations  22.7 us (3%)
  local copies, waits for them, and re-layouts  17.7 us (3%)
  other arithmetic  15.1 us (2%)
  matrix products  7.86 us (1%)
    ppermute x33, waiting for transfers between devices, ring_shift(): lax.ppermute(value, 'tensor', [(order[k], order[(k + by) % count]) for k...  221 us
    pallas_call x31, Pallas kernels, call(): pl.pallas_call(lambda *refs: kernel(*refs[:count], *refs[count + extra:])...  211 us
    pallas_call x3, Pallas kernels, weight_grad(): pl.pallas_call(kernel, grid=(extent // wide,), in_specs=[column_block(row...  51.5 us
    ppermute x33, starting transfers between devices, ring_shift(): lax.ppermute(value, 'tensor', [(order[k], order[(k + by) % count]) for k...  42.4 us
    ppermute x10, waiting for transfers between devices, flip(): return lax.ppermute(value, 'dp', [(k, k ^ bits) for k in range(count)])  21.9 us
    pallas_call x2, Pallas kernels, cube_call(): pl.pallas_call(body, grid_spec=pltpu.PrefetchScalarGridSpec(num_scalar_pr...  21.7 us
    pallas_call x1, Pallas kernels, attention_forward(): pl.pallas_call(lambda *refs: forward_kernel(count, *refs), grid=(groups,)...  19.1 us
    unnamed x80, local copies, waits for them, and re-layouts  16.4 us
  transfers between devices with their start and end apart: 50, of which 18 were waited for; matrix products, arithmetic and copies ran while one was open for 3% of the time, Pallas kernels for 44%

profile of v3, /device:TPU:0, one launch (start us, length us, event | category | flops | bytes accessed | tf_op | source)
XLA Modules:
  0.0 665.3 jit_solution(11462134514707724668)
XLA Ops:
  42.2 26.9 %collective-permute-done.refs_1_ = bf16[288,2048]{1,0:T(8,128)(2,1)S(1)} collective-permute-done((bf16[288,2048]{1,0:T(8,128)(2,1)S(1)}, bf16[288,2048]{1,0:T(8,128)(2,1)S(1)}, u32[]{:S(2)}, u32[]{:S(2)}) %collective-permute-start) | collective-permute-done | bytes 1179680 | tf_op jit(solution)/shard_map/ppermute | solution.py:873
  70.1 26.2 %collective-permute-done.1.refs_2_ = bf16[288,2048]{1,0:T(8,128)(2,1)} collective-permute-done((bf16[288,2048]{1,0:T(8,128)(2,1)S(1)}, bf16[288,2048]{1,0:T(8,128)(2,1)}, u32[]{:S(2)}, u32[]{:S(2)}) %collective-permute-start.1) | collective-permute-done | bytes 1179680 | tf_op jit(solution)/shard_map/ppermute | solution.py:873
  100.6 22.0 %collective-permute-done.2.refs_3_.refs_1_ = bf16[288,2048]{1,0:T(8,128)(2,1)S(1)} collective-permute-done((bf16[288,2048]{1,0:T(8,128)(2,1)}, bf16[288,2048]{1,0:T(8,128)(2,1)S(1)}, u32[]{:S(2)}, u32[]{:S(2)}) %collective-permute-start.2) | collective-permute-done | bytes 1179680 | tf_op jit(solution)/shard_map/ppermute | solution.py:873
  134.8 19.1 %shard_map.170 = (bf16[1152,512]{1,0:T(8,128)(2,1)}, bf16[2,4,1152,128]{3,2,1,0:T(8,128)(2,1)}, bf16[2,1152,128]{2,1,0:T(8,128)(2,1)}, bf16[2,1152,128]{2,1,0:T(8,128)(2,1)}) custom-call(f32[1152,768]{1,0:T(8,128)} %shard_map.169.refs_0_, f32[1152,128]{1,0:T(8,128)} %get-tuple-element.158.refs_1_.refs_9_, f32[1152,128]{1,0:T(8,128)} %get-tuple-element.157.refs_2_.refs_10_, ...), custom_call_target="tpu_custom_call" | custom-call | flops 8153726976 | bytes 1048576 | tf_op jit(solution)/shard_map/pallas_call | solution.py:142
  164.3 15.4 %collective-permute-done.4.refs_1_ = bf16[288,512]{1,0:T(8,128)(2,1)S(1)} collective-permute-done((bf16[288,512]{1,0:T(8,128)(2,1)}, bf16[288,512]{1,0:T(8,128)(2,1)S(1)}, u32[]{:S(2)}, u32[]{:S(2)}) %collective-permute-start.4) | collective-permute-done | bytes 294944 | tf_op jit(solution)/shard_map/ppermute | solution.py:873
  189.1 19.4 %collective-permute-done.10.refs_1_.refs_2_ = bf16[288,2048]{1,0:T(8,128)(2,1)S(1)} collective-permute-done((bf16[288,2048]{1,0:T(8,128)(2,1)}, bf16[288,2048]{1,0:T(8,128)(2,1)S(1)}, u32[]{:S(2)}, u32[]{:S(2)}) %collective-permute-start.10) | collective-permute-done | bytes 1179680 | tf_op jit(solution)/shard_map/ppermute | solution.py:873
  211.7 26.3 %collective-permute-done.11.refs_1_ = bf16[288,2048]{1,0:T(8,128)(2,1)S(1)} collective-permute-done((bf16[288,2048]{1,0:T(8,128)(2,1)}, bf16[288,2048]{1,0:T(8,128)(2,1)S(1)}, u32[]{:S(2)}, u32[]{:S(2)}) %collective-permute-start.11) | collective-permute-done | bytes 1179680 | tf_op jit(solution)/shard_map/ppermute | solution.py:873
  238.0 26.1 %collective-permute-done.12.refs_0_.refs_2_ = bf16[288,2048]{1,0:T(8,128)(2,1)S(1)} collective-permute-done((bf16[288,2048]{1,0:T(8,128)(2,1)S(1)}, bf16[288,2048]{1,0:T(8,128)(2,1)S(1)}, u32[]{:S(2)}, u32[]{:S(2)}) %collective-permute-start.12) | collective-permute-done | bytes 1179680 | tf_op jit(solution)/shard_map/ppermute | solution.py:873
  265.2 16.1 %shard_map.174 = (bf16[288,2048]{1,0:T(8,128)(2,1)}, bf16[288,2048]{1,0:T(8,128)(2,1)}, bf16[288,2048]{1,0:T(8,128)(2,1)}, bf16[288,2048]{1,0:T(8,128)(2,1)}, bf...) custom-call(bf16[288,2048]{1,0:T(8,128)(2,1)} %shard_map.173.refs_0_, bf16[288,2048]{1,0:T(8,128)(2,1)} %copy-done.31, ...), custom_call_target="tpu_custom_call" | custom-call | flops 9663676416 | bytes 1048576 | tf_op jit(solution)/shard_map/pallas_call | solution.py:259
  281.3 12.8 %collective-permute-done.13.refs_1_.refs_3_ = bf16[288,2048]{1,0:T(8,128)(2,1)} collective-permute-done((bf16[288,2048]{1,0:T(8,128)(2,1)S(1)}, bf16[288,2048]{1,0:T(8,128)(2,1)}, u32[]{:S(2)}, u32[]{:S(2)}) %collective-permute-start.13) | collective-permute-done | bytes 1179680 | tf_op jit(solution)/shard_map/ppermute | solution.py:873
  294.1 16.0 %shard_map.175 = (bf16[288,2048]{1,0:T(8,128)(2,1)}, bf16[288,2048]{1,0:T(8,128)(2,1)}, bf16[288,2048]{1,0:T(8,128)(2,1)}, bf16[288,2048]{1,0:T(8,128)(2,1)}, bf...) custom-call(bf16[288,2048]{1,0:T(8,128)(2,1)} %copy-done.32, ...), custom_call_target="tpu_custom_call" | custom-call | flops 9663676416 | bytes 1048576 | tf_op jit(solution)/shard_map/pallas_call | solution.py:259
  310.1 14.8 %shard_map.176 = (bf16[288,2048]{1,0:T(8,128)(2,1)}, bf16[288,2048]{1,0:T(8,128)(2,1)}, bf16[288,2048]{1,0:T(8,128)(2,1)}, bf16[288,2048]{1,0:T(8,128)(2,1)}) custom-call(bf16[288,2048]{1,0:T(8,128)(2,1)} %get-tuple-element.86.refs_0_.refs_4_, bf16[288,2048]{1,0:T(8,128)(2,1)} %get-tuple-element.87.refs_1_.refs_5_, ...), custom_call_target="tpu_custom_call" | custom-call | flops 9663676416 | bytes 1048576 | tf_op jit(solution)/shard_map/pallas_call | solution.py:259
  326.0 18.8 %shard_map.177 = (bf16[288,2048]{1,0:T(8,128)(2,1)}, bf16[288,2048]{1,0:T(8,128)(2,1)}, bf16[288,2048]{1,0:T(8,128)(2,1)}, bf16[288,2048]{1,0:T(8,128)(2,1)}, bf...) custom-call(bf16[288,2048]{1,0:T(8,128)(2,1)} %shard_map.171.refs_0_, ...), custom_call_target="tpu_custom_call" | custom-call | flops 9663676416 | bytes 1048576 | tf_op jit(solution)/shard_map/pallas_call | solution.py:259
  345.8 12.3 %shard_map.178.refs_8_ = bf16[288,2048]{1,0:T(8,128)(2,1)} custom-call(bf16[288,2048]{1,0:T(8,128)(2,1)} %get-tuple-element.101.refs_0_.refs_5_, bf16[288,2048]{1,0:T(8,128)(2,1)} %get-tuple-element.102.refs_1_.refs_5_, bf16[2048,2048]{1,0:T(8,128)(2,1)} %all-gather.10.cloned.1.call-done.refs_2_.refs_6_, ...), custom_call_target="tpu_custom_call" | custom-call | flops 4831838208 | bytes 1048576 | tf_op jit(solution)/shard_map/pallas_call | solution.py:259
  359.1 20.8 %shard_map.179 = (bf16[288,2048]{1,0:T(8,128)(2,1)}, bf16[288,2048]{1,0:T(8,128)(2,1)}, bf16[288,2048]{1,0:T(8,128)(2,1)}) custom-call(bf16[288,2048]{1,0:T(8,128)(2,1)} %get-tuple-element.103.refs_0_.refs_4_, bf16[288,2048]{1,0:T(8,128)(2,1)} %get-tuple-element.104.refs_1_.refs_6_, bf16[288,2048]{1,0:T(8,128)(2,1)} %get-tuple-element.105.refs_2_.refs_7_, ...), custom_call_target="tpu_custom_call" | custom-call | flops 14495514624 | bytes 1048576 | tf_op jit(solution)/shard_map/pallas_call | solution.py:259
  382.8 16.7 %shard_map.180.refs_2_ = bf16[2048,2048]{1,0:T(8,128)(2,1)} custom-call(bf16[288,2048]{1,0:T(8,128)(2,1)} %shard_map.173.refs_0_, bf16[288,2048]{1,0:T(8,128)(2,1)} %copy-done.31, bf16[288,2048]{1,0:T(8,128)(2,1)} %copy-done.32, bf16[288,2048]{1,0:T(8,128)(2,1)} %collective-permute-done.13.refs_1_.refs_3_, ...), custom_call_target="tpu_custom_call" | custom-call | flops 9663676416 | bytes 1048576 | tf_op jit(solution)/shard_map/pallas_call | solution.py:514
  408.7 17.9 %shard_map.183.refs_6_.refs_8_ = bf16[2048,4096]{1,0:T(8,128)(2,1)} custom-call(bf16[288,2048]{1,0:T(8,128)(2,1)} %shard_map.173.refs_0_, bf16[288,2048]{1,0:T(8,128)(2,1)} %copy-done.31, bf16[288,2048]{1,0:T(8,128)(2,1)} %copy-done.32, bf16[288,2048]{1,0:T(8,128)(2,1)} %collective-permute-done.13.refs_1_.refs_3_, ...), custom_call_target="tpu_custom_call" | custom-call | flops 9663676416 | bytes 1048576 | tf_op jit(solution)/shard_map/pallas_call | solution.py:514
  434.4 12.0 %shard_map.184 = (f32[288,2048]{1,0:T(8,128)}, bf16[288,2048]{1,0:T(8,128)(2,1)}, bf16[288,512]{1,0:T(8,128)(2,1)}, bf16[288,512]{1,0:T(8,128)(2,1)}, bf16[288,5...) custom-call(bf16[288,2048]{1,0:T(8,128)(2,1)} %get-tuple-element.112.refs_0_, bf16[288,2048]{1,0:T(8,128)(2,1)} %copy-done.11, ...), custom_call_target="tpu_custom_call" | custom-call | flops 31249999872 | bytes 1048576 | tf_op jit(solution)/shard_map/pallas_call | solution.py:259
  451.4 16.9 %shard_map.186.refs_5_.refs_12_ = bf16[2048,4096]{1,0:T(8,128)(2,1)} custom-call(bf16[288,2048]{1,0:T(8,128)(2,1)} %shard_map.171.refs_0_, bf16[288,2048]{1,0:T(8,128)(2,1)} %copy-done.2, bf16[288,2048]{1,0:T(8,128)(2,1)} %copy-done.1, bf16[288,2048]{1,0:T(8,128)(2,1)} %copy-done.5, ...), custom_call_target="tpu_custom_call", output_to_operand_aliasing={{}: (8, {})} | custom-call | flops 9663676416 | bytes 1048576 | tf_op jit(solution)/shard_map/pallas_call | solution.py:514
  468.3 10.8 %shard_map.187 = (bf16[4,2048,256]{2,1,0:T(8,128)(2,1)}, bf16[4,2048,256]{2,1,0:T(8,128)(2,1)}) custom-call(s32[1]{0:T(128)} %bitcast.5.me, bf16[288,512]{1,0:T(8,128)(2,1)} %get-tuple-element.82.refs_0_, bf16[288,512]{1,0:T(8,128)(2,1)} %copy-done.16, bf16[288,512]{1,0:T(8,128)(2,1)} %copy-done.17, bf16[288,512]{1,0:T(8,128)(2,1)} %copy-done.18, ...), custom_call_target="tpu_custom_call" | custom-call | flops 2415919104 | bytes 1048576 | tf_op jit(solution)/shard_map/pallas_call | solution.py:575
  484.4 22.2 %shard_map.188.refs_0_.refs_4_ = bf16[1152,768]{1,0:T(8,128)(2,1)} custom-call(bf16[2,4,1152,128]{3,2,1,0:T(8,128)(2,1)} %get-tuple-element.114.refs_0_, bf16[2,1152,128]{2,1,0:T(8,128)(2,1)} %get-tuple-element.115.refs_1_, bf16[2,1152,128]{2,1,0:T(8,128)(2,1)} %get-tuple-element.116.refs_2_, bf16[1152,512]{1,0:T(8,128)(2,1)} %get-tuple-element.81.refs_0_.refs_3_, ...), custom_call_target="tpu_custom_call" | custom-call | flops 999999995904 | bytes 1048576 | tf_op jit(solution)/shard_map/pallas_call | solution.py:259
  526.6 10.9 %shard_map.193 = (bf16[4,256,768]{2,1,0:T(8,128)(2,1)}, bf16[4,256,768]{2,1,0:T(8,128)(2,1)}) custom-call(s32[1]{0:T(128)} %bitcast.5.me, bf16[288,2048]{1,0:T(8,128)(2,1)} %copy-done.9, bf16[288,2048]{1,0:T(8,128)(2,1)} %copy-done.30, bf16[288,2048]{1,0:T(8,128)(2,1)} %collective-permute-done.1.refs_2_, bf16[288,2048]{1,0:T(8,128)(2,1)} %copy-done.7, ...), custom_call_target="tpu_custom_call" | custom-call | flops 999999995904 | bytes 1048576 | tf_op jit(solution)/shard_map/pallas_call | solution.py:575
  567.4 17.4 %collective-permute-done.28.refs_0_ = bf16[288,2048]{1,0:T(8,128)(2,1)S(1)} collective-permute-done((bf16[288,2048]{1,0:T(8,128)(2,1)}, bf16[288,2048]{1,0:T(8,128)(2,1)S(1)}, u32[]{:S(2)}, u32[]{:S(2)}) %collective-permute-start.28) | collective-permute-done | bytes 1179680 | tf_op jit(solution)/shard_map/ppermute | solution.py:873
  590.4 14.5 %collective-permute-done.31.refs_2_ = bf16[128,768]{1,0:T(8,128)(2,1)S(1)} collective-permute-done((bf16[128,768]{1,0:T(8,128)(2,1)S(1)}, bf16[128,768]{1,0:T(8,128)(2,1)S(1)}, u32[]{:S(2)}, u32[]{:S(2)}) %collective-permute-start.31) | collective-permute-done | bytes 196640 | tf_op jit(solution)/shard_map/ppermute | solution.py:928
  (231 shorter events, 210.3 us)
Async XLA Ops:
  7.2 119.4 %all-gather.6.cloned.1.call-start = ((), (), s32[]{:S(2)}) async-start(), calls=%async_computation.2 | async-start | bytes 3538944 | tf_op jit(solution)/shard_map/all_gather | solution.py:950
  7.9 171.8 %all-gather.8.cloned.1.call-start = ((), (), s32[]{:S(2)}) async-start(), calls=%async_computation.3 | async-start | bytes 9437184 | tf_op jit(solution)/shard_map/all_gather | solution.py:954
  31.8 233.4 %all-gather.10.cloned.1.call-start = ((), (), s32[]{:S(2)}) async-start(), calls=%async_computation.4 | async-start | bytes 9437184 | tf_op jit(solution)/shard_map/all_gather | solution.py:950
  32.6 232.6 %all-gather.12.cloned.1.call-start = ((), (), s32[]{:S(2)}) async-start(), calls=%async_computation.5 | async-start | bytes 9437184 | tf_op jit(solution)/shard_map/all_gather | solution.py:950
  33.2 277.0 %all-gather.14.cloned.1.call-start = ((), (), s32[]{:S(2)}) async-start(), calls=%async_computation.6 | async-start | bytes 9437184 | tf_op jit(solution)/shard_map/all_gather | solution.py:954
  33.8 531.0 %reduce-scatter.3.cloned.1.call-start = ((), (), s32[]{:S(2)}) async-start(), calls=%async_computation.7 | async-start | bytes 9437184 | tf_op jit(solution)/shard_map/reduce_scatter | solution.py:958
  35.6 33.5 %collective-permute-start = (bf16[288,2048]{1,0:T(8,128)(2,1)S(1)}, bf16[288,2048]{1,0:T(8,128)(2,1)S(1)}, u32[]{:S(2)}, u32[]{:S(2)}) collective-permute-start(bf16[288,2048]{1,0:T(8,128)(2,1)S(1)} %fusion.7.refs_0_), channel_id=1, source_target_pairs={{0,1},{1,3},{3,2},{2,0},{4,5},{5,7},{7,6},{6,4},{8,9},{9,11},{11,1... | collective-permute-start | bytes 3538952 | tf_op jit(solution)/shard_map/ppermute | solution.py:873
  125.7 28.2 %collective-permute-start.3 = (bf16[288,2048]{1,0:T(8,128)(2,1)}, bf16[288,2048]{1,0:T(8,128)(2,1)S(1)}, u32[]{:S(2)}, u32[]{:S(2)}) collective-permute-start(bf16[288,2048]{1,0:T(8,128)(2,1)} %shard_map.171.refs_0_), channel_id=1, source_target_pairs={{0,1},{1,3},{3,2},{2,0},{4,5},{5,7},{7,6},{6,4},{8,9},{9,11},{11,1... | collective-permute-start | bytes 3538952 | tf_op jit(solution)/shard_map/ppermute | solution.py:873
  161.8 46.7 %collective-permute-start.10 = (bf16[288,2048]{1,0:T(8,128)(2,1)}, bf16[288,2048]{1,0:T(8,128)(2,1)S(1)}, u32[]{:S(2)}, u32[]{:S(2)}) collective-permute-start(bf16[288,2048]{1,0:T(8,128)(2,1)} %copy-done.2), channel_id=1, source_target_pairs={{0,1},{1,3},{3,2},{2,0},{4,5},{5,7},{7,6},{6,4},{8,9},{9,11},{11,1... | collective-permute-start | bytes 3538952 | tf_op jit(solution)/shard_map/ppermute | solution.py:873
  264.2 29.9 %collective-permute-start.13 = (bf16[288,2048]{1,0:T(8,128)(2,1)S(1)}, bf16[288,2048]{1,0:T(8,128)(2,1)}, u32[]{:S(2)}, u32[]{:S(2)}) collective-permute-start(bf16[288,2048]{1,0:T(8,128)(2,1)S(1)} %collective-permute-done.12.refs_0_.refs_2_), channel_id=1, source_target_pairs={{0,1},{1,3},{3,2},{2,0},{4,5},{5,7},{7,6},{6,4},{8,9},{9,11},{11,1... | collective-permute-start | bytes 3538952 | tf_op jit(solution)/shard_map/ppermute | solution.py:873
  264.2 60.7 %collective-permute-start.15 = (bf16[288,2048]{1,0:T(8,128)(2,1)}, bf16[288,2048]{1,0:T(8,128)(2,1)S(1)}, u32[]{:S(2)}, u32[]{:S(2)}) collective-permute-start(bf16[288,2048]{1,0:T(8,128)(2,1)} %copy-done.1), channel_id=1, source_target_pairs={{0,1},{1,3},{3,2},{2,0},{4,5},{5,7},{7,6},{6,4},{8,9},{9,11},{11,1... | collective-permute-start | bytes 3538952 | tf_op jit(solution)/shard_map/ppermute | solution.py:873
  399.5 240.7 %reduce-scatter.5.cloned.1.call-start = ((), (), s32[]{:S(2)}) async-start(), calls=%async_computation.8 | async-start | bytes 18874368 | tf_op jit(solution)/shard_map/reduce_scatter | solution.py:958
  433.7 45.5 %collective-permute-start.19 = (bf16[288,2048]{1,0:T(8,128)(2,1)}, bf16[288,2048]{1,0:T(8,128)(2,1)S(1)}, u32[]{:S(2)}, u32[]{:S(2)}) collective-permute-start(bf16[288,2048]{1,0:T(8,128)(2,1)} %shard_map.182), channel_id=1, source_target_pairs={{0,1},{1,3},{3,2},{2,0},{4,5},{5,7},{7,6},{6,4},{8,9},{9,11},{11,1... | collective-permute-start | bytes 3538952 | tf_op jit(solution)/shard_map/ppermute | solution.py:873
  446.4 32.7 %collective-permute-start.20 = (bf16[288,512]{1,0:T(8,128)(2,1)}, bf16[288,512]{1,0:T(8,128)(2,1)S(1)}, u32[]{:S(2)}, u32[]{:S(2)}) collective-permute-start(bf16[288,512]{1,0:T(8,128)(2,1)} %get-tuple-element.113), channel_id=1, source_target_pairs={{0,2},{1,0},{3,1},{2,3},{4,6},{5,4},{7,5},{6,7},{8,10},{9,8},{11,9... | collective-permute-start | bytes 884744 | tf_op jit(solution)/shard_map/ppermute | solution.py:873
  448.5 35.1 %collective-permute-start.22 = (bf16[288,512]{1,0:T(8,128)(2,1)}, bf16[288,512]{1,0:T(8,128)(2,1)S(1)}, u32[]{:S(2)}, u32[]{:S(2)}) collective-permute-start(bf16[288,512]{1,0:T(8,128)(2,1)} %get-tuple-element.118), channel_id=1, source_target_pairs={{0,1},{1,3},{3,2},{2,0},{4,5},{5,7},{7,6},{6,4},{8,9},{9,11},{11,1... | collective-permute-start | bytes 884744 | tf_op jit(solution)/shard_map/ppermute | solution.py:873
  448.6 35.0 %collective-permute-start.23 = (bf16[288,512]{1,0:T(8,128)(2,1)}, bf16[288,512]{1,0:T(8,128)(2,1)S(1)}, u32[]{:S(2)}, u32[]{:S(2)}) collective-permute-start(bf16[288,512]{1,0:T(8,128)(2,1)} %get-tuple-element.119), channel_id=1, source_target_pairs={{0,3},{1,2},{3,0},{2,1},{4,7},{5,6},{7,4},{6,5},{8,11},{9,10},{11,... | collective-permute-start | bytes 884744 | tf_op jit(solution)/shard_map/ppermute | solution.py:873
  479.1 37.9 %collective-permute-start.25 = (bf16[4,2048,256]{2,1,0:T(8,128)(2,1)}, bf16[4,2048,256]{2,1,0:T(8,128)(2,1)}, u32[]{:S(2)}, u32[]{:S(2)}) collective-permute-start(bf16[4,2048,256]{2,1,0:T(8,128)(2,1)} %get-tuple-element.121.refs_13_), channel_id=1, source_target_pairs={{0,4},{4,0},{8,12},{12,8},{16,20},{20,16},{24,28},{28,24},{1,5},{5... | collective-permute-start | bytes 12582920 | tf_op jit(solution)/shard_map/ppermute | solution.py:928
  482.8 29.8 %collective-permute-start.21 = (bf16[288,2048]{1,0:T(8,128)(2,1)}, bf16[288,2048]{1,0:T(8,128)(2,1)}, u32[]{:S(2)}, u32[]{:S(2)}) collective-permute-start(bf16[288,2048]{1,0:T(8,128)(2,1)} %shard_map.185), channel_id=1, source_target_pairs={{0,1},{1,3},{3,2},{2,0},{4,5},{5,7},{7,6},{6,4},{8,9},{9,11},{11,1... | collective-permute-start | bytes 3538952 | tf_op jit(solution)/shard_map/ppermute | solution.py:873
  516.8 37.8 %collective-permute-start.24 = (bf16[288,2048]{1,0:T(8,128)(2,1)}, bf16[288,2048]{1,0:T(8,128)(2,1)}, u32[]{:S(2)}, u32[]{:S(2)}) collective-permute-start(bf16[288,2048]{1,0:T(8,128)(2,1)} %shard_map.189.refs_3_.refs_2_), channel_id=1, source_target_pairs={{0,1},{1,3},{3,2},{2,0},{4,5},{5,7},{7,6},{6,4},{8,9},{9,11},{11,1... | collective-permute-start | bytes 3538952 | tf_op jit(solution)/shard_map/ppermute | solution.py:873
  558.4 58.1 %collective-permute-start.38 = (bf16[2048,256]{1,0:T(8,128)(2,1)S(1)}, bf16[2048,256]{1,0:T(8,128)(2,1)S(1)}, u32[]{:S(2)}, u32[]{:S(2)}) collective-permute-start(bf16[2048,256]{1,0:T(8,128)(2,1)S(1)} %copy-done.13), channel_id=1, source_target_pairs={{0,8},{4,12},{8,0},{12,4},{16,24},{20,28},{24,16},{28,20},{1,9},{5... | collective-permute-start | bytes 3145736 | tf_op jit(solution)/shard_map/ppermute | solution.py:928
  558.6 57.9 %collective-permute-start.39 = (bf16[2048,256]{1,0:T(8,128)(2,1)}, bf16[2048,256]{1,0:T(8,128)(2,1)}, u32[]{:S(2)}, u32[]{:S(2)}) collective-permute-start(bf16[2048,256]{1,0:T(8,128)(2,1)} %get-tuple-element.147), channel_id=1, source_target_pairs={{0,16},{4,20},{8,24},{12,28},{16,0},{20,4},{24,8},{28,12},{1,17},{... | collective-permute-start | bytes 3145736 | tf_op jit(solution)/shard_map/ppermute | solution.py:928
  588.4 45.7 %collective-permute-start.30 = (bf16[288,2048]{1,0:T(8,128)(2,1)}, bf16[288,2048]{1,0:T(8,128)(2,1)S(1)}, u32[]{:S(2)}, u32[]{:S(2)}) collective-permute-start(bf16[288,2048]{1,0:T(8,128)(2,1)} %shard_map.197.refs_3_.refs_4_), channel_id=1, source_target_pairs={{0,1},{1,3},{3,2},{2,0},{4,5},{5,7},{7,6},{6,4},{8,9},{9,11},{11,1... | collective-permute-start | bytes 3538952 | tf_op jit(solution)/shard_map/ppermute | solution.py:873
  620.4 27.4 %collective-permute-start.40 = (bf16[512,256]{1,0:T(8,128)(2,1)}, bf16[512,256]{1,0:T(8,128)(2,1)S(1)}, u32[]{:S(2)}, u32[]{:S(2)}) collective-permute-start(bf16[512,256]{1,0:T(8,128)(2,1)} %get-tuple-element.149), channel_id=1, source_target_pairs={{0,1},{1,3},{3,2},{2,0},{4,5},{5,7},{7,6},{6,4},{8,9},{9,11},{11,1... | collective-permute-start | bytes 786440 | tf_op jit(solution)/shard_map/ppermute | solution.py:873
  621.8 29.2 %collective-permute-start.41 = (bf16[512,256]{1,0:T(8,128)(2,1)}, bf16[512,256]{1,0:T(8,128)(2,1)S(1)}, u32[]{:S(2)}, u32[]{:S(2)}) collective-permute-start(bf16[512,256]{1,0:T(8,128)(2,1)} %get-tuple-element.150), channel_id=1, source_target_pairs={{0,3},{1,2},{3,0},{2,1},{4,7},{5,6},{7,4},{6,5},{8,11},{9,10},{11,... | collective-permute-start | bytes 786440 | tf_op jit(solution)/shard_map/ppermute | solution.py:873
  (66 other events, 717.8 us)
Sparse Core Ops, SparseCore 0:
  9.9 35.0 all-gather.5
  46.8 55.9 all-gather.7
  104.7 54.3 all-gather.9
  160.9 54.3 all-gather.11
  217.1 55.9 all-gather.13
  399.7 72.9 reduce-scatter.2
  479.2 153.6 reduce-scatter.4

commit v4 on v3

--- a/solution.py
+++ b/solution.py
@@ -387,9 +387,12 @@
         for slot in range(count):
             one = dot(refs[slot][...], w_gate[...])
             two = dot(refs[slot][...], w_up[...])
-            out[slot][...] = (one * jax.nn.sigmoid(one) * two).astype(jnp.bfloat16)
-            out[count + slot][...] = one.astype(jnp.bfloat16)
-            out[2 * count + slot][...] = two.astype(jnp.bfloat16)
+            sigma = jax.nn.sigmoid(one)
+            silu = one * sigma
+            slope = two * (sigma + silu * (1.0 - sigma))
+            out[slot][...] = (silu * two).astype(jnp.bfloat16)
+            out[count + slot][...] = slope.astype(jnp.bfloat16)
+            out[2 * count + slot][...] = silu.astype(jnp.bfloat16)
 
     out = call(
         kernel,
@@ -404,7 +407,7 @@
     return out[:count], out[count : 2 * count], out[2 * count :]
 
 
-def feed_backward(grads, w_down, gates, ups, *earlier):
+def feed_backward(grads, w_down, slopes, silus, *earlier):
     count = len(grads)
     rows, width = grads[0].shape
     extent = w_down.shape[0]
@@ -415,17 +418,15 @@
         out = refs[3 * count + 1 :]
         for slot in range(count):
             hidden_grad = dot(refs[slot][...], w_down[...], NT)
-            one = refs[count + slot][...].astype(jnp.float32)
-            sigma = jax.nn.sigmoid(one)
-            scaled = hidden_grad * sigma
-            slope = refs[2 * count + slot][...].astype(jnp.float32) * (1.0 + one * (1.0 - sigma))
-            out[slot][...] = (scaled * slope).astype(jnp.bfloat16)
-            out[count + slot][...] = (scaled * one).astype(jnp.bfloat16)
+            slope = refs[count + slot][...].astype(jnp.float32)
+            silu = refs[2 * count + slot][...].astype(jnp.float32)
+            out[slot][...] = (hidden_grad * slope).astype(jnp.bfloat16)
+            out[count + slot][...] = (hidden_grad * silu).astype(jnp.bfloat16)
 
     out = call(
         kernel,
         extent // wide,
-        (*grads, *gates, *ups, w_down),
+        (*grads, *slopes, *silus, w_down),
         [whole(rows, width)] * count
         + [column_block(rows, wide)] * (2 * count)
         + [row_block(wide, width)],
@@ -675,6 +676,28 @@
     )
 
 
+def cube_sums(parts, *earlier):
+    away, home = parts
+    arrived = flip(away, 1)
+    _, rows, width = home.shape
+
+    def kernel(home, arrived, *out):
+        for at in range(4):
+            total = home[at].astype(jnp.float32) + arrived[at].astype(jnp.float32)
+            out[at][...] = total.astype(jnp.bfloat16)
+
+    return call(
+        kernel,
+        1,
+        (home, arrived),
+        [whole(4, rows, width)] * 2,
+        [whole(rows, width)] * 4,
+        [low_shape(rows, width)] * 4,
+        0,
+        earlier,
+    )
+
+
 def total_slots(terms, count, *earlier):
     rows, width = terms[0].shape
     local = rows // count
@@ -968,8 +991,20 @@
     start = lax.axis_index("dp") * rows
     own = [share[:, 0] / lax.dynamic_slice_in_dim(gain, start, rows, 0) for share, gain in zip(shares, gains)]
     cut = jnp.stack(own).reshape(len(own), count, -1)
-    pieces = [lax.dynamic_index_in_dim(cut, places[slot], 1, False) for slot in range(count)]
-    return sum(exchange(pieces))
+    if count & (count - 1):
+        pieces = [lax.dynamic_index_in_dim(cut, places[slot], 1, False) for slot in range(count)]
+        return sum(exchange(pieces))
+    me = lax.axis_index("tensor")
+    total = cut.transpose(1, 0, 2).reshape(count, -1)
+    bits = count // 2
+    while bits:
+        pair = total.reshape(2, bits, -1)
+        mine = (me // bits) % 2
+        keep = lax.dynamic_index_in_dim(pair, mine, 0, False)
+        give = lax.dynamic_index_in_dim(pair, 1 - mine, 0, False)
+        total = keep + lax.ppermute(give, "tensor", [(k, k ^ bits) for k in range(count)])
+        bits //= 2
+    return total.reshape(len(own), -1)
 
 
 def normalize(value, gain):
@@ -1011,9 +1046,11 @@
     half = max(count // 2, 1)
     ahead = feed_forward(second_slots[:half], gate_full, up_full)
     rest = feed_forward(second_slots[half:], gate_full, up_full)
-    hidden, gate, up = [list(one) + list(two) for one, two in zip(ahead, rest)]
+    hidden, slope, silu = [list(one) + list(two) for one, two in zip(ahead, rest)]
     block_parts = product(hidden, down_full)
-    gate_grad, up_grad = feed_backward(grad_slots, down_full, gate, up, block_parts[0])
+    down_wpart = weight_grad(hidden, grad_slots, block_parts[0])
+    down_wgrad = sum_columns(down_wpart)
+    gate_grad, up_grad = feed_backward(grad_slots, down_full, slope, silu, down_wpart)
     block_moving = ring_shift(block_parts[1], 1)
     pick = lambda slots: ((([gate_grad[s] for s in slots]), gate_full), ([up_grad[s] for s in slots], up_full))
     part_one = sum_of_products(pick([1]), block_moving)
@@ -1021,41 +1058,41 @@
     part_others = sum_of_products(pick(others), part_one[0])
     second_parts = [part_others[0], part_one[0]] + list(part_others[1:])
     second_early = ring_shift(second_parts[1], 1)
-    gate_wpart = weight_grad(second_slots, gate_grad, second_early)
+    gate_wpart = weight_grad(second_slots, gate_grad, second_early, part_others[0])
     gate_wgrad = sum_rows(gate_wpart)
-    second_grad, second_back = ring_scatter(second_parts, {3: [gate_wpart]}, 3)
-    up_wpart = weight_grad(second_slots, up_grad, second_back[1], half=0)
+    second_grad, second_back = ring_scatter(second_parts, {3: [gate_wpart, down_wgrad]}, 3)
+    up_wpart = weight_grad(second_slots, up_grad, second_back[1])
+    up_wgrad = sum_rows(up_wpart)
 
     mixed_total, branch, heads_back = norm_split(
         second_grad, mixed, gain_two, cotangent, output_full, count, up_wpart
     )
     heads_grad = exchange(heads_back)
-    both_wpart = weight_grad(grad_slots, hidden, branch, half=1, into=up_wpart)
-    both_wgrad = sum_rows(both_wpart)
-    block_sum, block_back = ring_scatter(block_parts, {2: [second_back[-1]], 3: [heads_grad[-1]]})
+    block_sum, block_back = ring_scatter(block_parts, {2: [gate_grad[0]], 3: [heads_grad[-1]]})
     cube = lax.axis_size("dp") == 8
-    output_parts = cube_columns(heads_own, branch, both_wpart) if cube else ()
+    output_parts = cube_columns(heads_own, branch) if cube else ()
     joint_grad = attention_backward(
-        query, key, value, heads, heads_grad, places, held, groups, block_back[1], both_wpart, *output_parts[:1]
+        query, key, value, heads, heads_grad, places, held, groups, block_back[1], gate_wgrad, *output_parts[:1]
     )
     first_one = spread_product(joint_grad, inputs_full, places, [1], block_back[2])
     first_others = spread_product(joint_grad, inputs_full, places, others, first_one[0])
     first_parts = [first_others[0], first_one[0]] + list(first_others[1:])
     gate_wgrad, gate_share = widen([gate_wgrad], w_gate)
+    down_grad = total_of([down_wgrad], jnp.float32)
     if cube:
         output_pairs = cube_pairs(output_parts, first_one[0])
-        output_turns = cube_turns(output_pairs)
         inputs_parts = cube_rows(first_slots, joint_grad, places, HEAVY, output_pairs[0])
-        second_pause = [output_turns[0], inputs_parts[0]]
+        second_pause = [inputs_parts[0]]
         first_next = tied_sum(ring_shift(first_parts[1], 1), first_parts[2], 0, *second_pause)
-        inputs_pairs = cube_pairs(inputs_parts, first_next)
-        third_pause = [inputs_pairs[0], gate_wgrad]
+        output_turns = cube_turns(output_pairs, first_next)
+        inputs_sums = cube_sums(inputs_parts, output_turns[0])
+        third_pause = [inputs_sums[0], gate_wgrad, up_wgrad]
         first_last = tied_sum(ring_shift(first_next, 1), first_parts[3], 0, *third_pause)
-        inputs_turns = cube_turns(inputs_pairs, first_last)
         output_cut = total_slots(cube_terms(output_pairs, output_turns), count, first_last)
         first_grad, first_back = ring_scatter(first_parts, {2: second_pause, 3: third_pause})
         block_out = total_of((*block_sum, mixed), low, first_last, cost=HEAVY)
-        inputs_grad, inputs_share = widen(cube_terms(inputs_pairs, inputs_turns), w_inputs)
+        inputs_terms = [inputs_sums[0]] + [flip(inputs_sums[at], 2 * at) for at in range(1, 4)]
+        inputs_grad, inputs_share = widen(inputs_terms, w_inputs, 0, output_cut[0])
     else:
         first_grad, first_back = ring_scatter(first_parts)
         block_out = total_of((*block_sum, mixed), low)
@@ -1065,8 +1102,7 @@
         output_sum = output_sum.reshape(count, -1, output_sum.shape[1])
         output_cut = [output_sum[slot] for slot in range(count)]
     tokens_grad = norm_backward(first_grad, tokens, gain_one, mixed_total, block_out)
-    up_wgrad, up_share = widen([both_wgrad], w_up, 0, tokens_grad)
-    down_grad = widen_turned(both_wgrad, 1)
+    up_wgrad, up_share = widen([up_wgrad], w_up, 0, output_cut[0])
     gain_grads = gain_sums([inputs_share, gate_share + up_share], [gain_one, gain_two], places)
     output_grad = exchange(output_cut)
     output_grad = total_of(output_grad, jnp.float32, tokens_grad)

time: 671 us -> 660 us (0.984)
  between operations: 22.7 us -> 14.8 us
    ppermute x33 -> x30, waiting for transfers between devices: 221 us -> 218 us  [ring_shift(): lax.ppermute(value, 'tensor', [(order[k], order[(k + by) % count]) for k...]
    ppermute x33 -> x30, starting transfers between devices: 42.4 us -> 40.1 us  [ring_shift(): lax.ppermute(value, 'tensor', [(order[k], order[(k + by) % count]) for k...]
    ppermute x10 -> x9, waiting for transfers between devices: 21.9 us -> 20.4 us  [flip(): return lax.ppermute(value, 'dp', [(k, k ^ bits) for k in range(count)])]
    pallas_call x31 -> x30, Pallas kernels: 211 us -> 211 us  [call(): pl.pallas_call(lambda *refs: kernel(*refs[:count], *refs[count + extra:])...]
    unnamed x80 -> x84, local copies, waits for them, and re-layouts: 16.4 us -> 16.5 us
  transfers between devices with their start and end apart: 50 -> 49, of which waited for: 18 -> 24; matrix products, arithmetic and copies ran while one was open for 3% -> 4% of each run, Pallas kernels for 44% -> 44%
where the time goes in v4:
time: 660 us; the launch traced here: 654 us
  Pallas kernels  304 us (46%)
  waiting for transfers between devices  245 us (37%)
  starting transfers between devices  50.6 us (8%)
  local copies, waits for them, and re-layouts  17.3 us (3%)
  other arithmetic  15.1 us (2%)
  between operations  14.8 us (2%)
  matrix products  7.87 us (1%)
    ppermute x30, waiting for transfers between devices, ring_shift(): lax.ppermute(value, 'tensor', [(order[k], order[(k + by) % count]) for k...  218 us
    pallas_call x30, Pallas kernels, call(): pl.pallas_call(lambda *refs: kernel(*refs[:count], *refs[count + extra:])...  211 us
    pallas_call x3, Pallas kernels, weight_grad(): pl.pallas_call(kernel, grid=(extent // wide,), in_specs=[column_block(row...  51.4 us
    ppermute x30, starting transfers between devices, ring_shift(): lax.ppermute(value, 'tensor', [(order[k], order[(k + by) % count]) for k...  40.1 us
    pallas_call x2, Pallas kernels, cube_call(): pl.pallas_call(body, grid_spec=pltpu.PrefetchScalarGridSpec(num_scalar_pr...  21.7 us
    ppermute x9, waiting for transfers between devices, flip(): return lax.ppermute(value, 'dp', [(k, k ^ bits) for k in range(count)])  20.4 us
    pallas_call x1, Pallas kernels, attention_forward(): pl.pallas_call(lambda *refs: forward_kernel(count, *refs), grid=(groups,)...  19.3 us
    unnamed x84, local copies, waits for them, and re-layouts  16.5 us
  transfers between devices with their start and end apart: 49, of which 24 were waited for; matrix products, arithmetic and copies ran while one was open for 4% of the time, Pallas kernels for 44%

profile of v4, /device:TPU:0, one launch (start us, length us, event | category | flops | bytes accessed | tf_op | source)
XLA Modules:
  0.0 654.4 jit_solution(1195129877905137082)
XLA Ops:
  41.3 26.9 %collective-permute-done.refs_1_ = bf16[288,2048]{1,0:T(8,128)(2,1)S(1)} collective-permute-done((bf16[288,2048]{1,0:T(8,128)(2,1)S(1)}, bf16[288,2048]{1,0:T(8,128)(2,1)S(1)}, u32[]{:S(2)}, u32[]{:S(2)}) %collective-permute-start) | collective-permute-done | bytes 1179680 | tf_op jit(solution)/shard_map/ppermute | solution.py:896
  68.6 26.8 %collective-permute-done.1.refs_2_ = bf16[288,2048]{1,0:T(8,128)(2,1)} collective-permute-done((bf16[288,2048]{1,0:T(8,128)(2,1)S(1)}, bf16[288,2048]{1,0:T(8,128)(2,1)}, u32[]{:S(2)}, u32[]{:S(2)}) %collective-permute-start.1) | collective-permute-done | bytes 1179680 | tf_op jit(solution)/shard_map/ppermute | solution.py:896
  99.7 22.0 %collective-permute-done.2.refs_3_.refs_1_ = bf16[288,2048]{1,0:T(8,128)(2,1)S(1)} collective-permute-done((bf16[288,2048]{1,0:T(8,128)(2,1)}, bf16[288,2048]{1,0:T(8,128)(2,1)S(1)}, u32[]{:S(2)}, u32[]{:S(2)}) %collective-permute-start.2) | collective-permute-done | bytes 1179680 | tf_op jit(solution)/shard_map/ppermute | solution.py:896
  125.7 8.3 %shard_map.169.refs_0_ = f32[1152,768]{1,0:T(8,128)} custom-call(bf16[288,2048]{1,0:T(8,128)(2,1)} %copy-done.9, bf16[288,2048]{1,0:T(8,128)(2,1)} %copy-done.24, bf16[288,2048]{1,0:T(8,128)(2,1)} %collective-permute-done.1.refs_2_, bf16[288,2048]{1,0:T(8,128)(2,1)} %copy-done.4, s32[4]{0:T(128)} %fusion.20.refs_4_.refs_1_.refs_8_.refs_5_, ...), custom_call_target="tpu_custom_call" | custom-call | flops 3623878656 | bytes 1048576 | tf_op jit(solution)/shard_map/pallas_call | solution.py:259
  133.9 19.3 %shard_map.170 = (bf16[1152,512]{1,0:T(8,128)(2,1)}, bf16[2,4,1152,128]{3,2,1,0:T(8,128)(2,1)}, bf16[2,1152,128]{2,1,0:T(8,128)(2,1)}, bf16[2,1152,128]{2,1,0:T(8,128)(2,1)}) custom-call(f32[1152,768]{1,0:T(8,128)} %shard_map.169.refs_0_, f32[1152,128]{1,0:T(8,128)} %get-tuple-element.152.refs_1_.refs_9_, f32[1152,128]{1,0:T(8,128)} %get-tuple-element.151.refs_2_.refs_10_, ...), custom_call_target="tpu_custom_call" | custom-call | flops 8153726976 | bytes 1048576 | tf_op jit(solution)/shard_map/pallas_call | solution.py:142
  163.6 15.1 %collective-permute-done.4.refs_1_ = bf16[288,512]{1,0:T(8,128)(2,1)S(1)} collective-permute-done((bf16[288,512]{1,0:T(8,128)(2,1)}, bf16[288,512]{1,0:T(8,128)(2,1)S(1)}, u32[]{:S(2)}, u32[]{:S(2)}) %collective-permute-start.4) | collective-permute-done | bytes 294944 | tf_op jit(solution)/shard_map/ppermute | solution.py:896
  178.7 7.9 %convert_add_fusion = (f32[288,2048]{1,0:T(8,128)}, f32[288]{0:T(512)S(1)}, f32[288,2048]{1,0:T(8,128)S(1)}) fusion(bf16[288,2048]{1,0:T(8,128)(2,1)S(1)} %copy-done, bf16[2048,2048]{1,0:T(8,128)(2,1)} %all-gather.8.cloned.1.call-done.refs_5_, bf16[288,512]{1,0:T(8,128)(2,1)S(1)} %collective-permute-done.6.refs_3_, ...), kind=kOutput, calls=%fused_computation | convolution fusion | flops 2422996736 | bytes 15467648 | tf_op jit(solution)/shard_map/dot_general | solution.py:52
  188.1 19.3 %collective-permute-done.10.refs_1_.refs_6_.refs_2_ = bf16[288,2048]{1,0:T(8,128)(2,1)S(1)} collective-permute-done((bf16[288,2048]{1,0:T(8,128)(2,1)}, bf16[288,2048]{1,0:T(8,128)(2,1)S(1)}, u32[]{:S(2)}, u32[]{:S(2)}) %collective-permute-start.10) | collective-permute-done | bytes 1179680 | tf_op jit(solution)/shard_map/ppermute | solution.py:896
  210.6 26.3 %collective-permute-done.11.refs_1_ = bf16[288,2048]{1,0:T(8,128)(2,1)S(1)} collective-permute-done((bf16[288,2048]{1,0:T(8,128)(2,1)}, bf16[288,2048]{1,0:T(8,128)(2,1)S(1)}, u32[]{:S(2)}, u32[]{:S(2)}) %collective-permute-start.11) | collective-permute-done | bytes 1179680 | tf_op jit(solution)/shard_map/ppermute | solution.py:896
  237.0 26.1 %collective-permute-done.12.refs_0_.refs_2_ = bf16[288,2048]{1,0:T(8,128)(2,1)S(1)} collective-permute-done((bf16[288,2048]{1,0:T(8,128)(2,1)S(1)}, bf16[288,2048]{1,0:T(8,128)(2,1)S(1)}, u32[]{:S(2)}, u32[]{:S(2)}) %collective-permute-start.12) | collective-permute-done | bytes 1179680 | tf_op jit(solution)/shard_map/ppermute | solution.py:896
  264.4 16.6 %shard_map.174 = (bf16[288,2048]{1,0:T(8,128)(2,1)}, bf16[288,2048]{1,0:T(8,128)(2,1)}, bf16[288,2048]{1,0:T(8,128)(2,1)}, bf16[288,2048]{1,0:T(8,128)(2,1)}, bf...) custom-call(bf16[288,2048]{1,0:T(8,128)(2,1)} %shard_map.173.refs_0_, bf16[288,2048]{1,0:T(8,128)(2,1)} %copy-done.25, ...), custom_call_target="tpu_custom_call" | custom-call | flops 9663676416 | bytes 1048576 | tf_op jit(solution)/shard_map/pallas_call | solution.py:259
  281.0 11.9 %collective-permute-done.13.refs_1_.refs_3_ = bf16[288,2048]{1,0:T(8,128)(2,1)S(1)} collective-permute-done((bf16[288,2048]{1,0:T(8,128)(2,1)S(1)}, bf16[288,2048]{1,0:T(8,128)(2,1)S(1)}, u32[]{:S(2)}, u32[]{:S(2)}) %collective-permute-start.13) | collective-permute-done | bytes 1179680 | tf_op jit(solution)/shard_map/ppermute | solution.py:896
  294.0 16.2 %shard_map.175 = (bf16[288,2048]{1,0:T(8,128)(2,1)}, bf16[288,2048]{1,0:T(8,128)(2,1)}, bf16[288,2048]{1,0:T(8,128)(2,1)}, bf16[288,2048]{1,0:T(8,128)(2,1)}, bf...) custom-call(bf16[288,2048]{1,0:T(8,128)(2,1)} %copy-done.26, bf16[288,2048]{1,0:T(8,128)(2,1)} %copy-done.27, ...), custom_call_target="tpu_custom_call" | custom-call | flops 9663676416 | bytes 1048576 | tf_op jit(solution)/shard_map/pallas_call | solution.py:259
  310.1 14.7 %shard_map.176 = (bf16[288,2048]{1,0:T(8,128)(2,1)}, bf16[288,2048]{1,0:T(8,128)(2,1)}, bf16[288,2048]{1,0:T(8,128)(2,1)}, bf16[288,2048]{1,0:T(8,128)(2,1)}) custom-call(bf16[288,2048]{1,0:T(8,128)(2,1)} %get-tuple-element.83.refs_0_, bf16[288,2048]{1,0:T(8,128)(2,1)} %get-tuple-element.84.refs_1_, bf16[288,2048]{1,0:T(8,128)(2,1)} %get-tuple-element.85.refs_2_, ...), custom_call_target="tpu_custom_call" | custom-call | flops 9663676416 | bytes 1048576 | tf_op jit(solution)/shard_map/pallas_call | solution.py:259
  324.9 16.8 %shard_map.177.refs_13_ = bf16[2048,2048]{1,0:T(8,128)(2,1)} custom-call(bf16[288,2048]{1,0:T(8,128)(2,1)} %get-tuple-element.83.refs_0_, bf16[288,2048]{1,0:T(8,128)(2,1)} %get-tuple-element.84.refs_1_, bf16[288,2048]{1,0:T(8,128)(2,1)} %get-tuple-element.85.refs_2_, bf16[288,2048]{1,0:T(8,128)(2,1)} %get-tuple-element.86.refs_3_, ...), custom_call_target="tpu_custom_call" | custom-call | flops 9663676416 | bytes 1048576 | tf_op jit(solution)/shard_map/pallas_call | solution.py:515
  343.0 20.1 %shard_map.178 = (bf16[288,2048]{1,0:T(8,128)(2,1)}, bf16[288,2048]{1,0:T(8,128)(2,1)}, bf16[288,2048]{1,0:T(8,128)(2,1)}, bf16[288,2048]{1,0:T(8,128)(2,1)}, bf...) custom-call(bf16[288,2048]{1,0:T(8,128)(2,1)} %shard_map.171.refs_4_, ...), custom_call_target="tpu_custom_call" | custom-call | flops 9663676416 | bytes 1048576 | tf_op jit(solution)/shard_map/pallas_call | solution.py:259
  364.1 13.4 %shard_map.180.refs_8_ = bf16[288,2048]{1,0:T(8,128)(2,1)} custom-call(bf16[288,2048]{1,0:T(8,128)(2,1)} %get-tuple-element.105.refs_0_.refs_5_, bf16[288,2048]{1,0:T(8,128)(2,1)} %get-tuple-element.106.refs_1_.refs_5_, bf16[2048,2048]{1,0:T(8,128)(2,1)} %all-gather.10.cloned.1.call-done.refs_2_.refs_6_, ...), custom_call_target="tpu_custom_call" | custom-call | flops 4831838208 | bytes 1048576 | tf_op jit(solution)/shard_map/pallas_call | solution.py:259
  377.7 21.1 %shard_map.181 = (bf16[288,2048]{1,0:T(8,128)(2,1)}, bf16[288,2048]{1,0:T(8,128)(2,1)}, bf16[288,2048]{1,0:T(8,128)(2,1)}) custom-call(bf16[288,2048]{1,0:T(8,128)(2,1)} %get-tuple-element.98.refs_2_.refs_0_.refs_4_, bf16[288,2048]{1,0:T(8,128)(2,1)} %get-tuple-element.100.refs_1_.refs_6_, bf16[288,2048]{1,0:T(8,128)(2,1)} %get-tuple-element.101.refs_2_.refs_7_, ...), custom_call_target="tpu_custom_call" | custom-call | flops 14495514624 | bytes 1048576 | tf_op jit(solution)/shard_map/pallas_call | solution.py:259
  402.4 16.8 %shard_map.182.refs_2_ = bf16[2048,2048]{1,0:T(8,128)(2,1)} custom-call(bf16[288,2048]{1,0:T(8,128)(2,1)} %shard_map.173.refs_0_, bf16[288,2048]{1,0:T(8,128)(2,1)} %copy-done.25, bf16[288,2048]{1,0:T(8,128)(2,1)} %copy-done.26, bf16[288,2048]{1,0:T(8,128)(2,1)} %copy-done.27, bf16[288,2048]{1,0:T(8,128)(2,1)} %get-tuple-element.98.refs_2_.refs_0_.refs_4_, ...), custom_call_target="tpu_custom_call" | custom-call | flops 9663676416 | bytes 1048576 | tf_op jit(solution)/shard_map/pallas_call | solution.py:515
  431.5 17.8 %shard_map.184.refs_6_ = bf16[2048,2048]{1,0:T(8,128)(2,1)} custom-call(bf16[288,2048]{1,0:T(8,128)(2,1)} %shard_map.173.refs_0_, bf16[288,2048]{1,0:T(8,128)(2,1)} %copy-done.25, bf16[288,2048]{1,0:T(8,128)(2,1)} %copy-done.26, bf16[288,2048]{1,0:T(8,128)(2,1)} %copy-done.27, bf16[288,2048]{1,0:T(8,128)(2,1)} %get-tuple-element.102.refs_3_.refs_4_, ...), custom_call_target="tpu_custom_call" | custom-call | flops 9663676416 | bytes 1048576 | tf_op jit(solution)/shard_map/pallas_call | solution.py:515
  456.9 12.0 %shard_map.185 = (f32[288,2048]{1,0:T(8,128)}, bf16[288,2048]{1,0:T(8,128)(2,1)}, bf16[288,512]{1,0:T(8,128)(2,1)}, bf16[288,512]{1,0:T(8,128)(2,1)}, bf16[288,5...) custom-call(bf16[288,2048]{1,0:T(8,128)(2,1)} %get-tuple-element.107.refs_9_.refs_0_, bf16[288,2048]{1,0:T(8,128)(2,1)} %copy-done.30, ...), custom_call_target="tpu_custom_call" | custom-call | flops 31249999872 | bytes 1048576 | tf_op jit(solution)/shard_map/pallas_call | solution.py:259
  472.8 10.8 %shard_map.187 = (bf16[4,2048,256]{2,1,0:T(8,128)(2,1)}, bf16[4,2048,256]{2,1,0:T(8,128)(2,1)}) custom-call(s32[1]{0:T(128)} %bitcast.5.me, bf16[288,512]{1,0:T(8,128)(2,1)} %get-tuple-element.79.refs_0_, bf16[288,512]{1,0:T(8,128)(2,1)} %copy-done.33, bf16[288,512]{1,0:T(8,128)(2,1)} %copy-done.34, bf16[288,512]{1,0:T(8,128)(2,1)} %copy-done.35, ...), custom_call_target="tpu_custom_call" | custom-call | flops 2415919104 | bytes 1048576 | tf_op jit(solution)/shard_map/pallas_call | solution.py:576
  494.6 22.0 %shard_map.188.refs_0_.refs_4_ = bf16[1152,768]{1,0:T(8,128)(2,1)} custom-call(bf16[2,4,1152,128]{3,2,1,0:T(8,128)(2,1)} %get-tuple-element.111.refs_0_, bf16[2,1152,128]{2,1,0:T(8,128)(2,1)} %get-tuple-element.112.refs_1_, bf16[2,1152,128]{2,1,0:T(8,128)(2,1)} %get-tuple-element.113.refs_2_, bf16[1152,512]{1,0:T(8,128)(2,1)} %get-tuple-element.78.refs_0_.refs_3_, ...), custom_call_target="tpu_custom_call" | custom-call | flops 999999995904 | bytes 1048576 | tf_op jit(solution)/shard_map/pallas_call | solution.py:259
  533.9 10.8 %shard_map.192 = (bf16[4,256,768]{2,1,0:T(8,128)(2,1)}, bf16[4,256,768]{2,1,0:T(8,128)(2,1)}) custom-call(s32[1]{0:T(128)} %bitcast.5.me, bf16[288,2048]{1,0:T(8,128)(2,1)} %copy-done.9, bf16[288,2048]{1,0:T(8,128)(2,1)} %copy-done.24, bf16[288,2048]{1,0:T(8,128)(2,1)} %collective-permute-done.1.refs_2_, bf16[288,2048]{1,0:T(8,128)(2,1)} %copy-done.4, ...), custom_call_target="tpu_custom_call" | custom-call | flops 999999995904 | bytes 1048576 | tf_op jit(solution)/shard_map/pallas_call | solution.py:576
  (236 shorter events, 220.6 us)
Async XLA Ops:
  7.2 118.5 %all-gather.6.cloned.1.call-start = ((), (), s32[]{:S(2)}) async-start(), calls=%async_computation.3 | async-start | bytes 3538944 | tf_op jit(solution)/shard_map/all_gather | solution.py:973
  7.9 170.8 %all-gather.8.cloned.1.call-start = ((), (), s32[]{:S(2)}) async-start(), calls=%async_computation.4 | async-start | bytes 9437184 | tf_op jit(solution)/shard_map/all_gather | solution.py:977
  31.9 232.5 %all-gather.10.cloned.1.call-start = ((), (), s32[]{:S(2)}) async-start(), calls=%async_computation.5 | async-start | bytes 9437184 | tf_op jit(solution)/shard_map/all_gather | solution.py:973
  32.6 231.7 %all-gather.12.cloned.1.call-start = ((), (), s32[]{:S(2)}) async-start(), calls=%async_computation.6 | async-start | bytes 9437184 | tf_op jit(solution)/shard_map/all_gather | solution.py:973
  33.2 276.9 %all-gather.14.cloned.1.call-start = ((), (), s32[]{:S(2)}) async-start(), calls=%async_computation.7 | async-start | bytes 9437184 | tf_op jit(solution)/shard_map/all_gather | solution.py:977
  33.8 388.3 %reduce-scatter.4.cloned.1.call-start = ((), (), s32[]{:S(2)}) async-start(), calls=%async_computation.8 | async-start | bytes 9437184 | tf_op jit(solution)/shard_map/reduce_scatter | solution.py:985
  34.6 33.6 %collective-permute-start = (bf16[288,2048]{1,0:T(8,128)(2,1)S(1)}, bf16[288,2048]{1,0:T(8,128)(2,1)S(1)}, u32[]{:S(2)}, u32[]{:S(2)}) collective-permute-start(bf16[288,2048]{1,0:T(8,128)(2,1)S(1)} %fusion.7.refs_0_), channel_id=1, source_target_pairs={{0,1},{1,3},{3,2},{2,0},{4,5},{5,7},{7,6},{6,4},{8,9},{9,11},{11,1... | collective-permute-start | bytes 3538952 | tf_op jit(solution)/shard_map/ppermute | solution.py:896
  68.2 27.2 %collective-permute-start.1 = (bf16[288,2048]{1,0:T(8,128)(2,1)S(1)}, bf16[288,2048]{1,0:T(8,128)(2,1)}, u32[]{:S(2)}, u32[]{:S(2)}) collective-permute-start(bf16[288,2048]{1,0:T(8,128)(2,1)S(1)} %collective-permute-done.refs_1_), channel_id=1, source_target_pairs={{0,1},{1,3},{3,2},{2,0},{4,5},{5,7},{7,6},{6,4},{8,9},{9,11},{11,1... | collective-permute-start | bytes 3538952 | tf_op jit(solution)/shard_map/ppermute | solution.py:896
  124.9 28.3 %collective-permute-start.3 = (bf16[288,2048]{1,0:T(8,128)(2,1)}, bf16[288,2048]{1,0:T(8,128)(2,1)S(1)}, u32[]{:S(2)}, u32[]{:S(2)}) collective-permute-start(bf16[288,2048]{1,0:T(8,128)(2,1)} %shard_map.171.refs_4_.refs_0_), channel_id=1, source_target_pairs={{0,1},{1,3},{3,2},{2,0},{4,5},{5,7},{7,6},{6,4},{8,9},{9,11},{11,1... | collective-permute-start | bytes 3538952 | tf_op jit(solution)/shard_map/ppermute | solution.py:896
  161.1 46.3 %collective-permute-start.10 = (bf16[288,2048]{1,0:T(8,128)(2,1)}, bf16[288,2048]{1,0:T(8,128)(2,1)S(1)}, u32[]{:S(2)}, u32[]{:S(2)}) collective-permute-start(bf16[288,2048]{1,0:T(8,128)(2,1)} %copy-done.8), channel_id=1, source_target_pairs={{0,1},{1,3},{3,2},{2,0},{4,5},{5,7},{7,6},{6,4},{8,9},{9,11},{11,1... | collective-permute-start | bytes 3538952 | tf_op jit(solution)/shard_map/ppermute | solution.py:896
  263.1 29.8 %collective-permute-start.13 = (bf16[288,2048]{1,0:T(8,128)(2,1)S(1)}, bf16[288,2048]{1,0:T(8,128)(2,1)S(1)}, u32[]{:S(2)}, u32[]{:S(2)}) collective-permute-start(bf16[288,2048]{1,0:T(8,128)(2,1)S(1)} %collective-permute-done.12.refs_0_.refs_2_), channel_id=1, source_target_pairs={{0,1},{1,3},{3,2},{2,0},{4,5},{5,7},{7,6},{6,4},{8,9},{9,11},{11,1... | collective-permute-start | bytes 3538952 | tf_op jit(solution)/shard_map/ppermute | solution.py:896
  263.1 61.8 %collective-permute-start.15 = (bf16[288,2048]{1,0:T(8,128)(2,1)}, bf16[288,2048]{1,0:T(8,128)(2,1)}, u32[]{:S(2)}, u32[]{:S(2)}) collective-permute-start(bf16[288,2048]{1,0:T(8,128)(2,1)} %copy-done.6), channel_id=1, source_target_pairs={{0,1},{1,3},{3,2},{2,0},{4,5},{5,7},{7,6},{6,4},{8,9},{9,11},{11,1... | collective-permute-start | bytes 3538952 | tf_op jit(solution)/shard_map/ppermute | solution.py:896
  341.7 152.1 %reduce-scatter.6.cloned.1.call-start = ((), (), s32[]{:S(2)}) async-start(), calls=%async_computation.9 | async-start | bytes 9437184 | tf_op jit(solution)/shard_map/reduce_scatter | solution.py:981
  419.3 169.9 %reduce-scatter.8.cloned.1.call-start = ((), (), s32[]{:S(2)}) async-start(), calls=%async_computation.10 | async-start | bytes 9437184 | tf_op jit(solution)/shard_map/reduce_scatter | solution.py:981
  425.8 30.1 %collective-permute-start.19 = (bf16[288,2048]{1,0:T(8,128)(2,1)}, bf16[288,2048]{1,0:T(8,128)(2,1)S(1)}, u32[]{:S(2)}, u32[]{:S(2)}) collective-permute-start(bf16[288,2048]{1,0:T(8,128)(2,1)} %shard_map.183), channel_id=1, source_target_pairs={{0,1},{1,3},{3,2},{2,0},{4,5},{5,7},{7,6},{6,4},{8,9},{9,11},{11,1... | collective-permute-start | bytes 3538952 | tf_op jit(solution)/shard_map/ppermute | solution.py:896
  429.6 56.9 %collective-permute-start.16 = (bf16[288,2048]{1,0:T(8,128)(2,1)}, bf16[288,2048]{1,0:T(8,128)(2,1)S(1)}, u32[]{:S(2)}, u32[]{:S(2)}) collective-permute-start(bf16[288,2048]{1,0:T(8,128)(2,1)} %shard_map.179), channel_id=1, source_target_pairs={{0,1},{1,3},{3,2},{2,0},{4,5},{5,7},{7,6},{6,4},{8,9},{9,11},{11,1... | collective-permute-start | bytes 3538952 | tf_op jit(solution)/shard_map/ppermute | solution.py:896
  483.7 44.3 %collective-permute-start.25 = (bf16[4,2048,256]{2,1,0:T(8,128)(2,1)}, bf16[4,2048,256]{2,1,0:T(8,128)(2,1)}, u32[]{:S(2)}, u32[]{:S(2)}) collective-permute-start(bf16[4,2048,256]{2,1,0:T(8,128)(2,1)} %get-tuple-element.118.refs_13_), channel_id=1, source_target_pairs={{0,4},{4,0},{8,12},{12,8},{16,20},{20,16},{24,28},{28,24},{1,5},{5... | collective-permute-start | bytes 12582920 | tf_op jit(solution)/shard_map/ppermute | solution.py:951
  490.2 31.2 %collective-permute-start.21 = (bf16[288,2048]{1,0:T(8,128)(2,1)}, bf16[288,2048]{1,0:T(8,128)(2,1)}, u32[]{:S(2)}, u32[]{:S(2)}) collective-permute-start(bf16[288,2048]{1,0:T(8,128)(2,1)} %shard_map.186), channel_id=1, source_target_pairs={{0,1},{1,3},{3,2},{2,0},{4,5},{5,7},{7,6},{6,4},{8,9},{9,11},{11,1... | collective-permute-start | bytes 3538952 | tf_op jit(solution)/shard_map/ppermute | solution.py:896
  525.9 27.9 %collective-permute-start.24 = (bf16[288,2048]{1,0:T(8,128)(2,1)}, bf16[288,2048]{1,0:T(8,128)(2,1)}, u32[]{:S(2)}, u32[]{:S(2)}) collective-permute-start(bf16[288,2048]{1,0:T(8,128)(2,1)} %shard_map.189.refs_3_.refs_2_), channel_id=1, source_target_pairs={{0,1},{1,3},{3,2},{2,0},{4,5},{5,7},{7,6},{6,4},{8,9},{9,11},{11,1... | collective-permute-start | bytes 3538952 | tf_op jit(solution)/shard_map/ppermute | solution.py:896
  544.7 28.5 %collective-permute-start.27 = (bf16[4,256,768]{2,1,0:T(8,128)(2,1)}, bf16[4,256,768]{2,1,0:T(8,128)(2,1)S(1)}, u32[]{:S(2)}, u32[]{:S(2)}) collective-permute-start(bf16[4,256,768]{2,1,0:T(8,128)(2,1)} %get-tuple-element.122.refs_2_), channel_id=1, source_target_pairs={{0,4},{4,0},{8,12},{12,8},{16,20},{20,16},{24,28},{28,24},{1,5},{5... | collective-permute-start | bytes 4718600 | tf_op jit(solution)/shard_map/ppermute | solution.py:951
  556.3 28.9 %collective-permute-start.26 = (bf16[288,2048]{1,0:T(8,128)(2,1)}, bf16[288,2048]{1,0:T(8,128)(2,1)S(1)}, u32[]{:S(2)}, u32[]{:S(2)}) collective-permute-start(bf16[288,2048]{1,0:T(8,128)(2,1)} %shard_map.193.refs_4_), channel_id=1, source_target_pairs={{0,1},{1,3},{3,2},{2,0},{4,5},{5,7},{7,6},{6,4},{8,9},{9,11},{11,1... | collective-permute-start | bytes 3538952 | tf_op jit(solution)/shard_map/ppermute | solution.py:896
  577.5 29.5 %collective-permute-start.31 = (bf16[256,768]{1,0:T(8,128)(2,1)}, bf16[256,768]{1,0:T(8,128)(2,1)}, u32[]{:S(2)}, u32[]{:S(2)}) collective-permute-start(bf16[256,768]{1,0:T(8,128)(2,1)} %get-tuple-element.134), channel_id=1, source_target_pairs={{0,8},{4,12},{8,0},{12,4},{16,24},{20,28},{24,16},{28,20},{1,9},{5... | collective-permute-start | bytes 1179656 | tf_op jit(solution)/shard_map/ppermute | solution.py:951
  578.9 28.1 %collective-permute-start.32 = (bf16[256,768]{1,0:T(8,128)(2,1)}, bf16[256,768]{1,0:T(8,128)(2,1)}, u32[]{:S(2)}, u32[]{:S(2)}) collective-permute-start(bf16[256,768]{1,0:T(8,128)(2,1)} %get-tuple-element.135), channel_id=1, source_target_pairs={{0,16},{4,20},{8,24},{12,28},{16,0},{20,4},{24,8},{28,12},{1,17},{... | collective-permute-start | bytes 1179656 | tf_op jit(solution)/shard_map/ppermute | solution.py:951
  597.6 34.3 %collective-permute-start.30 = (bf16[288,2048]{1,0:T(8,128)(2,1)}, bf16[288,2048]{1,0:T(8,128)(2,1)S(1)}, u32[]{:S(2)}, u32[]{:S(2)}) collective-permute-start(bf16[288,2048]{1,0:T(8,128)(2,1)} %shard_map.197.refs_3_), channel_id=1, source_target_pairs={{0,1},{1,3},{3,2},{2,0},{4,5},{5,7},{7,6},{6,4},{8,9},{9,11},{11,1... | collective-permute-start | bytes 3538952 | tf_op jit(solution)/shard_map/ppermute | solution.py:896
  (67 other events, 845.3 us)
Sparse Core Ops, SparseCore 0:
  9.9 35.0 all-gather.5
  46.8 55.9 all-gather.7
  104.7 54.3 all-gather.9
  160.9 54.3 all-gather.11
  217.0 55.9 all-gather.13
  341.8 69.9 reduce-scatter.3
  419.4 73.7 reduce-scatter.5
  496.6 76.8 reduce-scatter.7

commit v5 on v4

--- a/solution.py
+++ b/solution.py
@@ -829,7 +829,7 @@
         [block] * 2 + [whole(rows, wide)] * count,
         [jax.ShapeDtypeStruct((rows, width), jnp.float32), low_shape(rows, width)]
         + [low_shape(rows, wide)] * count,
-        HEAVY // 32,
+        0,
         earlier,
     )
     return out[0], out[1], out[2:]
@@ -1038,7 +1038,7 @@
 
     joint = project(first_slots, inputs_full, places)
     heads, query, key, value = attention_forward(joint, held, sequences, groups)
-    grad_slots = ring_gather(tied(cotangent, first_slots[-1]))
+    grad_slots = ring_gather(tied(cotangent, first_slots[max(count - 2, 0)]))
     heads_own = exchange(to_slots(heads, places, grad_slots[1]))
     mixed = base + dot(jnp.concatenate(heads_own, 1), output_full)
     second = tied(normalize(mixed, gain_two)[0].astype(low), grad_slots[min(2, count - 1)])
@@ -1081,7 +1081,7 @@
     down_grad = total_of([down_wgrad], jnp.float32)
     if cube:
         output_pairs = cube_pairs(output_parts, first_one[0])
-        inputs_parts = cube_rows(first_slots, joint_grad, places, HEAVY, output_pairs[0])
+        inputs_parts = cube_rows(first_slots, joint_grad, places, 0, output_pairs[0])
         second_pause = [inputs_parts[0]]
         first_next = tied_sum(ring_shift(first_parts[1], 1), first_parts[2], 0, *second_pause)
         output_turns = cube_turns(output_pairs, first_next)

time: 660 us -> 656 us (level)
  starting transfers between devices: 50.6 us -> 43.9 us
    unnamed x84 -> x82, local copies, waits for them, and re-layouts: 16.5 us -> 15.6 us
  transfers between devices with their start and end apart: 49 -> 49, of which waited for: 24 -> 25; matrix products, arithmetic and copies ran while one was open for 4% -> 4% of each run, Pallas kernels for 44% -> 44%
where the time goes in v5:
time: 656 us; the launch traced here: 651 us
  Pallas kernels  304 us (46%)
  waiting for transfers between devices  249 us (38%)
  starting transfers between devices  43.9 us (7%)
  local copies, waits for them, and re-layouts  16.5 us (3%)
  other arithmetic  15.1 us (2%)
  between operations  14.8 us (2%)
  matrix products  7.7 us (1%)
    ppermute x30, waiting for transfers between devices, ring_shift(): lax.ppermute(value, 'tensor', [(order[k], order[(k + by) % count]) for k...  220 us
    pallas_call x30, Pallas kernels, call(): pl.pallas_call(lambda *refs: kernel(*refs[:count], *refs[count + extra:])...  211 us
    pallas_call x3, Pallas kernels, weight_grad(): pl.pallas_call(kernel, grid=(extent // wide,), in_specs=[column_block(row...  51.5 us
    ppermute x30, starting transfers between devices, ring_shift(): lax.ppermute(value, 'tensor', [(order[k], order[(k + by) % count]) for k...  35.6 us
    ppermute x9, waiting for transfers between devices, flip(): return lax.ppermute(value, 'dp', [(k, k ^ bits) for k in range(count)])  22.2 us
    pallas_call x2, Pallas kernels, cube_call(): pl.pallas_call(body, grid_spec=pltpu.PrefetchScalarGridSpec(num_scalar_pr...  21.9 us
    pallas_call x1, Pallas kernels, attention_forward(): pl.pallas_call(lambda *refs: forward_kernel(count, *refs), grid=(groups,)...  19.5 us
    unnamed x82, local copies, waits for them, and re-layouts  15.6 us
  transfers between devices with their start and end apart: 49, of which 25 were waited for; matrix products, arithmetic and copies ran while one was open for 4% of the time, Pallas kernels for 44%

profile of v5, /device:TPU:0, one launch (start us, length us, event | category | flops | bytes accessed | tf_op | source)
XLA Modules:
  0.0 650.6 jit_solution(18217289407200879442)
XLA Ops:
  41.2 27.0 %collective-permute-done.refs_1_ = bf16[288,2048]{1,0:T(8,128)(2,1)} collective-permute-done((bf16[288,2048]{1,0:T(8,128)(2,1)S(1)}, bf16[288,2048]{1,0:T(8,128)(2,1)}, u32[]{:S(2)}, u32[]{:S(2)}) %collective-permute-start) | collective-permute-done | bytes 1179680 | tf_op jit(solution)/shard_map/ppermute | solution.py:896
  68.6 26.9 %collective-permute-done.1.refs_2_.refs_1_ = bf16[288,2048]{1,0:T(8,128)(2,1)S(1)} collective-permute-done((bf16[288,2048]{1,0:T(8,128)(2,1)}, bf16[288,2048]{1,0:T(8,128)(2,1)S(1)}, u32[]{:S(2)}, u32[]{:S(2)}) %collective-permute-start.1) | collective-permute-done | bytes 1179680 | tf_op jit(solution)/shard_map/ppermute | solution.py:896
  103.9 21.5 %collective-permute-done.2.refs_3_ = bf16[288,2048]{1,0:T(8,128)(2,1)} collective-permute-done((bf16[288,2048]{1,0:T(8,128)(2,1)S(1)}, bf16[288,2048]{1,0:T(8,128)(2,1)}, u32[]{:S(2)}, u32[]{:S(2)}) %collective-permute-start.2) | collective-permute-done | bytes 1179680 | tf_op jit(solution)/shard_map/ppermute | solution.py:896
  125.4 8.3 %shard_map.169.refs_0_ = f32[1152,768]{1,0:T(8,128)} custom-call(bf16[288,2048]{1,0:T(8,128)(2,1)} %copy-done.2, bf16[288,2048]{1,0:T(8,128)(2,1)} %collective-permute-done.refs_1_, bf16[288,2048]{1,0:T(8,128)(2,1)} %copy-done.1, bf16[288,2048]{1,0:T(8,128)(2,1)} %collective-permute-done.2.refs_3_, s32[4]{0:T(128)} %fusion.20.refs_4_.refs_1_.refs_8_.refs_5_, ...), custom_call_target="tpu_custom_call" | custom-call | flops 3623878656 | bytes 1048576 | tf_op jit(solution)/shard_map/pallas_call | solution.py:259
  133.7 19.5 %shard_map.170 = (bf16[1152,512]{1,0:T(8,128)(2,1)}, bf16[2,4,1152,128]{3,2,1,0:T(8,128)(2,1)}, bf16[2,1152,128]{2,1,0:T(8,128)(2,1)}, bf16[2,1152,128]{2,1,0:T(8,128)(2,1)}) custom-call(f32[1152,768]{1,0:T(8,128)} %shard_map.169.refs_0_, f32[1152,128]{1,0:T(8,128)} %get-tuple-element.152.refs_1_.refs_9_, f32[1152,128]{1,0:T(8,128)} %get-tuple-element.151.refs_2_.refs_10_, ...), custom_call_target="tpu_custom_call" | custom-call | flops 8153726976 | bytes 1048576 | tf_op jit(solution)/shard_map/pallas_call | solution.py:142
  159.7 9.3 %collective-permute-done.4.refs_1_ = bf16[288,512]{1,0:T(8,128)(2,1)S(1)} collective-permute-done((bf16[288,512]{1,0:T(8,128)(2,1)}, bf16[288,512]{1,0:T(8,128)(2,1)S(1)}, u32[]{:S(2)}, u32[]{:S(2)}) %collective-permute-start.4) | collective-permute-done | bytes 294944 | tf_op jit(solution)/shard_map/ppermute | solution.py:896
  185.3 17.2 %collective-permute-done.10.refs_1_.refs_6_.refs_2_ = bf16[288,2048]{1,0:T(8,128)(2,1)S(1)} collective-permute-done((bf16[288,2048]{1,0:T(8,128)(2,1)}, bf16[288,2048]{1,0:T(8,128)(2,1)S(1)}, u32[]{:S(2)}, u32[]{:S(2)}) %collective-permute-start.10) | collective-permute-done | bytes 1179680 | tf_op jit(solution)/shard_map/ppermute | solution.py:896
  205.6 26.7 %collective-permute-done.11.refs_1_ = bf16[288,2048]{1,0:T(8,128)(2,1)S(1)} collective-permute-done((bf16[288,2048]{1,0:T(8,128)(2,1)}, bf16[288,2048]{1,0:T(8,128)(2,1)S(1)}, u32[]{:S(2)}, u32[]{:S(2)}) %collective-permute-start.11) | collective-permute-done | bytes 1179680 | tf_op jit(solution)/shard_map/ppermute | solution.py:896
  232.3 26.1 %collective-permute-done.12.refs_0_.refs_2_ = bf16[288,2048]{1,0:T(8,128)(2,1)S(1)} collective-permute-done((bf16[288,2048]{1,0:T(8,128)(2,1)S(1)}, bf16[288,2048]{1,0:T(8,128)(2,1)S(1)}, u32[]{:S(2)}, u32[]{:S(2)}) %collective-permute-start.12) | collective-permute-done | bytes 1179680 | tf_op jit(solution)/shard_map/ppermute | solution.py:896
  258.5 16.7 %shard_map.174 = (bf16[288,2048]{1,0:T(8,128)(2,1)}, bf16[288,2048]{1,0:T(8,128)(2,1)}, bf16[288,2048]{1,0:T(8,128)(2,1)}, bf16[288,2048]{1,0:T(8,128)(2,1)}, bf...) custom-call(bf16[288,2048]{1,0:T(8,128)(2,1)} %shard_map.173.refs_0_, bf16[288,2048]{1,0:T(8,128)(2,1)} %copy-done.25, ...), custom_call_target="tpu_custom_call" | custom-call | flops 9663676416 | bytes 1048576 | tf_op jit(solution)/shard_map/pallas_call | solution.py:259
  275.2 13.0 %collective-permute-done.13.refs_1_.refs_3_ = bf16[288,2048]{1,0:T(8,128)(2,1)S(1)} collective-permute-done((bf16[288,2048]{1,0:T(8,128)(2,1)S(1)}, bf16[288,2048]{1,0:T(8,128)(2,1)S(1)}, u32[]{:S(2)}, u32[]{:S(2)}) %collective-permute-start.13) | collective-permute-done | bytes 1179680 | tf_op jit(solution)/shard_map/ppermute | solution.py:896
  289.2 16.2 %shard_map.175 = (bf16[288,2048]{1,0:T(8,128)(2,1)}, bf16[288,2048]{1,0:T(8,128)(2,1)}, bf16[288,2048]{1,0:T(8,128)(2,1)}, bf16[288,2048]{1,0:T(8,128)(2,1)}, bf...) custom-call(bf16[288,2048]{1,0:T(8,128)(2,1)} %copy-done.26, bf16[288,2048]{1,0:T(8,128)(2,1)} %copy-done.27, ...), custom_call_target="tpu_custom_call" | custom-call | flops 9663676416 | bytes 1048576 | tf_op jit(solution)/shard_map/pallas_call | solution.py:259
  305.4 14.7 %shard_map.176 = (bf16[288,2048]{1,0:T(8,128)(2,1)}, bf16[288,2048]{1,0:T(8,128)(2,1)}, bf16[288,2048]{1,0:T(8,128)(2,1)}, bf16[288,2048]{1,0:T(8,128)(2,1)}) custom-call(bf16[288,2048]{1,0:T(8,128)(2,1)} %get-tuple-element.83.refs_0_, bf16[288,2048]{1,0:T(8,128)(2,1)} %get-tuple-element.84.refs_1_, bf16[288,2048]{1,0:T(8,128)(2,1)} %get-tuple-element.85.refs_2_, ...), custom_call_target="tpu_custom_call" | custom-call | flops 9663676416 | bytes 1048576 | tf_op jit(solution)/shard_map/pallas_call | solution.py:259
  320.2 16.8 %shard_map.177.refs_13_ = bf16[2048,2048]{1,0:T(8,128)(2,1)} custom-call(bf16[288,2048]{1,0:T(8,128)(2,1)} %get-tuple-element.83.refs_0_, bf16[288,2048]{1,0:T(8,128)(2,1)} %get-tuple-element.84.refs_1_, bf16[288,2048]{1,0:T(8,128)(2,1)} %get-tuple-element.85.refs_2_, bf16[288,2048]{1,0:T(8,128)(2,1)} %get-tuple-element.86.refs_3_, ...), custom_call_target="tpu_custom_call" | custom-call | flops 9663676416 | bytes 1048576 | tf_op jit(solution)/shard_map/pallas_call | solution.py:515
  338.2 20.2 %shard_map.178 = (bf16[288,2048]{1,0:T(8,128)(2,1)}, bf16[288,2048]{1,0:T(8,128)(2,1)}, bf16[288,2048]{1,0:T(8,128)(2,1)}, bf16[288,2048]{1,0:T(8,128)(2,1)}, bf...) custom-call(bf16[288,2048]{1,0:T(8,128)(2,1)} %shard_map.171.refs_4_, ...), custom_call_target="tpu_custom_call" | custom-call | flops 9663676416 | bytes 1048576 | tf_op jit(solution)/shard_map/pallas_call | solution.py:259
  359.5 13.3 %shard_map.180.refs_8_ = bf16[288,2048]{1,0:T(8,128)(2,1)} custom-call(bf16[288,2048]{1,0:T(8,128)(2,1)} %get-tuple-element.105.refs_0_.refs_5_, bf16[288,2048]{1,0:T(8,128)(2,1)} %get-tuple-element.106.refs_1_.refs_5_, bf16[2048,2048]{1,0:T(8,128)(2,1)} %all-gather.10.cloned.1.call-done.refs_2_.refs_6_, ...), custom_call_target="tpu_custom_call" | custom-call | flops 4831838208 | bytes 1048576 | tf_op jit(solution)/shard_map/pallas_call | solution.py:259
  372.8 21.1 %shard_map.181 = (bf16[288,2048]{1,0:T(8,128)(2,1)}, bf16[288,2048]{1,0:T(8,128)(2,1)}, bf16[288,2048]{1,0:T(8,128)(2,1)}) custom-call(bf16[288,2048]{1,0:T(8,128)(2,1)} %get-tuple-element.98.refs_2_.refs_0_.refs_4_, bf16[288,2048]{1,0:T(8,128)(2,1)} %get-tuple-element.100.refs_1_.refs_6_, bf16[288,2048]{1,0:T(8,128)(2,1)} %get-tuple-element.101.refs_2_.refs_7_, ...), custom_call_target="tpu_custom_call" | custom-call | flops 14495514624 | bytes 1048576 | tf_op jit(solution)/shard_map/pallas_call | solution.py:259
  397.4 16.9 %shard_map.182.refs_2_ = bf16[2048,2048]{1,0:T(8,128)(2,1)} custom-call(bf16[288,2048]{1,0:T(8,128)(2,1)} %shard_map.173.refs_0_, bf16[288,2048]{1,0:T(8,128)(2,1)} %copy-done.25, bf16[288,2048]{1,0:T(8,128)(2,1)} %copy-done.26, bf16[288,2048]{1,0:T(8,128)(2,1)} %copy-done.27, bf16[288,2048]{1,0:T(8,128)(2,1)} %get-tuple-element.98.refs_2_.refs_0_.refs_4_, ...), custom_call_target="tpu_custom_call" | custom-call | flops 9663676416 | bytes 1048576 | tf_op jit(solution)/shard_map/pallas_call | solution.py:515
  425.6 17.8 %shard_map.184.refs_6_ = bf16[2048,2048]{1,0:T(8,128)(2,1)} custom-call(bf16[288,2048]{1,0:T(8,128)(2,1)} %shard_map.173.refs_0_, bf16[288,2048]{1,0:T(8,128)(2,1)} %copy-done.25, bf16[288,2048]{1,0:T(8,128)(2,1)} %copy-done.26, bf16[288,2048]{1,0:T(8,128)(2,1)} %copy-done.27, bf16[288,2048]{1,0:T(8,128)(2,1)} %get-tuple-element.102.refs_3_.refs_4_, ...), custom_call_target="tpu_custom_call" | custom-call | flops 9663676416 | bytes 1048576 | tf_op jit(solution)/shard_map/pallas_call | solution.py:515
  443.4 8.0 %collective-permute-done.19.refs_1_ = bf16[288,2048]{1,0:T(8,128)(2,1)S(1)} collective-permute-done((bf16[288,2048]{1,0:T(8,128)(2,1)}, bf16[288,2048]{1,0:T(8,128)(2,1)S(1)}, u32[]{:S(2)}, u32[]{:S(2)}) %collective-permute-start.19) | collective-permute-done | bytes 1179680 | tf_op jit(solution)/shard_map/ppermute | solution.py:896
  452.5 11.9 %shard_map.185 = (f32[288,2048]{1,0:T(8,128)}, bf16[288,2048]{1,0:T(8,128)(2,1)}, bf16[288,512]{1,0:T(8,128)(2,1)}, bf16[288,512]{1,0:T(8,128)(2,1)}, bf16[288,5...) custom-call(bf16[288,2048]{1,0:T(8,128)(2,1)} %get-tuple-element.107.refs_9_.refs_0_, bf16[288,2048]{1,0:T(8,128)(2,1)} %copy-done.6, ...), custom_call_target="tpu_custom_call" | custom-call | bytes 1048576 | tf_op jit(solution)/shard_map/pallas_call | solution.py:259
  467.5 10.9 %shard_map.187 = (bf16[4,2048,256]{2,1,0:T(8,128)(2,1)}, bf16[4,2048,256]{2,1,0:T(8,128)(2,1)}) custom-call(s32[1]{0:T(128)} %bitcast.5.me, bf16[288,512]{1,0:T(8,128)(2,1)} %get-tuple-element.79.refs_0_, bf16[288,512]{1,0:T(8,128)(2,1)} %copy-done.32, bf16[288,512]{1,0:T(8,128)(2,1)} %copy-done.33, bf16[288,512]{1,0:T(8,128)(2,1)} %copy-done.34, ...), custom_call_target="tpu_custom_call" | custom-call | flops 2415919104 | bytes 1048576 | tf_op jit(solution)/shard_map/pallas_call | solution.py:576
  490.5 22.0 %shard_map.188.refs_0_.refs_4_ = bf16[1152,768]{1,0:T(8,128)(2,1)} custom-call(bf16[2,4,1152,128]{3,2,1,0:T(8,128)(2,1)} %get-tuple-element.111.refs_0_, bf16[2,1152,128]{2,1,0:T(8,128)(2,1)} %get-tuple-element.112.refs_1_, bf16[2,1152,128]{2,1,0:T(8,128)(2,1)} %get-tuple-element.113.refs_2_, bf16[1152,512]{1,0:T(8,128)(2,1)} %get-tuple-element.78.refs_0_.refs_3_, ...), custom_call_target="tpu_custom_call" | custom-call | flops 999999995904 | bytes 1048576 | tf_op jit(solution)/shard_map/pallas_call | solution.py:259
  529.9 11.0 %shard_map.192 = (bf16[4,256,768]{2,1,0:T(8,128)(2,1)}, bf16[4,256,768]{2,1,0:T(8,128)(2,1)}) custom-call(s32[1]{0:T(128)} %bitcast.5.me, bf16[288,2048]{1,0:T(8,128)(2,1)} %copy-done.2, bf16[288,2048]{1,0:T(8,128)(2,1)} %collective-permute-done.refs_1_, bf16[288,2048]{1,0:T(8,128)(2,1)} %copy-done.1, bf16[288,2048]{1,0:T(8,128)(2,1)} %collective-permute-done.2.refs_3_, ...), custom_call_target="tpu_custom_call" | custom-call | bytes 1048576 | tf_op jit(solution)/shard_map/pallas_call | solution.py:576
  (234 shorter events, 222.8 us)
Async XLA Ops:
  7.2 118.2 %all-gather.6.cloned.1.call-start = ((), (), s32[]{:S(2)}) async-start(), calls=%async_computation.3 | async-start | bytes 3538944 | tf_op jit(solution)/shard_map/all_gather | solution.py:973
  7.9 168.2 %all-gather.8.cloned.1.call-start = ((), (), s32[]{:S(2)}) async-start(), calls=%async_computation.4 | async-start | bytes 9437184 | tf_op jit(solution)/shard_map/all_gather | solution.py:977
  31.8 226.6 %all-gather.10.cloned.1.call-start = ((), (), s32[]{:S(2)}) async-start(), calls=%async_computation.5 | async-start | bytes 9437184 | tf_op jit(solution)/shard_map/all_gather | solution.py:973
  32.6 225.9 %all-gather.12.cloned.1.call-start = ((), (), s32[]{:S(2)}) async-start(), calls=%async_computation.6 | async-start | bytes 9437184 | tf_op jit(solution)/shard_map/all_gather | solution.py:973
  33.1 272.3 %all-gather.14.cloned.1.call-start = ((), (), s32[]{:S(2)}) async-start(), calls=%async_computation.7 | async-start | bytes 9437184 | tf_op jit(solution)/shard_map/all_gather | solution.py:977
  33.7 384.0 %reduce-scatter.4.cloned.1.call-start = ((), (), s32[]{:S(2)}) async-start(), calls=%async_computation.8 | async-start | bytes 9437184 | tf_op jit(solution)/shard_map/reduce_scatter | solution.py:985
  34.6 33.7 %collective-permute-start = (bf16[288,2048]{1,0:T(8,128)(2,1)S(1)}, bf16[288,2048]{1,0:T(8,128)(2,1)}, u32[]{:S(2)}, u32[]{:S(2)}) collective-permute-start(bf16[288,2048]{1,0:T(8,128)(2,1)S(1)} %fusion.7.refs_0_), channel_id=1, source_target_pairs={{0,1},{1,3},{3,2},{2,0},{4,5},{5,7},{7,6},{6,4},{8,9},{9,11},{11,1... | collective-permute-start | bytes 3538952 | tf_op jit(solution)/shard_map/ppermute | solution.py:896
  95.5 29.9 %collective-permute-start.2 = (bf16[288,2048]{1,0:T(8,128)(2,1)S(1)}, bf16[288,2048]{1,0:T(8,128)(2,1)}, u32[]{:S(2)}, u32[]{:S(2)}) collective-permute-start(bf16[288,2048]{1,0:T(8,128)(2,1)S(1)} %collective-permute-done.1.refs_2_.refs_1_), channel_id=1, source_target_pairs={{0,1},{1,3},{3,2},{2,0},{4,5},{5,7},{7,6},{6,4},{8,9},{9,11},{11,1... | collective-permute-start | bytes 3538952 | tf_op jit(solution)/shard_map/ppermute | solution.py:896
  102.2 51.1 %collective-permute-start.3 = (bf16[288,2048]{1,0:T(8,128)(2,1)}, bf16[288,2048]{1,0:T(8,128)(2,1)}, u32[]{:S(2)}, u32[]{:S(2)}) collective-permute-start(bf16[288,2048]{1,0:T(8,128)(2,1)} %shard_map.171.refs_4_.refs_0_), channel_id=1, source_target_pairs={{0,1},{1,3},{3,2},{2,0},{4,5},{5,7},{7,6},{6,4},{8,9},{9,11},{11,1... | collective-permute-start | bytes 3538952 | tf_op jit(solution)/shard_map/ppermute | solution.py:896
  158.6 43.8 %collective-permute-start.10 = (bf16[288,2048]{1,0:T(8,128)(2,1)}, bf16[288,2048]{1,0:T(8,128)(2,1)S(1)}, u32[]{:S(2)}, u32[]{:S(2)}) collective-permute-start(bf16[288,2048]{1,0:T(8,128)(2,1)} %collective-permute-done.3.refs_2_.refs_5_.refs_1_), channel_id=1, source_target_pairs={{0,1},{1,3},{3,2},{2,0},{4,5},{5,7},{7,6},{6,4},{8,9},{9,11},{11,1... | collective-permute-start | bytes 3538952 | tf_op jit(solution)/shard_map/ppermute | solution.py:896
  258.4 29.8 %collective-permute-start.13 = (bf16[288,2048]{1,0:T(8,128)(2,1)S(1)}, bf16[288,2048]{1,0:T(8,128)(2,1)S(1)}, u32[]{:S(2)}, u32[]{:S(2)}) collective-permute-start(bf16[288,2048]{1,0:T(8,128)(2,1)S(1)} %collective-permute-done.12.refs_0_.refs_2_), channel_id=1, source_target_pairs={{0,1},{1,3},{3,2},{2,0},{4,5},{5,7},{7,6},{6,4},{8,9},{9,11},{11,1... | collective-permute-start | bytes 3538952 | tf_op jit(solution)/shard_map/ppermute | solution.py:896
  258.4 61.8 %collective-permute-start.15 = (bf16[288,2048]{1,0:T(8,128)(2,1)}, bf16[288,2048]{1,0:T(8,128)(2,1)}, u32[]{:S(2)}, u32[]{:S(2)}) collective-permute-start(bf16[288,2048]{1,0:T(8,128)(2,1)} %copy-done.8), channel_id=1, source_target_pairs={{0,1},{1,3},{3,2},{2,0},{4,5},{5,7},{7,6},{6,4},{8,9},{9,11},{11,1... | collective-permute-start | bytes 3538952 | tf_op jit(solution)/shard_map/ppermute | solution.py:896
  337.0 152.7 %reduce-scatter.6.cloned.1.call-start = ((), (), s32[]{:S(2)}) async-start(), calls=%async_computation.9 | async-start | bytes 9437184 | tf_op jit(solution)/shard_map/reduce_scatter | solution.py:981
  414.3 171.4 %reduce-scatter.8.cloned.1.call-start = ((), (), s32[]{:S(2)}) async-start(), calls=%async_computation.10 | async-start | bytes 9437184 | tf_op jit(solution)/shard_map/reduce_scatter | solution.py:981
  421.3 30.1 %collective-permute-start.19 = (bf16[288,2048]{1,0:T(8,128)(2,1)}, bf16[288,2048]{1,0:T(8,128)(2,1)S(1)}, u32[]{:S(2)}, u32[]{:S(2)}) collective-permute-start(bf16[288,2048]{1,0:T(8,128)(2,1)} %shard_map.183), channel_id=1, source_target_pairs={{0,1},{1,3},{3,2},{2,0},{4,5},{5,7},{7,6},{6,4},{8,9},{9,11},{11,1... | collective-permute-start | bytes 3538952 | tf_op jit(solution)/shard_map/ppermute | solution.py:896
  424.1 57.7 %collective-permute-start.16 = (bf16[288,2048]{1,0:T(8,128)(2,1)}, bf16[288,2048]{1,0:T(8,128)(2,1)S(1)}, u32[]{:S(2)}, u32[]{:S(2)}) collective-permute-start(bf16[288,2048]{1,0:T(8,128)(2,1)} %shard_map.179), channel_id=1, source_target_pairs={{0,1},{1,3},{3,2},{2,0},{4,5},{5,7},{7,6},{6,4},{8,9},{9,11},{11,1... | collective-permute-start | bytes 3538952 | tf_op jit(solution)/shard_map/ppermute | solution.py:896
  478.4 45.6 %collective-permute-start.25 = (bf16[4,2048,256]{2,1,0:T(8,128)(2,1)}, bf16[4,2048,256]{2,1,0:T(8,128)(2,1)}, u32[]{:S(2)}, u32[]{:S(2)}) collective-permute-start(bf16[4,2048,256]{2,1,0:T(8,128)(2,1)} %get-tuple-element.118.refs_13_), channel_id=1, source_target_pairs={{0,4},{4,0},{8,12},{12,8},{16,20},{20,16},{24,28},{28,24},{1,5},{5... | collective-permute-start | bytes 12582920 | tf_op jit(solution)/shard_map/ppermute | solution.py:951
  485.5 31.2 %collective-permute-start.21 = (bf16[288,2048]{1,0:T(8,128)(2,1)}, bf16[288,2048]{1,0:T(8,128)(2,1)}, u32[]{:S(2)}, u32[]{:S(2)}) collective-permute-start(bf16[288,2048]{1,0:T(8,128)(2,1)} %shard_map.186), channel_id=1, source_target_pairs={{0,1},{1,3},{3,2},{2,0},{4,5},{5,7},{7,6},{6,4},{8,9},{9,11},{11,1... | collective-permute-start | bytes 3538952 | tf_op jit(solution)/shard_map/ppermute | solution.py:896
  520.8 28.4 %collective-permute-start.24 = (bf16[288,2048]{1,0:T(8,128)(2,1)}, bf16[288,2048]{1,0:T(8,128)(2,1)S(1)}, u32[]{:S(2)}, u32[]{:S(2)}) collective-permute-start(bf16[288,2048]{1,0:T(8,128)(2,1)} %shard_map.189.refs_3_.refs_2_), channel_id=1, source_target_pairs={{0,1},{1,3},{3,2},{2,0},{4,5},{5,7},{7,6},{6,4},{8,9},{9,11},{11,1... | collective-permute-start | bytes 3538952 | tf_op jit(solution)/shard_map/ppermute | solution.py:896
  540.9 29.8 %collective-permute-start.27 = (bf16[4,256,768]{2,1,0:T(8,128)(2,1)}, bf16[4,256,768]{2,1,0:T(8,128)(2,1)S(1)}, u32[]{:S(2)}, u32[]{:S(2)}) collective-permute-start(bf16[4,256,768]{2,1,0:T(8,128)(2,1)} %get-tuple-element.122.refs_2_), channel_id=1, source_target_pairs={{0,4},{4,0},{8,12},{12,8},{16,20},{20,16},{24,28},{28,24},{1,5},{5... | collective-permute-start | bytes 4718600 | tf_op jit(solution)/shard_map/ppermute | solution.py:951
  552.8 28.9 %collective-permute-start.26 = (bf16[288,2048]{1,0:T(8,128)(2,1)}, bf16[288,2048]{1,0:T(8,128)(2,1)S(1)}, u32[]{:S(2)}, u32[]{:S(2)}) collective-permute-start(bf16[288,2048]{1,0:T(8,128)(2,1)} %shard_map.193.refs_4_), channel_id=1, source_target_pairs={{0,1},{1,3},{3,2},{2,0},{4,5},{5,7},{7,6},{6,4},{8,9},{9,11},{11,1... | collective-permute-start | bytes 3538952 | tf_op jit(solution)/shard_map/ppermute | solution.py:896
  575.0 29.5 %collective-permute-start.31 = (bf16[256,768]{1,0:T(8,128)(2,1)}, bf16[256,768]{1,0:T(8,128)(2,1)}, u32[]{:S(2)}, u32[]{:S(2)}) collective-permute-start(bf16[256,768]{1,0:T(8,128)(2,1)} %get-tuple-element.134), channel_id=1, source_target_pairs={{0,8},{4,12},{8,0},{12,4},{16,24},{20,28},{24,16},{28,20},{1,9},{5... | collective-permute-start | bytes 1179656 | tf_op jit(solution)/shard_map/ppermute | solution.py:951
  575.8 33.7 %collective-permute-start.32 = (bf16[256,768]{1,0:T(8,128)(2,1)}, bf16[256,768]{1,0:T(8,128)(2,1)}, u32[]{:S(2)}, u32[]{:S(2)}) collective-permute-start(bf16[256,768]{1,0:T(8,128)(2,1)} %get-tuple-element.135), channel_id=1, source_target_pairs={{0,16},{4,20},{8,24},{12,28},{16,0},{20,4},{24,8},{28,12},{1,17},{... | collective-permute-start | bytes 1179656 | tf_op jit(solution)/shard_map/ppermute | solution.py:951
  595.0 33.5 %collective-permute-start.30 = (bf16[288,2048]{1,0:T(8,128)(2,1)}, bf16[288,2048]{1,0:T(8,128)(2,1)S(1)}, u32[]{:S(2)}, u32[]{:S(2)}) collective-permute-start(bf16[288,2048]{1,0:T(8,128)(2,1)} %shard_map.197.refs_3_), channel_id=1, source_target_pairs={{0,1},{1,3},{3,2},{2,0},{4,5},{5,7},{7,6},{6,4},{8,9},{9,11},{11,1... | collective-permute-start | bytes 3538952 | tf_op jit(solution)/shard_map/ppermute | solution.py:896
  (66 other events, 796.0 us)
Sparse Core Ops, SparseCore 0:
  9.9 35.0 all-gather.5
  47.4 55.9 all-gather.7
  105.3 54.3 all-gather.9
  161.4 54.3 all-gather.11
  217.6 55.9 all-gather.13
  337.1 69.7 reduce-scatter.3
  414.5 72.5 reduce-scatter.5
  490.5 78.5 reduce-scatter.7
